TPU v7x, 128 devices: a whole 4x4x4 slice. The times are simulated.
128 devices in a mesh: rows: 16 (over z_hi, y, core), cols: 8 (over z_lo, x).
Axes of the slice: x: 4, y: 4, z: 4 (z_hi: 2, z_lo: 2; z = z_hi * 2 + z_lo), core: 2. Of those that a mesh axis runs over, the one named last changes fastest.
Arguments:
- field_real: float32 [6144, 6144], P('rows', 'cols'), may hold values from -6 to 6
- field_imag: float32 [6144, 6144], P('rows', 'cols'), may hold values from -6 to 6
- kerr_map: float32 [6144, 6144], P('rows', 'cols'), may hold values from 0.1 to 1
- pinhole: int32 [6144, 6144], P(None, ('rows', 'cols')), may hold values from 0 to 1, as said below
Outputs:
- out_real: float32 [6144, 6144], P('rows', 'cols')
- out_imag: float32 [6144, 6144], P('rows', 'cols')
- b_integral: float32 [6144, 6144], P('rows', 'cols')
Inputs may be any that keep to these rules, and one draw needn't show every extreme that they name: pinhole is 1 at every far-field pixel whose frequency (indices above 3072 taken as negative, so the disc wraps to the corners) lies inside a disc about zero frequency of radius R, and 0 outside it, except within about two pixels of the disc's rim, where it may take either value; R lies between 1536 and 2048 and varies from draw to draw.
All inputs are finite; a program needn't handle non-finite values.
Results may differ from a plain program's by a relative error of at most 0.00014.
Values sent between devices are 32-bit elements; how exact they have to be, the bound alone decides.
No kernel may reach another device: no remote copies, remote signals or barrier semaphores. Data moves between devices by JAX's collectives and lax.ppermute only.
A program may use at most 192 MiB of HBM per device.

v0:
```python
import math

import jax
import jax.numpy as jnp
from jax import lax
from jax.sharding import PartitionSpec as P

RADIX = 128


def in_one_piece(arrays, axis, split_dim, concat_dim, along):
    widths = [a.shape[along] for a in arrays]
    both = jnp.concatenate(arrays, axis=along)
    filled = lax.all_to_all(both, axis, split_axis=split_dim, concat_axis=concat_dim, tiled=True)
    return tuple(jnp.split(filled, [sum(widths[:k]) for k in range(1, len(widths))], axis=along))


def phase_pair(first, second, period):
    product = first[:, None] * second[None, :] % period
    angle = 2.0 * math.pi / period * product.astype(jnp.float32)
    return (jnp.cos(angle), jnp.sin(angle))


def complex_apply(form, real_part, imag_part, cos_table, sin_table, backward):
    weight = 1.0 if backward else -1.0
    real_cos = jnp.einsum(form, real_part, cos_table, precision=lax.Precision.HIGHEST)
    real_sin = jnp.einsum(form, real_part, sin_table, precision=lax.Precision.HIGHEST)
    imag_cos = jnp.einsum(form, imag_part, cos_table, precision=lax.Precision.HIGHEST)
    imag_sin = jnp.einsum(form, imag_part, sin_table, precision=lax.Precision.HIGHEST)
    return (real_cos - weight * imag_sin, imag_cos + weight * real_sin)


def twiddle(real_part, imag_part, cos_table, sin_table, backward):
    weight = 1.0 if backward else -1.0
    return (
        real_part * cos_table - weight * imag_part * sin_table,
        imag_part * cos_table + weight * real_part * sin_table,
    )


def transform_last(real_part, imag_part, backward):
    rows_here, length = real_part.shape
    blocks = length // RADIX
    outer = jnp.arange(blocks, dtype=jnp.int32)
    inner = jnp.arange(RADIX, dtype=jnp.int32)
    real_part = real_part.reshape(rows_here, blocks, RADIX)
    imag_part = imag_part.reshape(rows_here, blocks, RADIX)
    cos_outer, sin_outer = phase_pair(outer, outer, blocks)
    real_part, imag_part = complex_apply(
        "mab,ak->mkb", real_part, imag_part, cos_outer, sin_outer, backward
    )
    cos_mid, sin_mid = phase_pair(outer, inner, length)
    real_part, imag_part = twiddle(real_part, imag_part, cos_mid, sin_mid, backward)
    cos_inner, sin_inner = phase_pair(inner, inner, RADIX)
    real_part, imag_part = complex_apply(
        "mkb,bj->mkj", real_part, imag_part, cos_inner, sin_inner, backward
    )
    scale = 1.0 / math.sqrt(length)
    real_part = jnp.transpose(real_part, (0, 2, 1)).reshape(rows_here, length) * scale
    imag_part = jnp.transpose(imag_part, (0, 2, 1)).reshape(rows_here, length) * scale
    return (real_part, imag_part)


def kerr_phase(real_part, imag_part, kerr_part):
    power = real_part * real_part + imag_part * imag_part
    phase = kerr_part * power
    cosine = jnp.cos(phase)
    sine = jnp.sin(phase)
    return (real_part * cosine - imag_part * sine, real_part * sine + imag_part * cosine, phase)


def to_tall(real_part, imag_part):
    rows_here, length = real_part.shape
    device_count = lax.axis_size(("rows", "cols"))
    each = length // device_count
    real_part = real_part.reshape(rows_here, device_count, each)
    imag_part = imag_part.reshape(rows_here, device_count, each)
    real_part, imag_part = in_one_piece((real_part, imag_part), ("rows", "cols"), 1, 0, 2)
    real_part = jnp.transpose(real_part.reshape(device_count, rows_here, each), (2, 0, 1))
    imag_part = jnp.transpose(imag_part.reshape(device_count, rows_here, each), (2, 0, 1))
    return (real_part.reshape(each, length), imag_part.reshape(each, length))


def from_tall(real_part, imag_part):
    each, length = real_part.shape
    device_count = lax.axis_size(("rows", "cols"))
    rows_here = length // device_count
    real_part = jnp.transpose(real_part.reshape(each, device_count, rows_here), (1, 2, 0))
    imag_part = jnp.transpose(imag_part.reshape(each, device_count, rows_here), (1, 2, 0))
    real_part, imag_part = in_one_piece((real_part, imag_part), ("rows", "cols"), 0, 2, 1)
    return (real_part.reshape(rows_here, length), imag_part.reshape(rows_here, length))


def chirp_block(length, each):
    first = lax.axis_index(("rows", "cols")) * each + jnp.arange(each, dtype=jnp.int32)
    second = jnp.arange(length, dtype=jnp.int32)
    total = (first * first % (2 * length))[:, None] + (second * second % (2 * length))[None, :]
    total = total % (2 * length)
    angle = -(math.pi / length) * total.astype(jnp.float32)
    return (jnp.cos(angle), jnp.sin(angle))


def chirp_apply(real_part, imag_part, chirp_cos, chirp_sin):
    return (
        real_part * chirp_cos - imag_part * chirp_sin,
        real_part * chirp_sin + imag_part * chirp_cos,
    )


def per_device(field_real, field_imag, kerr_map, pinhole):
    real_part, imag_part, phase_one = kerr_phase(field_real, field_imag, kerr_map)
    real_part, imag_part, kerr_wide = (
        lax.all_to_all(real_part, "cols", split_axis=0, concat_axis=1, tiled=True),
        lax.all_to_all(imag_part, "cols", split_axis=0, concat_axis=1, tiled=True),
        lax.all_to_all(kerr_map, "cols", split_axis=0, concat_axis=1, tiled=True),
    )
    chirp_cos, chirp_sin = chirp_block(real_part.shape[1], pinhole.shape[1])
    aperture = jnp.transpose(pinhole).astype(jnp.float32)
    real_part, imag_part = transform_last(real_part, imag_part, False)
    real_part, imag_part = to_tall(real_part, imag_part)
    real_part, imag_part = transform_last(real_part, imag_part, False)
    real_part, imag_part = chirp_apply(real_part, imag_part, chirp_cos, chirp_sin)
    real_part, imag_part = transform_last(real_part, imag_part, True)
    real_part, imag_part = from_tall(real_part, imag_part)
    real_part, imag_part = transform_last(real_part, imag_part, True)
    real_part, imag_part, phase_two = kerr_phase(real_part, imag_part, kerr_wide)
    real_part, imag_part = transform_last(real_part, imag_part, False)
    real_part, imag_part = to_tall(real_part, imag_part)
    real_part, imag_part = transform_last(real_part, imag_part, False)
    real_part, imag_part = chirp_apply(real_part, imag_part, chirp_cos, chirp_sin)
    real_part = real_part * aperture
    imag_part = imag_part * aperture
    real_part, imag_part = transform_last(real_part, imag_part, False)
    real_part, imag_part = from_tall(real_part, imag_part)
    real_part, imag_part = transform_last(real_part, imag_part, False)
    out_real, out_imag, phase_back = (
        lax.all_to_all(real_part, "cols", split_axis=1, concat_axis=0, tiled=True),
        lax.all_to_all(imag_part, "cols", split_axis=1, concat_axis=0, tiled=True),
        lax.all_to_all(phase_two, "cols", split_axis=1, concat_axis=0, tiled=True),
    )
    return (out_real, out_imag, phase_one + phase_back)


def solution(mesh):
    placed = (P("rows", "cols"), P("rows", "cols"), P("rows", "cols"), P(None, ("rows", "cols")))
    return jax.shard_map(
        per_device,
        mesh=mesh,
        in_specs=placed,
        out_specs=(P("rows", "cols"), P("rows", "cols"), P("rows", "cols")),
        check_vma=False,
    )
```

profile of v0, /device:TPU:1, one launch (start us, length us, event | category | flops | bytes accessed | tf_op | source)
XLA Modules:
  0.0 551.5 jit_solution(4994066655461274510)
XLA Ops:
  0.7 5.4 fusion.612
  6.1 4.8 multiply_add_fusion.2
  10.9 22.4 %all_to_all.171 = f32[8,48,768]{2,1,0:T(8,128)S(1)} all-to-all(f32[8,48,768]{2,1,0:T(8,128)S(1)} %bitcast.319), channel_id=1, replica_groups=mesh['rows'=16,'cols'=8] {'cols'}, dimensions={0} | all-to-all | bytes 2359296 | tf_op jit(solution)/shard_map/all_to_all | solution.py:113
  33.3 4.1 all-to-all-start.1
  38.9 15.1 %all-to-all-done.1 = f32[8,48,768]{2,1,0:T(8,128)S(1)} async-done(((f32[8,48,768]{2,1,0:T(8,128)}), f32[8,48,768]{2,1,0:T(8,128)S(1)}, u32[]{:S(2)}, u32[]{:S(2)}) %all-to-all-start.1) | async-done | bytes 1179680 | tf_op jit(solution)/shard_map/all_to_all | solution.py:114
  69.0 8.2 %all-to-all-start.2 = ((f32[48,128,96]{2,0,1:T(8,128)}), f32[48,128,96]{2,0,1:T(8,128)S(1)}, u32[]{:S(2)}, u32[]{:S(2)}) async-start(f32[48,128,96]{2,0,1:T(8,128)} %copy.225), calls=%async_computation.2 | async-start | bytes 6291456 | tf_op jit(solution)/shard_map/all_to_all | solution.py:14
  77.5 40.3 %all-to-all-done.2 = f32[48,128,96]{2,0,1:T(8,128)S(1)} async-done(((f32[48,128,96]{2,0,1:T(8,128)}), f32[48,128,96]{2,0,1:T(8,128)S(1)}, u32[]{:S(2)}, u32[]{:S(2)}) %all-to-all-start.2) | async-done | bytes 2359328 | tf_op jit(solution)/shard_map/all_to_all | solution.py:14
  117.8 5.0 all-to-all-start.4
  122.8 3.6 fusion.616
  126.4 4.2 copy.327
  133.3 4.2 copy.326
  137.5 3.1 reshape_reshape.24
  157.6 2.9 mul.1747
  165.4 7.8 %fusion.230 = f32[48,48,128]{2,0,1:T(8,128)S(1)} fusion(f32[48,48,128]{2,1,0:T(8,128)} %mul.1747, f32[48,48,128]{2,1,0:T(8,128)} %mul.1736, s32[48,128]{1,0:T(8,128)S(1)} %add_select_fusion.4, s32[48]{0:T(128)S(1)} %and_select_fusion), kind=kOutput, calls=%fused_computation.274 | convolution fusion | flops 173428992 | bytes 3563712 | tf_op jit(solution)/shard_map/mab,ak->mkb/dot_general | solution.py:28
  173.2 6.0 %fusion.232 = f32[48,48,128]{2,0,1:T(8,128)S(1)} fusion(f32[48,48,128]{2,1,0:T(8,128)S(1)} %copy-done.12, f32[48,48,128]{2,1,0:T(8,128)S(1)} %copy-done.13, s32[48,128]{1,0:T(8,128)S(1)} %add_select_fusion.4, s32[48]{0:T(128)S(1)} %and_select_fusion), kind=kOutput, calls=%fused_computation.276 | convolution fusion | flops 173428992 | bytes 3563712 | tf_op jit(solution)/shard_map/mab,ak->mkb/dot_general | solution.py:26
  179.2 6.5 %convolution_add_fusion.3 = f32[48,48,128]{2,0,1:T(8,128)S(1)} fusion(f32[48,48,128]{2,0,1:T(8,128)S(1)} %fusion.230, f32[48,48,128]{2,1,0:T(8,128)S(1)} %copy-done.12, f32[48,48,128]{2,1,0:T(8,128)S(1)} %copy-done.13, s32[48,128]{1,0:T(8,128)S(1)} %add_select_fusion.4, s32[48]{0:T(128)S(1)} %and_select_fusion), kind=kOutput, calls=%fused_computation.66 | convolution fusion | flops 173723904 | bytes 4743360 | tf_op jit(solution)/shard_map/mab,ak->mkb/dot_general | solution.py:27
  185.7 6.3 %subtract_bitcast_fusion.5 = (f32[48,48,128]{2,1,0:T(8,128)S(1)}, f32[48,48,128]{2,1,0:T(8,128)S(1)}) fusion(f32[48,48,128]{2,0,1:T(8,128)S(1)} %convolution_add_fusion.3, f32[48,128]{1,0:T(8,128)S(1)} %fusion.248, f32[48,128]{1,0:T(8,128)S(1)} %copy-done.19, f32[48,48,128]{2,0,1:T(8,128)S(1)} %fusion.232, f32[48,48,128]{2,1,0:T(8,128)S(1)} %copy-done.12, ...), kind=kOutput, calls=%fused_computation.122 | convolution fusion | flops 175493376 | bytes 7151808 | tf_op jit(solution)/shard_map/mab,ak->mkb/dot_general | solution.py:29
  200.8 8.0 %all-to-all-start.3 = ((f32[128,96,48]{1,2,0:T(8,128)}), f32[128,96,48]{1,2,0:T(8,128)}, u32[]{:S(2)}, u32[]{:S(2)}) async-start(f32[128,96,48]{1,2,0:T(8,128)} %copy.238), calls=%async_computation.3 | async-start | bytes 6291456 | tf_op jit(solution)/shard_map/all_to_all | solution.py:14
  210.8 38.1 %all-to-all-done.3 = f32[128,96,48]{1,2,0:T(8,128)} async-done(((f32[128,96,48]{1,2,0:T(8,128)}), f32[128,96,48]{1,2,0:T(8,128)}, u32[]{:S(2)}, u32[]{:S(2)}) %all-to-all-start.3) | async-done | bytes 2359328 | tf_op jit(solution)/shard_map/all_to_all | solution.py:14
  248.9 6.4 %fusion.615 = (f32[1,48,6144]{1,2,0:T(8,128)}, f32[1,48,6144]{1,2,0:T(8,128)}) fusion(f32[1,96,6144]{1,2,0:T(8,128)} %bitcast.31), kind=kLoop, calls=%fused_computation.601 | loop fusion | bytes 4718592 | tf_op jit(solution)/shard_map/split | solution.py:15
  274.1 3.3 mul.1766
  279.7 3.7 mul.1770
  283.4 5.5 fusion.222
  288.8 5.5 fusion.224
  294.3 5.6 %fusion.30 = f32[48,48,128]{2,0,1:T(8,128)S(1)} fusion(f32[48,48,128]{2,0,1:T(8,128)S(1)} %fusion.222, f32[48,48,128]{2,1,0:T(8,128)S(1)} %mul.1770, f32[48,48,128]{2,1,0:T(8,128)S(1)} %mul.1766, f32[48,48,128]{2,1,0:T(8,128)S(1)} %all_to_all.143), kind=kOutput, calls=%fused_computation.51 | convolution fusion | flops 172544256 | bytes 5898240 | tf_op jit(solution)/shard_map/mab,ak->mkb/dot_general | solution.py:27
  300.0 5.7 %subtract_bitcast_fusion.3 = (f32[48,48,128]{2,1,0:T(8,128)S(1)}, f32[48,48,128]{2,1,0:T(8,128)S(1)}) fusion(f32[48,48,128]{2,0,1:T(8,128)S(1)} %fusion.30, f32[48,128]{1,0:T(8,128)S(1)} %copy-done.24, f32[48,128]{1,0:T(8,128)S(1)} %copy-done.21, f32[48,48,128]{2,0,1:T(8,128)S(1)} %fusion.224, f32[48,48,128]{2,1,0:T(8,128)S(1)} %mul.1770, ...), kind=kOutput, calls=%fused_computation.115 | convolution fusion | flops 174313728 | bytes 8306688 | tf_op jit(solution)/shard_map/mab,ak->mkb/dot_general | solution.py:29
  314.8 5.9 %all-to-all-start.5 = ((f32[48,128,96]{2,0,1:T(8,128)}), f32[48,128,96]{2,0,1:T(8,128)S(1)}, u32[]{:S(2)}, u32[]{:S(2)}) async-start(f32[48,128,96]{2,0,1:T(8,128)} %copy.252), calls=%async_computation.5 | async-start | bytes 6291456 | tf_op jit(solution)/shard_map/all_to_all | solution.py:14
  320.7 40.4 %all-to-all-done.5 = f32[48,128,96]{2,0,1:T(8,128)S(1)} async-done(((f32[48,128,96]{2,0,1:T(8,128)}), f32[48,128,96]{2,0,1:T(8,128)S(1)}, u32[]{:S(2)}, u32[]{:S(2)}) %all-to-all-start.5) | async-done | bytes 2359328 | tf_op jit(solution)/shard_map/all_to_all | solution.py:14
  361.2 3.6 fusion.614
  364.8 4.2 copy.331
  371.7 4.2 copy.330
  375.9 2.9 reshape_reshape.28
  395.9 3.1 mul.1806
  401.0 3.1 mul.1798
  404.1 7.5 %fusion.59 = (f32[6,8,48,128]{3,1,2,0:T(8,128)S(1)}, f32[6,8,48,128]{3,1,2,0:T(8,128)S(1)}) fusion(f32[48,6144]{1,0:T(8,128)} %mul.1806, f32[48,6144]{1,0:T(8,128)} %mul.1798, s32[6144,48]{0,1:T(8,128)} %param.7, s32[6144]{0:T(1024)S(1)} %add_select_fusion.3, s32[48]{0:T(128)S(1)} %and_select_fusion), kind=kLoop, calls=%fused_computation.100 | loop fusion | flops 5308416 | bytes 5923008
  426.4 5.9 %all-to-all-start.6 = ((f32[128,96,48]{1,2,0:T(8,128)}), f32[128,96,48]{1,2,0:T(8,128)S(1)}, u32[]{:S(2)}, u32[]{:S(2)}) async-start(f32[128,96,48]{1,2,0:T(8,128)} %copy.265), calls=%async_computation.6 | async-start | bytes 6291456 | tf_op jit(solution)/shard_map/all_to_all | solution.py:14
  432.2 2.8 add_bitcast_fusion
  435.0 3.2 copy.276
  438.2 3.6 add.535
  441.8 3.2 copy_multiply_fusion
  445.0 27.7 %all-to-all-done.6 = f32[128,96,48]{1,2,0:T(8,128)S(1)} async-done(((f32[128,96,48]{1,2,0:T(8,128)}), f32[128,96,48]{1,2,0:T(8,128)S(1)}, u32[]{:S(2)}, u32[]{:S(2)}) %all-to-all-start.6) | async-done | bytes 2359328 | tf_op jit(solution)/shard_map/all_to_all | solution.py:14
  472.7 5.0 all-to-all-start.9
  477.7 3.5 fusion.613
  481.2 3.3 copy.332
  504.3 5.5 %all-to-all-start.7 = ((f32[48,8,768]{2,0,1:T(8,128)}), f32[48,8,768]{2,0,1:T(8,128)}, u32[]{:S(2)}, u32[]{:S(2)}) async-start(f32[48,8,768]{2,0,1:T(8,128)} %copy.271), calls=%async_computation.7 | async-start | bytes 2359296 | tf_op jit(solution)/shard_map/all_to_all | solution.py:137
  520.9 6.2 %all-to-all-done.7 = f32[48,8,768]{2,0,1:T(8,128)} async-done(((f32[48,8,768]{2,0,1:T(8,128)}), f32[48,8,768]{2,0,1:T(8,128)}, u32[]{:S(2)}, u32[]{:S(2)}) %all-to-all-start.7) | async-done | bytes 1179680 | tf_op jit(solution)/shard_map/all_to_all | solution.py:137
  527.1 3.6 all-to-all-start.8
  533.1 14.7 %all-to-all-done.8 = f32[48,8,768]{2,0,1:T(8,128)S(1)} async-done(((f32[48,8,768]{2,0,1:T(8,128)}), f32[48,8,768]{2,0,1:T(8,128)S(1)}, u32[]{:S(2)}, u32[]{:S(2)}) %all-to-all-start.8) | async-done | bytes 1179680 | tf_op jit(solution)/shard_map/all_to_all | solution.py:138
  (156 shorter events, 154.7 us)
Async XLA Ops:
  0.6 5.5 copy-start.17
  0.6 5.5 copy-start.18
  6.1 4.8 copy-start.1
  33.3 20.7 %all-to-all-start.1 = ((f32[8,48,768]{2,1,0:T(8,128)}), f32[8,48,768]{2,1,0:T(8,128)S(1)}, u32[]{:S(2)}, u32[]{:S(2)}) async-start(f32[8,48,768]{2,1,0:T(8,128)} %bitcast.4), calls=%async_computation.1 | async-start | bytes 2359296 | tf_op jit(solution)/shard_map/all_to_all | solution.py:114
  57.3 1.3 copy-start.19
  57.3 1.3 copy-start.23
  69.0 48.7 %all-to-all-start.2 = ((f32[48,128,96]{2,0,1:T(8,128)}), f32[48,128,96]{2,0,1:T(8,128)S(1)}, u32[]{:S(2)}, u32[]{:S(2)}) async-start(f32[48,128,96]{2,0,1:T(8,128)} %copy.225), calls=%async_computation.2 | async-start | bytes 6291456 | tf_op jit(solution)/shard_map/all_to_all | solution.py:14
  77.5 108.3 %copy-start.26 = (f32[48,128]{1,0:T(8,128)}, f32[48,128]{1,0:T(8,128)S(1)}, u32[]{:S(2)}) copy-start(f32[48,128]{1,0:T(8,128)S(1)} %fusion.248) | copy-start | bytes 73732
  117.8 83.0 %all-to-all-start.4 = ((f32[8,48,768]{2,1,0:T(8,128)}), f32[8,48,768]{2,1,0:T(8,128)}, u32[]{:S(2)}, u32[]{:S(2)}) async-start(f32[8,48,768]{2,1,0:T(8,128)} %bitcast.323), calls=%async_computation.4 | async-start | bytes 2359296 | tf_op jit(solution)/shard_map/all_to_all | solution.py:115
  140.6 2.6 copy-start.14
  143.2 1.3 copy-start.10
  165.3 7.8 %copy-start.12 = (f32[48,48,128]{2,1,0:T(8,128)S(1)}, f32[48,48,128]{2,1,0:T(8,128)}, u32[]{:S(2)}) copy-start(f32[48,48,128]{2,1,0:T(8,128)} %mul.1747) | copy-start | bytes 3538948
  165.3 7.8 %copy-start.13 = (f32[48,48,128]{2,1,0:T(8,128)S(1)}, f32[48,48,128]{2,1,0:T(8,128)}, u32[]{:S(2)}) copy-start(f32[48,48,128]{2,1,0:T(8,128)} %mul.1736) | copy-start | bytes 3538948
  200.8 48.2 %all-to-all-start.3 = ((f32[128,96,48]{1,2,0:T(8,128)}), f32[128,96,48]{1,2,0:T(8,128)}, u32[]{:S(2)}, u32[]{:S(2)}) async-start(f32[128,96,48]{1,2,0:T(8,128)} %copy.238), calls=%async_computation.3 | async-start | bytes 6291456 | tf_op jit(solution)/shard_map/all_to_all | solution.py:14
  262.8 1.3 copy-start.20
  262.8 1.3 copy-start.27
  270.3 1.6 copy-start.3
  271.9 5.6 %copy-start.4 = (f32[48,48,128]{2,0,1:T(8,128)}, f32[48,48,128]{2,0,1:T(8,128)S(1)}, u32[]{:S(2)}) copy-start(f32[48,48,128]{2,0,1:T(8,128)S(1)} %fusion.32) | copy-start | bytes 3538948
  294.3 5.7 %copy-start.21 = (f32[48,128]{1,0:T(8,128)S(1)}, f32[48,128]{1,0:T(8,128)}, u32[]{:S(2)}) copy-start(f32[48,128]{1,0:T(8,128)} %get-tuple-element.33) | copy-start | bytes 73732
  294.3 5.7 %copy-start.24 = (f32[48,128]{1,0:T(8,128)S(1)}, f32[48,128]{1,0:T(8,128)}, u32[]{:S(2)}) copy-start(f32[48,128]{1,0:T(8,128)} %get-tuple-element.34) | copy-start | bytes 73732
  314.8 46.3 %all-to-all-start.5 = ((f32[48,128,96]{2,0,1:T(8,128)}), f32[48,128,96]{2,0,1:T(8,128)S(1)}, u32[]{:S(2)}, u32[]{:S(2)}) async-start(f32[48,128,96]{2,0,1:T(8,128)} %copy.252), calls=%async_computation.5 | async-start | bytes 6291456 | tf_op jit(solution)/shard_map/all_to_all | solution.py:14
  378.8 2.6 copy-start.15
  381.4 1.3 copy-start.11
  382.6 1.3 copy-start.22
  382.7 1.3 copy-start.25
  426.4 46.3 %all-to-all-start.6 = ((f32[128,96,48]{1,2,0:T(8,128)}), f32[128,96,48]{1,2,0:T(8,128)S(1)}, u32[]{:S(2)}, u32[]{:S(2)}) async-start(f32[128,96,48]{1,2,0:T(8,128)} %copy.265), calls=%async_computation.6 | async-start | bytes 6291456 | tf_op jit(solution)/shard_map/all_to_all | solution.py:14
  472.7 31.6 %all-to-all-start.9 = ((f32[48,8,768]{2,0,1:T(8,128)}), f32[48,8,768]{2,0,1:T(8,128)}, u32[]{:S(2)}, u32[]{:S(2)}) async-start(f32[48,8,768]{2,0,1:T(8,128)} %copy_multiply_fusion), calls=%async_computation.9 | async-start | bytes 2359296 | tf_op jit(solution)/shard_map/all_to_all | solution.py:139
  481.2 3.3 copy-start
  486.5 2.6 copy-start.9
  490.4 1.3 copy-start.16
  493.2 1.6 copy-start.5
  493.2 1.6 copy-start.7
  504.3 5.6 %copy-start.8 = (f32[48,48,128]{2,1,0:T(8,128)S(1)}, f32[48,48,128]{2,1,0:T(8,128)}, u32[]{:S(2)}) copy-start(f32[48,48,128]{2,1,0:T(8,128)} %copy-done.7) | copy-start | bytes 3538948
  504.3 22.8 %all-to-all-start.7 = ((f32[48,8,768]{2,0,1:T(8,128)}), f32[48,8,768]{2,0,1:T(8,128)}, u32[]{:S(2)}, u32[]{:S(2)}) async-start(f32[48,8,768]{2,0,1:T(8,128)} %copy.271), calls=%async_computation.7 | async-start | bytes 2359296 | tf_op jit(solution)/shard_map/all_to_all | solution.py:137
  509.8 1.6 copy-start.6
  520.9 9.8 %copy-start.2 = (f32[384,768]{1,0:T(8,128)S(1)}, f32[384,768]{1,0:T(8,128)}, u32[]{:S(2)}) copy-start(f32[384,768]{1,0:T(8,128)} %copy-done.1) | copy-start | bytes 3538948
  527.1 20.7 %all-to-all-start.8 = ((f32[48,8,768]{2,0,1:T(8,128)}), f32[48,8,768]{2,0,1:T(8,128)S(1)}, u32[]{:S(2)}, u32[]{:S(2)}) async-start(f32[48,8,768]{2,0,1:T(8,128)} %copy.275), calls=%async_computation.8 | async-start | bytes 2359296 | tf_op jit(solution)/shard_map/all_to_all | solution.py:138
where the time goes:
time: 555 us; the launch traced here: 551 us
  waiting for transfers between devices  183 us (33%)
  matrix products  141 us (25%)
  local copies, waits for them, and re-layouts  125 us (23%)
  starting transfers between devices  51.1 us (9%)
  other arithmetic  27.8 us (5%)
  blocking collectives  22.4 us (4%)
    all_to_all x4, waiting for transfers between devices, in_one_piece(): lax.all_to_all(both, axis, split_axis=split_dim, concat_axis=concat_dim,...  147 us
    dot_general x16, matrix products, complex_apply(): jnp.einsum(form, imag_part, sin_table, precision=lax.Precision.HIGHEST)  36.9 us
    dot_general x16, matrix products, complex_apply(): jnp.einsum(form, real_part, sin_table, precision=lax.Precision.HIGHEST)  35.3 us
    dot_general x16, matrix products, complex_apply(): jnp.einsum(form, real_part, cos_table, precision=lax.Precision.HIGHEST)  34.4 us
    dot_general x16, matrix products, complex_apply(): jnp.einsum(form, imag_part, cos_table, precision=lax.Precision.HIGHEST)  34.3 us
    all_to_all x4, starting transfers between devices, in_one_piece(): lax.all_to_all(both, axis, split_axis=split_dim, concat_axis=concat_dim,...  27.9 us
    mul x9, local copies, waits for them, and re-layouts, transform_last(): jnp.transpose(imag_part, (0, 2, 1)).reshape(rows_here, length) * scale  23 us
    mul x9, local copies, waits for them, and re-layouts, transform_last(): jnp.transpose(real_part, (0, 2, 1)).reshape(rows_here, length) * scale  22.4 us
  transfers between devices with their start and end apart: 9, of which 7 were waited for; matrix products, arithmetic and copies ran while one was open for 24% of the time, Pallas kernels for 0%

commit v1 on v0

v1 whole, which is shorter than its diff:
```python
import math

import jax
import jax.numpy as jnp
import ml_dtypes
import numpy as np
from jax import lax
from jax.experimental import pallas as pl
from jax.experimental.pallas import tpu as pltpu
from jax.sharding import PartitionSpec as P

N = 6144
DEV = 128
PITCH = 40
F32 = jnp.float32
BF16 = jnp.bfloat16
NT = (((1,), (1,)), ((), ()))
NN = (((1,), (0,)), ((), ()))
VMEM_LIMIT = 56 * 1024 * 1024


def root(period, product):
    return np.exp(-2j * np.pi * (np.asarray(product) % period) / period)


def real_form(matrix):
    return np.block([[matrix.real, -matrix.imag], [matrix.imag, matrix.real]])


def halves(matrix):
    high = matrix.astype(np.float32).astype(ml_dtypes.bfloat16)
    low = (matrix - high.astype(np.float64)).astype(ml_dtypes.bfloat16)
    return np.stack([high, low])


def planes(table):
    return np.stack([table.real, table.imag]).astype(np.float32)


def make_tables():
    t = {}
    r128 = np.arange(128)
    n1_of_src = 16 * (r128 % 8) + r128 // 8
    s128 = 1 / math.sqrt(128)
    s48 = 1 / math.sqrt(48)
    d_hi, jj, d_lo = np.meshgrid(np.arange(16), np.arange(3), np.arange(8), indexing="ij")
    k = (3 * (8 * d_hi + d_lo) + jj).reshape(-1)
    d384 = root(384, k[:, None] * np.arange(384)[None, :]) / math.sqrt(N)
    t["d384"] = halves(real_form(d384))
    q16 = np.arange(16)
    t["tw1"] = planes(root(N, q16[:, None] * np.arange(384)[None, :]).reshape(16, 1, 384))
    t["l_mixed"] = halves(real_form(root(128, r128[:, None] * n1_of_src[None, :]) * s128))
    t["l_plain"] = halves(real_form(root(128, r128[:, None] * r128[None, :]) * s128))
    lane_q, lane_8 = r128 // 8, r128 % 8
    row_8, row_q = r128 // 16, r128 % 16
    same = (row_q[:, None] == lane_q[None, :]).astype(np.float64)
    g6 = np.arange(6)[:, None, None]
    first = same * root(48, lane_8[None, None, :] * g6 + 6 * row_8[None, :, None] * lane_8[None, None, :]) * s48
    t["m_first"] = np.stack([halves(real_form(m)) for m in first], 1)
    second = same.T * root(48, g6 * lane_8[None, :, None] + 6 * row_8[None, None, :] * lane_8[None, :, None]) * s48
    t["m_second"] = np.stack([halves(real_form(m)) for m in second], 1)
    a = lane_8[None, :] + 8 * np.arange(6)[:, None]
    tw = root(N, r128[None, :, None] * a[:, None, :])
    t["tw_u_a"] = planes(tw)
    t["tw_a_u"] = planes(tw.transpose(0, 2, 1))
    keep = (lane_8[:, None] == lane_8[None, :]).astype(np.float64)
    v3 = np.arange(3)[:, None, None]
    into = keep * root(48, lane_q[None, :, None] * v3 + 3 * lane_q[None, :, None] * lane_q[None, None, :]) * s48
    t["r_in"] = np.stack([halves(real_form(m.T).T) for m in into], 1)
    back = keep * root(48, lane_q[None, None, :] * v3 + 3 * lane_q[None, :, None] * lane_q[None, None, :]) * s48
    t["r_out"] = np.stack([halves(real_form(m.T).T) for m in back], 1)
    rho = lane_q[None, :] + 16 * np.arange(3)[:, None]
    t["tw_u_rho"] = planes(root(N, r128[None, :, None] * rho[:, None, :]))
    kx = r128[None, :, None] + 128 * (np.arange(3)[:, None, None] + 3 * lane_q[None, None, :])
    t["h_x"] = planes(root(2 * N, kx * kx))
    y = r128[None, None, :] + 128 * (np.arange(6)[:, None, None] + 6 * row_8[None, :, None])
    t["chirp_y"] = (math.pi / N * ((y * y + N) % (2 * N) - N)).astype(np.float32)
    return t


TABLES = make_tables()


def chirp_angle(index):
    return math.pi / N * ((index * index + N) % (2 * N) - N).astype(F32)


def sin_cos(angle):
    turns = jnp.floor(angle * (2.0 / math.pi) + 0.5)
    r = angle - turns * 1.5703125
    r = r - turns * 4.837512969970703e-4
    r = r - turns * 7.549789948768648e-8
    quarter = turns.astype(jnp.int32)
    r2 = r * r
    sine = r + r * r2 * (-1.6666654611e-1 + r2 * (8.3321608736e-3 + r2 * -1.9515295891e-4))
    cosine = 1.0 - 0.5 * r2 + r2 * r2 * (4.166664568298827e-2 + r2 * (-1.388731625493765e-3 + r2 * 2.443315711809948e-5))
    odd = (quarter & 1) == 1
    s = jnp.where(odd, cosine, sine)
    c = jnp.where(odd, sine, cosine)
    s = jnp.where((quarter & 2) == 2, -s, s)
    c = jnp.where(((quarter + 1) & 2) == 2, -c, c)
    return s, c


def split(x):
    high = x.astype(BF16)
    return high, (x - high.astype(F32)).astype(BF16)


def mm(a, b, dims):
    return lax.dot_general(a, b, dims, preferred_element_type=F32)


def dot_left(table, data, dims):
    return mm(table[0], data[0], dims) + (mm(table[0], data[1], dims) + mm(table[1], data[0], dims))


def dot_right(data, table, dims):
    return mm(data[0], table[0], dims) + (mm(data[1], table[0], dims) + mm(data[0], table[1], dims))


def turn(z, w):
    return (z[0] * w[0] - z[1] * w[1], z[0] * w[1] + z[1] * w[0])


def add(a, b):
    return (a[0] + b[0], a[1] + b[1])


def sub(a, b):
    return (a[0] - b[0], a[1] - b[1])


def minus_i(a):
    return (a[1], -a[0])


def by_const(a, w):
    return (a[0] * w.real - a[1] * w.imag, a[0] * w.imag + a[1] * w.real)


def dft2(a, b):
    return add(a, b), sub(a, b)


def dft3(a, b, c):
    s = add(b, c)
    d = sub(b, c)
    h = math.sqrt(0.75)
    m = (a[0] - 0.5 * s[0], a[1] - 0.5 * s[1])
    e = (h * d[1], -h * d[0])
    return add(a, s), add(m, e), sub(m, e)


def dft4(a, b, c, d):
    p, q = dft2(a, c)
    r, s = dft2(b, d)
    s = minus_i(s)
    return add(p, r), add(q, s), sub(p, r), sub(q, s)


def dft6(z):
    even = dft3(z[0], z[2], z[4])
    odd = dft3(z[3], z[5], z[1])
    out = [None] * 6
    for k in range(6):
        f = add if k % 2 == 0 else sub
        out[k] = f(even[k % 3], odd[k % 3])
    return out


def dft16(z):
    cols = [dft4(z[i], z[i + 4], z[i + 8], z[i + 12]) for i in range(4)]
    out = [None] * 16
    for k1 in range(4):
        row = []
        for i in range(4):
            e = (i * k1) % 16
            row.append(cols[i][k1] if e == 0 else by_const(cols[i][k1], np.exp(-2j * np.pi * e / 16)))
        res = dft4(*row)
        for k2 in range(4):
            out[k1 + 4 * k2] = res[k2]
    return out


def enter_kernel(re_ref, im_ref, kerr_ref, ax_ref, ay_ref, out_ref, phase_ref):
    def body(jb, _):
        rows = pl.ds(pl.multiple_of(jb * 128, 128), 128)
        for lb in range(6):
            cols = slice(128 * lb, 128 * lb + 128)
            re, im = re_ref[rows, cols], im_ref[rows, cols]
            phase = kerr_ref[rows, cols] * (re * re + im * im)
            phase_ref[rows, cols] = phase
            s, c = sin_cos(phase + (ax_ref[rows, :] + ay_ref[:, cols]))
            both = turn((re, im), (c, s))
            for p in range(2):
                turned = both[p].T
                for i in range(8):
                    l = 128 * lb + 16 * i
                    out_ref[l // 48, pl.ds(48 * p + l % 48, 16), rows] = turned[16 * i:16 * i + 16]
        return 0

    lax.fori_loop(0, 3, body, 0)


def columns_kernel(in_ref, d_ref, tw_ref, out_ref, high_ref, low_ref):
    for lh in range(6):
        for t in range(3):
            lanes = slice(128 * t, 128 * t + 128)
            z = [(in_ref[r, 8 * lh:8 * lh + 8, lanes], in_ref[r, 48 + 8 * lh:56 + 8 * lh, lanes]) for r in range(16)]
            z = dft16(z)
            z = [z[0]] + [turn(z[q], (tw_ref[0, q, :, lanes], tw_ref[1, q, :, lanes])) for q in range(1, 16)]
            for q in range(0, 16, 2):
                rows = slice(128 * lh + 8 * q, 128 * lh + 8 * q + 16)
                for p in range(2):
                    h, l = split(jnp.concatenate([z[q][p], z[q + 1][p]], 0))
                    where = slice(384 * p + 128 * t, 384 * p + 128 * t + 128)
                    high_ref[rows, where] = h
                    low_ref[rows, where] = l
        rows = slice(128 * lh, 128 * lh + 128)
        res = dot_left((d_ref[0], d_ref[1]), (high_ref[rows, :], low_ref[rows, :]), NT)
        for p in range(2):
            for dh in range(16):
                for j in range(3):
                    at = 384 * p + 24 * dh + 8 * j
                    start = dh * 8 * PITCH + 12 * j + 6 * p + lh
                    out_ref[pl.ds(start, 8, stride=PITCH), :] = res[at:at + 8]


def gather_rows(in_ref, row):
    return in_ref[pl.ds(row, 128, stride=PITCH), :]


def over_senders(in_ref, base, tiles, table, out_ref):
    data = jnp.concatenate(
        [jnp.concatenate([gather_rows(in_ref, base + off), gather_rows(in_ref, base + off + 6)], 0) for off in tiles], 1
    )
    out_ref[...] = dot_left(table, split(data), NN)


def rows_first(in_ref, j, l_ref, tw_ref, y_ref, high_ref, low_ref):
    over_senders(in_ref, 12 * j, range(6), (l_ref[0], l_ref[1]), y_ref)
    for u in range(0, 128, 16):
        z = []
        for t in range(6):
            lanes = slice(128 * t, 128 * t + 128)
            w = (tw_ref[0, t, u:u + 16, :], tw_ref[1, t, u:u + 16, :])
            z.append(turn((y_ref[u:u + 16, lanes], y_ref[128 + u:144 + u, lanes]), w))
        z = dft6(z)
        for t in range(6):
            for p in range(2):
                h, l = split(z[t][p])
                high_ref[t, u:u + 16, 128 * p:128 * p + 128] = h
                low_ref[t, u:u + 16, 128 * p:128 * p + 128] = l


def rows_kernel(in_ref, kerr_ref, ax_ref, ay_ref, l_ref, m_ref, m2_ref, l2_ref, tw_ref, tw2_ref,
                out_ref, phase_ref, y_ref, w_ref, high_ref, low_ref):
    def body(j, _):
        rows_first(in_ref, j, l_ref, tw_ref, y_ref, high_ref, low_ref)
        rows = pl.ds(pl.multiple_of(16 * j, 16), 16)
        ax = ax_ref[pl.ds(pl.multiple_of(128 * j, 128), 128), :]
        for t in range(6):
            z = dot_left((m_ref[0, t], m_ref[1, t]), (high_ref[t], low_ref[t]), NT)
            re, im = z[:128], z[128:]
            lanes = slice(128 * t, 128 * t + 128)
            phase = kerr_ref[:, rows, lanes].reshape(128, 128) * (re * re + im * im)
            phase_ref[:, rows, lanes] = phase.reshape(8, 16, 128)
            s, c = sin_cos(phase + (ax + ay_ref[t]))
            both = jnp.concatenate(turn((im, -re), (c, s)), 0)
            w_ref[t] = dot_left((m2_ref[0, t], m2_ref[1, t]), split(both), NN)
        for r in range(0, 128, 16):
            z = dft6([(w_ref[t, r:r + 16, :], w_ref[t, 128 + r:144 + r, :]) for t in range(6)])
            for t in range(6):
                q = turn(z[t], (tw2_ref[0, t, r:r + 16, :], tw2_ref[1, t, r:r + 16, :]))
                for p in range(2):
                    h, l = split(q[p])
                    high_ref[t, r:r + 16, 128 * p:128 * p + 128] = h
                    low_ref[t, r:r + 16, 128 * p:128 * p + 128] = l
        for t in range(6):
            res = dot_left((l2_ref[0], l2_ref[1]), (high_ref[t], low_ref[t]), NT)
            for p in range(2):
                out_ref[pl.ds(12 * j + 6 * p + t, 128, stride=PITCH), :] = res[128 * p:128 * p + 128]
        return 0

    lax.fori_loop(0, 3, body, 0)


def far_field_kernel(in_ref, ph_ref, l_ref, r_ref, r2_ref, tw_ref, out_ref, y_ref, w_ref, high_ref, low_ref):
    def body(g, _):
        over_senders(in_ref, g, (0, 12, 24), (l_ref[0], l_ref[1]), y_ref)
        for u in range(0, 128, 16):
            z = []
            for t in range(3):
                lanes = slice(128 * t, 128 * t + 128)
                w = (tw_ref[0, t, u:u + 16, :], tw_ref[1, t, u:u + 16, :])
                z.append(turn((y_ref[u:u + 16, lanes], y_ref[128 + u:144 + u, lanes]), w))
            z = dft3(*z)
            for t in range(3):
                for p in range(2):
                    h, l = split(z[t][p])
                    high_ref[t, u:u + 16, 128 * p:128 * p + 128] = h
                    low_ref[t, u:u + 16, 128 * p:128 * p + 128] = l
        for t in range(3):
            z = dot_right((high_ref[t], low_ref[t]), (r_ref[0, t], r_ref[1, t]), NN)
            z = turn((z[:, :128], z[:, 128:]), (ph_ref[0, t, g], ph_ref[1, t, g]))
            w_ref[t] = dot_right(split(jnp.concatenate(z, 1)), (r2_ref[0, t], r2_ref[1, t]), NN)
        for u in range(0, 128, 16):
            z = dft3(*[(w_ref[t, u:u + 16, :128], w_ref[t, u:u + 16, 128:]) for t in range(3)])
            for t in range(3):
                q = turn(z[t], (tw_ref[0, t, u:u + 16, :], tw_ref[1, t, u:u + 16, :]))
                for p in range(2):
                    y_ref[128 * p + u:128 * p + u + 16, 128 * t:128 * t + 128] = q[p]
        res = dot_left((l_ref[0], l_ref[1]), split(y_ref[...]), NN)
        for t in range(3):
            for p in range(2):
                out_ref[pl.ds(12 * t + 6 * p + g, 128, stride=PITCH), :] = res[128 * p:128 * p + 128, 128 * t:128 * t + 128]
        return 0

    lax.fori_loop(0, 6, body, 0)


def leave_kernel(in_ref, l_ref, m_ref, tw_ref, out_ref, y_ref, high_ref, low_ref):
    def body(j, _):
        rows_first(in_ref, j, l_ref, tw_ref, y_ref, high_ref, low_ref)
        for t in range(6):
            z = dot_left((m_ref[0, t], m_ref[1, t]), (high_ref[t], low_ref[t]), NT)
            for p in range(2):
                rows = pl.ds(pl.multiple_of(48 * p + 16 * j, 16), 16)
                out_ref[:, rows, 128 * t:128 * t + 128] = z[128 * p:128 * p + 128].reshape(8, 16, 128)
        return 0

    lax.fori_loop(0, 3, body, 0)


def aperture_kernel(pin_ref, hx_ref, hy_ref, out_ref, t_ref):
    for v in range(48):
        t_ref[:, 128 * v:128 * v + 128] = pin_ref[128 * v:128 * v + 128, :].astype(F32).T
    for t in range(3):
        for g in range(6):
            block = jnp.concatenate([t_ref[8 * g:8 * g + 8, 128 * (t + 3 * k):128 * (t + 3 * k) + 128] for k in range(16)], 0)
            block = block.T
            h = turn((hx_ref[0, t], hx_ref[1, t]), (hy_ref[0, g:g + 1, :], hy_ref[1, g:g + 1, :]))
            for p in range(2):
                out_ref[p, t, g] = block * h[p]


def call(kernel, outs, args, scratch=(), flops=0):
    size = sum(a.size * a.dtype.itemsize for a in args)
    return pl.pallas_call(
        kernel,
        out_shape=outs,
        scratch_shapes=list(scratch),
        compiler_params=pltpu.CompilerParams(vmem_limit_bytes=VMEM_LIMIT),
        cost_estimate=pl.CostEstimate(flops=flops, bytes_accessed=size + 2_400_000, transcendentals=0),
    )(*args)


def shape(*dims):
    return jax.ShapeDtypeStruct(dims, F32)


def exchange(x, axis):
    return lax.all_to_all(x, axis, split_axis=0, concat_axis=0, tiled=True)


def per_device(field_real, field_imag, kerr_map, pinhole):
    tb = {k: jnp.asarray(v) for k, v in TABLES.items()}
    row_at, col_at = lax.axis_index("rows"), lax.axis_index("cols")
    me = lax.axis_index(("rows", "cols"))
    both = ("rows", "cols")
    ints = lambda n: jnp.arange(n, dtype=jnp.int32)
    kerr_rows = exchange(kerr_map.reshape(8, 48, 768), "cols")
    ax0 = chirp_angle(row_at * 384 + ints(384)).reshape(384, 1)
    ay0 = chirp_angle(col_at * 768 + ints(768)).reshape(1, 768)
    sent, phase_one = call(
        enter_kernel, (shape(16, 96, 384), shape(384, 768)), (field_real, field_imag, kerr_map, ax0, ay0)
    )
    cols = exchange(sent, "rows")
    sent = call(
        columns_kernel, shape(DEV * PITCH, 128), (cols, tb["d384"], tb["tw1"]),
        (pltpu.VMEM((768, 768), BF16), pltpu.VMEM((768, 768), BF16)),
    )
    rows = exchange(sent.reshape(DEV, PITCH, 128), both).reshape(DEV * PITCH, 128)
    ax1 = chirp_angle(me * 48 + 16 * ints(3)[:, None, None] + ints(16)[None, None, :])
    ax1 = jnp.broadcast_to(ax1, (3, 8, 16)).reshape(384, 1)
    pair6 = (pltpu.VMEM((6, 128, 256), BF16), pltpu.VMEM((6, 128, 256), BF16))
    sent, phase_two = call(
        rows_kernel, (shape(DEV * PITCH, 128), shape(8, 48, 768)),
        (rows, kerr_rows, ax1, tb["chirp_y"], tb["l_mixed"], tb["m_first"], tb["m_second"], tb["l_plain"],
         tb["tw_u_a"], tb["tw_a_u"]),
        (pltpu.VMEM((256, 768), F32), pltpu.VMEM((6, 256, 128), F32)) + pair6,
    )
    far = exchange(sent.reshape(DEV, PITCH, 128), both).reshape(DEV * PITCH, 128)
    ky = me * 48 + 8 * ints(6)[:, None, None] + ints(8)[None, None, :]
    ky_angle = -chirp_angle(jnp.broadcast_to(ky, (6, 16, 8)).reshape(6, 128))
    h_y = jnp.stack([jnp.cos(ky_angle), jnp.sin(ky_angle)])
    aperture = call(
        aperture_kernel, shape(2, 3, 6, 128, 128), (pinhole, tb["h_x"], h_y), (pltpu.VMEM((48, N), F32),)
    )
    pair3 = (pltpu.VMEM((3, 128, 256), BF16), pltpu.VMEM((3, 128, 256), BF16))
    sent = call(
        far_field_kernel, shape(DEV * PITCH, 128),
        (far, aperture, tb["l_plain"], tb["r_in"], tb["r_out"], tb["tw_u_rho"]),
        (pltpu.VMEM((256, 384), F32), pltpu.VMEM((3, 128, 256), F32)) + pair3,
    )
    phase_back = exchange(phase_two, "cols").reshape(384, 768)
    b_integral = phase_one + phase_back
    near = exchange(sent.reshape(DEV, PITCH, 128), both).reshape(DEV * PITCH, 128)
    sent = call(
        leave_kernel, shape(8, 96, 768), (near, tb["l_plain"], tb["m_first"], tb["tw_u_a"]),
        (pltpu.VMEM((256, 768), F32),) + pair6,
    )
    out = exchange(sent, "cols")
    return (out[:, :48].reshape(384, 768), out[:, 48:].reshape(384, 768), b_integral)


def solution(mesh):
    tiles = P("rows", "cols")
    return jax.shard_map(
        per_device,
        mesh=mesh,
        in_specs=(tiles, tiles, tiles, P(None, ("rows", "cols"))),
        out_specs=(tiles, tiles, tiles),
        check_vma=False,
    )
```

time: 555 us -> 286 us (0.52)
  matrix products: 141 us -> 0 us
  local copies, waits for them, and re-layouts: 125 us -> 9.72 us
  waiting for transfers between devices: 183 us -> 103 us
  Pallas kernels: 0 us -> 60.2 us
  blocking collectives: 22.4 us -> 81.4 us
  starting transfers between devices: 51.1 us -> 22.9 us
  other arithmetic: 27.8 us -> 4.66 us
    dot_general x64 -> x0, matrix products: 141 us -> none  [the longest x16 36.9 us: complex_apply(): jnp.einsum(form, imag_part, sin_table, precision=lax.Precision.HIGHEST)]
    all_to_all x9 -> x5, waiting for transfers between devices: 183 us -> 103 us  [exchange(): return lax.all_to_all(x, axis, split_axis=0, concat_axis=0, tiled=True)]
    pallas_call x0 -> x6, Pallas kernels: none -> 60.2 us  [call(): pl.pallas_call(kernel, out_shape=outs, scratch_shapes=list(scratch), comp...]
    all_to_all x1 -> x2, blocking collectives: 22.4 us -> 81.4 us  [exchange(): return lax.all_to_all(x, axis, split_axis=0, concat_axis=0, tiled=True)]
    mul x18 -> x0, local copies, waits for them, and re-layouts: 45.4 us -> none  [the longest x9 23 us: transform_last(): jnp.transpose(imag_part, (0, 2, 1)).reshape(rows_here, length) * scale]
    all_to_all x9 -> x5, starting transfers between devices: 51.1 us -> 22.9 us  [exchange(): return lax.all_to_all(x, axis, split_axis=0, concat_axis=0, tiled=True)]
    another operation x8 -> x0, local copies, waits for them, and re-layouts: 21.7 us -> none  [the longest x4 11.9 us: transform_last(): real_part = real_part.reshape(rows_here, blocks, RADIX)]
    split x4 -> x0, local copies, waits for them, and re-layouts: 17.2 us -> none  [in_one_piece(): jnp.split(filled, [sum(widths[:k]) for k in range(1, len(widths))], axis=...]
  transfers between devices with their start and end apart: 9 -> 5, of which waited for: 7 -> 5; matrix products, arithmetic and copies ran while one was open for 24% -> 3% of each run, Pallas kernels for 0% -> 8%
where the time goes in v1:
time: 286 us; the launch traced here: 283 us
  waiting for transfers between devices  103 us (36%)
  blocking collectives  81.4 us (28%)
  Pallas kernels  60.2 us (21%)
  starting transfers between devices  22.9 us (8%)
  local copies, waits for them, and re-layouts  9.72 us (3%)
  other arithmetic  4.66 us (2%)
    all_to_all x5, waiting for transfers between devices, exchange(): return lax.all_to_all(x, axis, split_axis=0, concat_axis=0, tiled=True)  103 us
    all_to_all x2, blocking collectives, exchange(): return lax.all_to_all(x, axis, split_axis=0, concat_axis=0, tiled=True)  81.4 us
    pallas_call x6, Pallas kernels, call(): pl.pallas_call(kernel, out_shape=outs, scratch_shapes=list(scratch), comp...  60.2 us
    all_to_all x5, starting transfers between devices, exchange(): return lax.all_to_all(x, axis, split_axis=0, concat_axis=0, tiled=True)  22.9 us
    unnamed x7, local copies, waits for them, and re-layouts  7.23 us
  transfers between devices with their start and end apart: 5, of which 5 were waited for; matrix products, arithmetic and copies ran while one was open for 3% of the time, Pallas kernels for 8%

profile of v1, /device:TPU:1, one launch (start us, length us, event | category | flops | bytes accessed | tf_op | source)
XLA Modules:
  0.0 282.7 jit_solution(13781377942990501365)
XLA Ops:
  0.6 0.8 fusion.2.ax_ref
  1.5 0.6 fusion.12.ay_ref
  2.1 6.0 %shard_map.184 = (f32[16,96,384]{2,1,0:T(8,128)}, f32[384,768]{1,0:T(8,128)}) custom-call(f32[384,768]{1,0:T(8,128)} %re_ref.1, f32[384,768]{1,0:T(8,128)} %im_ref.1, f32[384,768]{1,0:T(8,128)} %kerr_ref.1, f32[384,1]{1,0:T(8,128)} %fusion.2.ax_ref, f32[1,768]{1,0:T(1,128)} %fusion.12.ay_ref), custom_call_target="tpu_custom_call" | custom-call | bytes 5943552 | tf_op jit(solution)/shard_map/pallas_call | solution.py:350
  8.1 40.5 %all_to_all.35.in_ref = f32[16,96,384]{2,1,0:T(8,128)} all-to-all(f32[16,96,384]{2,1,0:T(8,128)} %get-tuple-element.7), channel_id=1, replica_groups=mesh['rows'=16,'cols'=8] {'rows'}, dimensions={0} | all-to-all | bytes 4718592 | tf_op jit(solution)/shard_map/all_to_all | solution.py:364
  48.6 4.5 %all-to-all-start.2 = ((f32[8,48,768]{2,1,0:T(8,128)}), f32[8,48,768]{2,1,0:T(8,128)S(1)}, u32[]{:S(2)}, u32[]{:S(2)}) async-start(f32[8,48,768]{2,1,0:T(8,128)} %bitcast.2), calls=%async_computation.2 | async-start | bytes 2359296 | tf_op jit(solution)/shard_map/all_to_all | solution.py:364
  53.1 10.1 %shard_map.185 = f32[5120,128]{1,0:T(8,128)} custom-call(f32[16,96,384]{2,1,0:T(8,128)} %all_to_all.35.in_ref, bf16[2,768,768]{2,1,0:T(8,128)(2,1)} %constant.91.clone.d_ref, f32[2,16,1,384]{3,2,1,0:T(1,128)} %constant.92.clone.tw_ref), custom_call_target="tpu_custom_call" | custom-call | bytes 7167744 | tf_op jit(solution)/shard_map/pallas_call | solution.py:350
  63.3 7.1 %all-to-all-done.2.kerr_ref = f32[8,48,768]{2,1,0:T(8,128)S(1)} async-done(((f32[8,48,768]{2,1,0:T(8,128)}), f32[8,48,768]{2,1,0:T(8,128)S(1)}, u32[]{:S(2)}, u32[]{:S(2)}) %all-to-all-start.2) | async-done | bytes 1179680 | tf_op jit(solution)/shard_map/all_to_all | solution.py:364
  70.3 0.0 copy-start.2
  70.3 1.0 copy-done.2
  71.3 4.5 %all-to-all-start.1 = ((f32[128,40,128]{2,1,0:T(8,128)}), f32[128,40,128]{2,1,0:T(8,128)S(1)}, u32[]{:S(2)}, u32[]{:S(2)}) async-start(f32[128,40,128]{2,1,0:T(8,128)} %bitcast.12), calls=%async_computation.1 | async-start | bytes 5242880 | tf_op jit(solution)/shard_map/all_to_all | solution.py:364
  75.9 0.1 fusion.17
  76.0 0.8 reshape.271.ax_ref
  76.8 33.9 %all-to-all-done.1 = f32[128,40,128]{2,1,0:T(8,128)S(1)} async-done(((f32[128,40,128]{2,1,0:T(8,128)}), f32[128,40,128]{2,1,0:T(8,128)S(1)}, u32[]{:S(2)}, u32[]{:S(2)}) %all-to-all-start.1) | async-done | bytes 2621472 | tf_op jit(solution)/shard_map/all_to_all | solution.py:364
  110.6 0.0 copy-start
  110.6 1.5 copy-done
  112.1 17.2 %shard_map.186 = (f32[5120,128]{1,0:T(8,128)}, f32[8,48,768]{2,1,0:T(8,128)}) custom-call(f32[5120,128]{1,0:T(8,128)} %bitcast.11, f32[8,48,768]{2,1,0:T(8,128)} %copy-done.2, f32[384,1]{1,0:T(8,128)} %reshape.271.ax_ref, f32[6,128,128]{2,1,0:T(8,128)} %constant.103.clone.ay_ref, bf16[2,256,256]{2,1,0:T(8,128)(2,1)} %constant.93.clone.l_ref, ...), custom_call_target="tpu_custom_call" | custom-call | bytes 11838720 | tf_op jit(solution)/shard_map/pallas_call | solution.py:350
  129.3 5.6 %all-to-all-start.3 = ((f32[128,40,128]{2,1,0:T(8,128)}), f32[128,40,128]{2,1,0:T(8,128)S(1)}, u32[]{:S(2)}, u32[]{:S(2)}) async-start(f32[128,40,128]{2,1,0:T(8,128)} %bitcast.16), calls=%async_computation.3 | async-start | bytes 5242880 | tf_op jit(solution)/shard_map/all_to_all | solution.py:364
  134.9 3.2 %copy.26.pin_ref = s32[6144,48]{1,0:T(8,128)} copy(s32[6144,48]{0,1:T(8,128)} %param.20) | data formatting | bytes 2359296 | tf_op args[3]
  138.1 0.1 add_remainder_fusion.1
  138.2 0.1 rem.76
  138.4 0.6 pad_maximum_fusion.hy_ref
  139.0 4.7 %shard_map.187.ph_ref = f32[2,3,6,128,128]{4,3,2,1,0:T(8,128)} custom-call(s32[6144,48]{1,0:T(8,128)} %copy.26.pin_ref, f32[2,3,128,128]{3,2,1,0:T(8,128)} %constant.102.clone.hx_ref, f32[2,6,128]{2,1,0:T(8,128)} %pad_maximum_fusion.hy_ref), custom_call_target="tpu_custom_call" | custom-call | bytes 3979008 | tf_op jit(solution)/shard_map/pallas_call | solution.py:350
  143.7 26.0 %all-to-all-done.3 = f32[128,40,128]{2,1,0:T(8,128)S(1)} async-done(((f32[128,40,128]{2,1,0:T(8,128)}), f32[128,40,128]{2,1,0:T(8,128)S(1)}, u32[]{:S(2)}, u32[]{:S(2)}) %all-to-all-start.3) | async-done | bytes 2621472 | tf_op jit(solution)/shard_map/all_to_all | solution.py:364
  169.7 0.0 copy-start.1
  169.7 1.5 copy-done.1
  171.2 13.6 %shard_map.188 = f32[5120,128]{1,0:T(8,128)} custom-call(f32[5120,128]{1,0:T(8,128)} %bitcast.13, f32[2,3,6,128,128]{4,3,2,1,0:T(8,128)} %shard_map.187.ph_ref, bf16[2,256,256]{2,1,0:T(8,128)(2,1)} %constant.94.clone.l2_ref.l_ref, bf16[2,3,256,256]{3,2,1,0:T(8,128)(2,1)} %constant.99.clone.r_ref, bf16[2,3,256,256]{3,2,1,0:T(8,128)(2,1)} %constant.100.clone.r2_ref, ...), custom_call_target="tpu_custom_call" | custom-call | bytes 9608960 | tf_op jit(solution)/shard_map/pallas_call | solution.py:350
  184.8 40.9 %all_to_all.36 = f32[128,40,128]{2,1,0:T(8,128)} all-to-all(f32[128,40,128]{2,1,0:T(8,128)} %bitcast.15), channel_id=1, replica_groups=mesh['rows'=16,'cols'=8] {'rows','cols'}, dimensions={0} | all-to-all | bytes 5242880 | tf_op jit(solution)/shard_map/all_to_all | solution.py:364
  225.7 4.7 %all-to-all-start.6 = ((f32[8,48,768]{2,1,0:T(8,128)}), f32[8,48,768]{2,1,0:T(8,128)S(1)}, u32[]{:S(2)}, u32[]{:S(2)}) async-start(f32[8,48,768]{2,1,0:T(8,128)} %get-tuple-element.10), calls=%async_computation.6 | async-start | bytes 2359296 | tf_op jit(solution)/shard_map/all_to_all | solution.py:364
  230.4 8.6 %shard_map.189 = f32[8,96,768]{2,1,0:T(8,128)} custom-call(f32[5120,128]{1,0:T(8,128)} %bitcast.14, bf16[2,256,256]{2,1,0:T(8,128)(2,1)} %constant.94.clone.l2_ref.l_ref, bf16[2,6,256,256]{3,2,1,0:T(8,128)(2,1)} %constant.95.clone.m_ref, f32[2,6,128,128]{3,2,1,0:T(8,128)} %constant.97.clone.tw_ref), custom_call_target="tpu_custom_call" | custom-call | bytes 7642880 | tf_op jit(solution)/shard_map/pallas_call | solution.py:350
  239.0 8.7 %all-to-all-done.6 = f32[8,48,768]{2,1,0:T(8,128)S(1)} async-done(((f32[8,48,768]{2,1,0:T(8,128)}), f32[8,48,768]{2,1,0:T(8,128)S(1)}, u32[]{:S(2)}, u32[]{:S(2)}) %all-to-all-start.6) | async-done | bytes 1179680 | tf_op jit(solution)/shard_map/all_to_all | solution.py:364
  247.7 3.6 %all-to-all-start.5 = ((f32[8,96,768]{2,1,0:T(8,128)}), f32[8,96,768]{2,1,0:T(8,128)S(1)}, u32[]{:S(2)}, u32[]{:S(2)}) async-start(f32[8,96,768]{2,1,0:T(8,128)} %shard_map.189), calls=%async_computation.5 | async-start | bytes 4718592 | tf_op jit(solution)/shard_map/all_to_all | solution.py:364
  251.3 2.4 bitcast_add_fusion
  253.7 27.4 %all-to-all-done.5 = f32[8,96,768]{2,1,0:T(8,128)S(1)} async-done(((f32[8,96,768]{2,1,0:T(8,128)}), f32[8,96,768]{2,1,0:T(8,128)S(1)}, u32[]{:S(2)}, u32[]{:S(2)}) %all-to-all-start.5) | async-done | bytes 2359328 | tf_op jit(solution)/shard_map/all_to_all | solution.py:364
  281.1 1.6 fusion.21
  (5 shorter events, 0.1 us)
Async XLA Ops:
  48.6 21.7 %all-to-all-start.2 = ((f32[8,48,768]{2,1,0:T(8,128)}), f32[8,48,768]{2,1,0:T(8,128)S(1)}, u32[]{:S(2)}, u32[]{:S(2)}) async-start(f32[8,48,768]{2,1,0:T(8,128)} %bitcast.2), calls=%async_computation.2 | async-start | bytes 2359296 | tf_op jit(solution)/shard_map/all_to_all | solution.py:364
  70.3 1.0 copy-start.2
  71.3 39.3 %all-to-all-start.1 = ((f32[128,40,128]{2,1,0:T(8,128)}), f32[128,40,128]{2,1,0:T(8,128)S(1)}, u32[]{:S(2)}, u32[]{:S(2)}) async-start(f32[128,40,128]{2,1,0:T(8,128)} %bitcast.12), calls=%async_computation.1 | async-start | bytes 5242880 | tf_op jit(solution)/shard_map/all_to_all | solution.py:364
  110.6 1.5 copy-start
  129.3 40.4 %all-to-all-start.3 = ((f32[128,40,128]{2,1,0:T(8,128)}), f32[128,40,128]{2,1,0:T(8,128)S(1)}, u32[]{:S(2)}, u32[]{:S(2)}) async-start(f32[128,40,128]{2,1,0:T(8,128)} %bitcast.16), calls=%async_computation.3 | async-start | bytes 5242880 | tf_op jit(solution)/shard_map/all_to_all | solution.py:364
  169.7 1.5 copy-start.1
  225.7 22.0 %all-to-all-start.6 = ((f32[8,48,768]{2,1,0:T(8,128)}), f32[8,48,768]{2,1,0:T(8,128)S(1)}, u32[]{:S(2)}, u32[]{:S(2)}) async-start(f32[8,48,768]{2,1,0:T(8,128)} %get-tuple-element.10), calls=%async_computation.6 | async-start | bytes 2359296 | tf_op jit(solution)/shard_map/all_to_all | solution.py:364
  247.7 33.4 %all-to-all-start.5 = ((f32[8,96,768]{2,1,0:T(8,128)}), f32[8,96,768]{2,1,0:T(8,128)S(1)}, u32[]{:S(2)}, u32[]{:S(2)}) async-start(f32[8,96,768]{2,1,0:T(8,128)} %shard_map.189), calls=%async_computation.5 | async-start | bytes 4718592 | tf_op jit(solution)/shard_map/all_to_all | solution.py:364

commit v2 on v1

--- a/solution.py
+++ b/solution.py
@@ -12,11 +12,13 @@
 N = 6144
 DEV = 128
 PITCH = 40
+EDGE = 44
+KEPT = 32
+MOVED = (np.arange(40), np.arange(88, 128), np.array([40, 41, 42, 43, 84, 85, 86, 87]))
 F32 = jnp.float32
 BF16 = jnp.bfloat16
 NT = (((1,), (1,)), ((), ()))
 NN = (((1,), (0,)), ((), ()))
-VMEM_LIMIT = 56 * 1024 * 1024
 
 
 def root(period, product):
@@ -43,14 +45,13 @@
     n1_of_src = 16 * (r128 % 8) + r128 // 8
     s128 = 1 / math.sqrt(128)
     s48 = 1 / math.sqrt(48)
-    d_hi, jj, d_lo = np.meshgrid(np.arange(16), np.arange(3), np.arange(8), indexing="ij")
-    k = (3 * (8 * d_hi + d_lo) + jj).reshape(-1)
-    d384 = root(384, k[:, None] * np.arange(384)[None, :]) / math.sqrt(N)
-    t["d384"] = halves(real_form(d384))
-    q16 = np.arange(16)
-    t["tw1"] = planes(root(N, q16[:, None] * np.arange(384)[None, :]).reshape(16, 1, 384))
+    t["tw_rho_j"] = planes(root(N, np.arange(48)[:, None] * r128[None, :]).reshape(48, 1, 128) * s48)
     t["l_mixed"] = halves(real_form(root(128, r128[:, None] * n1_of_src[None, :]) * s128))
-    t["l_plain"] = halves(real_form(root(128, r128[:, None] * r128[None, :]) * s128))
+    plain = root(128, r128[:, None] * r128[None, :]) * s128
+    t["l_plain"] = halves(real_form(plain))
+    outer = (r128 >= EDGE) & (r128 < DEV - EDGE)
+    t["l_kept"] = halves(real_form(np.where(outer[None, :], 0, plain)))
+    t["l_moved"] = halves(real_form(plain[:, np.concatenate(MOVED)]))
     lane_q, lane_8 = r128 // 8, r128 % 8
     row_8, row_q = r128 // 16, r128 % 16
     same = (row_q[:, None] == lane_q[None, :]).astype(np.float64)
@@ -112,11 +113,13 @@
 
 
 def dot_left(table, data, dims):
-    return mm(table[0], data[0], dims) + (mm(table[0], data[1], dims) + mm(table[1], data[0], dims))
+    left = jnp.concatenate([table[0], table[0], table[1]], 1)
+    return mm(left, jnp.concatenate([data[0], data[1], data[0]], dims[0][1][0]), dims)
 
 
 def dot_right(data, table, dims):
-    return mm(data[0], table[0], dims) + (mm(data[1], table[0], dims) + mm(data[0], table[1], dims))
+    right = jnp.concatenate([table[0], table[0], table[1]], 0)
+    return mm(jnp.concatenate([data[0], data[1], data[0]], 1), right, dims)
 
 
 def turn(z, w):
@@ -184,62 +187,64 @@
 
 
 def enter_kernel(re_ref, im_ref, kerr_ref, ax_ref, ay_ref, out_ref, phase_ref):
-    def body(jb, _):
-        rows = pl.ds(pl.multiple_of(jb * 128, 128), 128)
-        for lb in range(6):
-            cols = slice(128 * lb, 128 * lb + 128)
-            re, im = re_ref[rows, cols], im_ref[rows, cols]
-            phase = kerr_ref[rows, cols] * (re * re + im * im)
-            phase_ref[rows, cols] = phase
-            s, c = sin_cos(phase + (ax_ref[rows, :] + ay_ref[:, cols]))
-            both = turn((re, im), (c, s))
-            for p in range(2):
-                turned = both[p].T
-                for i in range(8):
-                    l = 128 * lb + 16 * i
-                    out_ref[l // 48, pl.ds(48 * p + l % 48, 16), rows] = turned[16 * i:16 * i + 16]
+    for lb in range(6):
+        cols = slice(128 * lb, 128 * lb + 128)
+        re, im = re_ref[:, cols], im_ref[:, cols]
+        phase = kerr_ref[:, cols] * (re * re + im * im)
+        phase_ref[:, cols] = phase
+        s, c = sin_cos(phase + (ax_ref[...] + ay_ref[:, cols]))
+        both = turn((re, im), (c, s))
+        for p in range(2):
+            turned = both[p].T
+            for i in range(8):
+                l = 128 * lb + 16 * i
+                out_ref[l // 48, pl.ds(48 * p + l % 48, 16), :] = turned[16 * i:16 * i + 16]
+
+
+def columns_kernel(in_ref, l_ref, tw_ref, out_ref, z_ref, high_ref, low_ref):
+    def body(lh, _):
+        low = pl.ds(pl.multiple_of(8 * lh, 8), 8)
+        high = pl.ds(pl.multiple_of(48 + 8 * lh, 8), 8)
+        for j3 in range(3):
+            lanes = slice(128 * j3, 128 * j3 + 128)
+            at = [(n + 5 * j3) % 16 for n in range(16)]
+            z = dft16([(in_ref[r, low, lanes], in_ref[r, high, lanes]) for r in at])
+            for k in range(16):
+                z_ref[j3, k, 0] = z[k][0]
+                z_ref[j3, k, 1] = z[k][1]
+        for k in range(0, 16, 2):
+            found = {}
+            for m in (k, k + 1):
+                z = dft3(*[(z_ref[j3, m, 0], z_ref[j3, m, 1]) for j3 in range(3)])
+                for k3 in range(3):
+                    rho = next(r for r in range(48) if r % 16 == m and r % 3 == k3)
+                    found[rho] = turn(z[k3], (tw_ref[0, rho], tw_ref[1, rho]))
+            for rho in sorted(found):
+                if rho % 2 == 0:
+                    rows = slice(8 * rho, 8 * rho + 16)
+                    for p in range(2):
+                        h, l = split(jnp.concatenate([found[rho][p], found[rho + 1][p]], 0))
+                        high_ref[rows, 128 * p:128 * p + 128] = h
+                        low_ref[rows, 128 * p:128 * p + 128] = l
+        res = dot_left((l_ref[0], l_ref[1]), (high_ref[...], low_ref[...]), NT)
+        for j in range(3):
+            for p in range(2):
+                out_ref[pl.ds(12 * j + 6 * p + lh, 128, stride=PITCH), :] = res[128 * p:128 * p + 128, 128 * j:128 * j + 128]
         return 0
 
-    lax.fori_loop(0, 3, body, 0)
-
-
-def columns_kernel(in_ref, d_ref, tw_ref, out_ref, high_ref, low_ref):
-    for lh in range(6):
-        for t in range(3):
-            lanes = slice(128 * t, 128 * t + 128)
-            z = [(in_ref[r, 8 * lh:8 * lh + 8, lanes], in_ref[r, 48 + 8 * lh:56 + 8 * lh, lanes]) for r in range(16)]
-            z = dft16(z)
-            z = [z[0]] + [turn(z[q], (tw_ref[0, q, :, lanes], tw_ref[1, q, :, lanes])) for q in range(1, 16)]
-            for q in range(0, 16, 2):
-                rows = slice(128 * lh + 8 * q, 128 * lh + 8 * q + 16)
-                for p in range(2):
-                    h, l = split(jnp.concatenate([z[q][p], z[q + 1][p]], 0))
-                    where = slice(384 * p + 128 * t, 384 * p + 128 * t + 128)
-                    high_ref[rows, where] = h
-                    low_ref[rows, where] = l
-        rows = slice(128 * lh, 128 * lh + 128)
-        res = dot_left((d_ref[0], d_ref[1]), (high_ref[rows, :], low_ref[rows, :]), NT)
-        for p in range(2):
-            for dh in range(16):
-                for j in range(3):
-                    at = 384 * p + 24 * dh + 8 * j
-                    start = dh * 8 * PITCH + 12 * j + 6 * p + lh
-                    out_ref[pl.ds(start, 8, stride=PITCH), :] = res[at:at + 8]
-
-
-def gather_rows(in_ref, row):
-    return in_ref[pl.ds(row, 128, stride=PITCH), :]
-
-
-def over_senders(in_ref, base, tiles, table, out_ref):
-    data = jnp.concatenate(
-        [jnp.concatenate([gather_rows(in_ref, base + off), gather_rows(in_ref, base + off + 6)], 0) for off in tiles], 1
-    )
-    out_ref[...] = dot_left(table, split(data), NN)
-
-
-def rows_first(in_ref, j, l_ref, tw_ref, y_ref, high_ref, low_ref):
-    over_senders(in_ref, 12 * j, range(6), (l_ref[0], l_ref[1]), y_ref)
+    lax.fori_loop(0, 6, body, 0)
+
+
+def gather_rows(in_ref, row, pitch, count=128, first=0):
+    return in_ref[pl.ds(first * pitch + row, count, stride=pitch), :]
+
+
+def over_senders(in_ref, rows, pitch, table, out_ref):
+    data = jnp.concatenate([jnp.concatenate([gather_rows(in_ref, r, pitch) for r in pair], 0) for pair in rows], 1)
+    out_ref[:, :data.shape[1]] = dot_left(table, split(data), NN)
+
+
+def after_senders(tw_ref, y_ref, high_ref, low_ref):
     for u in range(0, 128, 16):
         z = []
         for t in range(6):
@@ -257,7 +262,8 @@
 def rows_kernel(in_ref, kerr_ref, ax_ref, ay_ref, l_ref, m_ref, m2_ref, l2_ref, tw_ref, tw2_ref,
                 out_ref, phase_ref, y_ref, w_ref, high_ref, low_ref):
     def body(j, _):
-        rows_first(in_ref, j, l_ref, tw_ref, y_ref, high_ref, low_ref)
+        over_senders(in_ref, [(12 * j + t, 12 * j + 6 + t) for t in range(6)], PITCH, (l_ref[0], l_ref[1]), y_ref)
+        after_senders(tw_ref, y_ref, high_ref, low_ref)
         rows = pl.ds(pl.multiple_of(16 * j, 16), 16)
         ax = ax_ref[pl.ds(pl.multiple_of(128 * j, 128), 128), :]
         for t in range(6):
@@ -280,7 +286,16 @@
         for t in range(6):
             res = dot_left((l2_ref[0], l2_ref[1]), (high_ref[t], low_ref[t]), NT)
             for p in range(2):
-                out_ref[pl.ds(12 * j + 6 * p + t, 128, stride=PITCH), :] = res[128 * p:128 * p + 128]
+                row = 2 * j + p
+                if t < 5:
+                    out_ref[pl.ds(6 * t + row, 128, stride=KEPT), :] = res[128 * p:128 * p + 128]
+                else:
+                    y_ref[128 * p:128 * p + 128, :128] = res[128 * p:128 * p + 128]
+                    for slot in range(2):
+                        b = 128 * p + int(MOVED[slot][0])
+                        out_ref[pl.ds(EDGE * KEPT + 6 * slot + row, 40, stride=KEPT), :] = y_ref[b:b + 40, :128]
+                    out_ref[pl.ds(EDGE * KEPT + 12 + row, 4, stride=KEPT), :] = y_ref[128 * p + 40:128 * p + 44, :128]
+                    out_ref[pl.ds((EDGE + 4) * KEPT + 12 + row, 4, stride=KEPT), :] = y_ref[128 * p + 84:128 * p + 88, :128]
         return 0
 
     lax.fori_loop(0, 3, body, 0)
@@ -288,7 +303,7 @@
 
 def far_field_kernel(in_ref, ph_ref, l_ref, r_ref, r2_ref, tw_ref, out_ref, y_ref, w_ref, high_ref, low_ref):
     def body(g, _):
-        over_senders(in_ref, g, (0, 12, 24), (l_ref[0], l_ref[1]), y_ref)
+        over_senders(in_ref, [(6 * g + 2 * j, 6 * g + 2 * j + 1) for j in range(3)], KEPT, (l_ref[0], l_ref[1]), y_ref)
         for u in range(0, 128, 16):
             z = []
             for t in range(3):
@@ -314,15 +329,19 @@
         res = dot_left((l_ref[0], l_ref[1]), split(y_ref[...]), NN)
         for t in range(3):
             for p in range(2):
-                out_ref[pl.ds(12 * t + 6 * p + g, 128, stride=PITCH), :] = res[128 * p:128 * p + 128, 128 * t:128 * t + 128]
+                out_ref[pl.ds(6 * g + 2 * t + p, 128, stride=KEPT), :] = res[128 * p:128 * p + 128, 128 * t:128 * t + 128]
         return 0
 
-    lax.fori_loop(0, 6, body, 0)
-
-
-def leave_kernel(in_ref, l_ref, m_ref, tw_ref, out_ref, y_ref, high_ref, low_ref):
+    lax.fori_loop(0, 5, body, 0)
+
+
+def leave_kernel(in_ref, l_ref, lm_ref, m_ref, tw_ref, out_ref, y_ref, high_ref, low_ref):
     def body(j, _):
-        rows_first(in_ref, j, l_ref, tw_ref, y_ref, high_ref, low_ref)
+        row = 2 * j
+        over_senders(in_ref, [(6 * t + row, 6 * t + row + 1) for t in range(5)], KEPT, (l_ref[0], l_ref[1]), y_ref)
+        moved = [gather_rows(in_ref, 6 * slot + row + p, KEPT, len(MOVED[slot]), EDGE) for p in range(2) for slot in range(3)]
+        y_ref[:, 640:] = dot_left((lm_ref[0], lm_ref[1]), split(jnp.concatenate(moved, 0)), NN)
+        after_senders(tw_ref, y_ref, high_ref, low_ref)
         for t in range(6):
             z = dot_left((m_ref[0, t], m_ref[1, t]), (high_ref[t], low_ref[t]), NT)
             for p in range(2):
@@ -333,26 +352,36 @@
     lax.fori_loop(0, 3, body, 0)
 
 
-def aperture_kernel(pin_ref, hx_ref, hy_ref, out_ref, t_ref):
-    for v in range(48):
-        t_ref[:, 128 * v:128 * v + 128] = pin_ref[128 * v:128 * v + 128, :].astype(F32).T
-    for t in range(3):
-        for g in range(6):
-            block = jnp.concatenate([t_ref[8 * g:8 * g + 8, 128 * (t + 3 * k):128 * (t + 3 * k) + 128] for k in range(16)], 0)
+def aperture_kernel(at_ref, pin_ref, m0_ref, m1_ref, m2_ref, hx_ref, hy_ref, out_ref):
+    outer = at_ref[0]
+    for g in range(5):
+        if g < 3:
+            moved = (m0_ref, m1_ref, m2_ref)[g]
+            rows = jnp.where(outer > g, moved[...], pin_ref[8 * g:8 * g + 8, :]).astype(F32)
+        else:
+            rows = pin_ref[8 * g:8 * g + 8, :].astype(F32)
+        for t in range(3):
+            block = jnp.concatenate([rows[:, 128 * (t + 3 * k):128 * (t + 3 * k) + 128] for k in range(16)], 0)
             block = block.T
             h = turn((hx_ref[0, t], hx_ref[1, t]), (hy_ref[0, g:g + 1, :], hy_ref[1, g:g + 1, :]))
             for p in range(2):
                 out_ref[p, t, g] = block * h[p]
 
 
-def call(kernel, outs, args, scratch=(), flops=0):
-    size = sum(a.size * a.dtype.itemsize for a in args)
+def nbytes(a):
+    return math.prod(a.shape) * jnp.dtype(a.dtype).itemsize
+
+
+def call(kernel, outs, args, scratch=(), spec=None):
+    size = sum(nbytes(a) for a in args) + sum(nbytes(o) for o in jax.tree.leaves(outs))
+    held = sum(math.prod(r.shape) * jnp.dtype(r.dtype).itemsize for r in scratch)
     return pl.pallas_call(
         kernel,
         out_shape=outs,
         scratch_shapes=list(scratch),
-        compiler_params=pltpu.CompilerParams(vmem_limit_bytes=VMEM_LIMIT),
-        cost_estimate=pl.CostEstimate(flops=flops, bytes_accessed=size + 2_400_000, transcendentals=0),
+        compiler_params=pltpu.CompilerParams(vmem_limit_bytes=size + held + 8 * 2**20),
+        cost_estimate=pl.CostEstimate(flops=0, bytes_accessed=size, transcendentals=0),
+        **(spec or {}),
     )(*args)
 
 
@@ -362,6 +391,27 @@
 
 def exchange(x, axis):
     return lax.all_to_all(x, axis, split_axis=0, concat_axis=0, tiled=True)
+
+
+def make_aperture(pinhole, me, tb):
+    turned = pinhole.T
+    moves = [[(int(b), EDGE + i) for i, b in enumerate(m)] for m in MOVED]
+    moved = [lax.ppermute(turned[40:48], ("rows", "cols"), pairs) for pairs in moves]
+    place = me - EDGE
+    inside = (place >= 0) & (place < DEV - 2 * EDGE)
+    taken = jnp.where(inside, 2 + (place < len(MOVED[2])).astype(jnp.int32), 0)
+    ky = 48 * me + 8 * jnp.arange(6, dtype=jnp.int32)
+    for slot, m in enumerate(MOVED):
+        source = jnp.asarray(m, jnp.int32)[jnp.clip(place, 0, len(m) - 1)]
+        ky = ky.at[slot].set(jnp.where(taken > slot, 48 * source + 40, ky[slot]))
+    ky = ky[:, None, None] + jnp.arange(8, dtype=jnp.int32)[None, None, :]
+    angle = -chirp_angle(jnp.broadcast_to(ky, (6, 16, 8)).reshape(6, 128))
+    h_y = jnp.stack([jnp.cos(angle), jnp.sin(angle)])
+    whole = pl.BlockSpec(memory_space=pltpu.VMEM)
+    return call(
+        aperture_kernel, shape(2, 3, 5, 128, 128), (taken.reshape(1), turned, *moved, tb["h_x"], h_y),
+        spec=dict(in_specs=[pl.BlockSpec(memory_space=pltpu.SMEM)] + [whole] * 6),
+    )
 
 
 def per_device(field_real, field_imag, kerr_map, pinhole):
@@ -373,42 +423,45 @@
     kerr_rows = exchange(kerr_map.reshape(8, 48, 768), "cols")
     ax0 = chirp_angle(row_at * 384 + ints(384)).reshape(384, 1)
     ay0 = chirp_angle(col_at * 768 + ints(768)).reshape(1, 768)
+    strip = pl.BlockSpec((128, 768), lambda i: (i, 0))
+    enter = dict(
+        grid=(3,),
+        in_specs=[strip, strip, strip, pl.BlockSpec((128, 1), lambda i: (i, 0)), pl.BlockSpec((1, 768), lambda i: (0, 0))],
+        out_specs=(pl.BlockSpec((16, 96, 128), lambda i: (0, 0, i)), strip),
+    )
     sent, phase_one = call(
-        enter_kernel, (shape(16, 96, 384), shape(384, 768)), (field_real, field_imag, kerr_map, ax0, ay0)
+        enter_kernel, (shape(16, 96, 384), shape(384, 768)), (field_real, field_imag, kerr_map, ax0, ay0), spec=enter
     )
     cols = exchange(sent, "rows")
     sent = call(
-        columns_kernel, shape(DEV * PITCH, 128), (cols, tb["d384"], tb["tw1"]),
-        (pltpu.VMEM((768, 768), BF16), pltpu.VMEM((768, 768), BF16)),
+        columns_kernel, shape(DEV * PITCH, 128), (cols, tb["l_plain"], tb["tw_rho_j"]),
+        (pltpu.VMEM((3, 16, 2, 8, 128), F32), pltpu.VMEM((384, 256), BF16), pltpu.VMEM((384, 256), BF16)),
     )
     rows = exchange(sent.reshape(DEV, PITCH, 128), both).reshape(DEV * PITCH, 128)
     ax1 = chirp_angle(me * 48 + 16 * ints(3)[:, None, None] + ints(16)[None, None, :])
     ax1 = jnp.broadcast_to(ax1, (3, 8, 16)).reshape(384, 1)
     pair6 = (pltpu.VMEM((6, 128, 256), BF16), pltpu.VMEM((6, 128, 256), BF16))
     sent, phase_two = call(
-        rows_kernel, (shape(DEV * PITCH, 128), shape(8, 48, 768)),
+        rows_kernel, (shape(DEV * KEPT, 128), shape(8, 48, 768)),
         (rows, kerr_rows, ax1, tb["chirp_y"], tb["l_mixed"], tb["m_first"], tb["m_second"], tb["l_plain"],
          tb["tw_u_a"], tb["tw_a_u"]),
         (pltpu.VMEM((256, 768), F32), pltpu.VMEM((6, 256, 128), F32)) + pair6,
     )
-    far = exchange(sent.reshape(DEV, PITCH, 128), both).reshape(DEV * PITCH, 128)
-    ky = me * 48 + 8 * ints(6)[:, None, None] + ints(8)[None, None, :]
-    ky_angle = -chirp_angle(jnp.broadcast_to(ky, (6, 16, 8)).reshape(6, 128))
-    h_y = jnp.stack([jnp.cos(ky_angle), jnp.sin(ky_angle)])
-    aperture = call(
-        aperture_kernel, shape(2, 3, 6, 128, 128), (pinhole, tb["h_x"], h_y), (pltpu.VMEM((48, N), F32),)
-    )
+    far = exchange(sent.reshape(DEV, KEPT, 128), both).reshape(DEV * KEPT, 128)
+    far, phase_two = lax.optimization_barrier((far, phase_two))
+    phase_back = exchange(phase_two, "cols").reshape(384, 768)
+    aperture = make_aperture(pinhole, me, tb)
     pair3 = (pltpu.VMEM((3, 128, 256), BF16), pltpu.VMEM((3, 128, 256), BF16))
     sent = call(
-        far_field_kernel, shape(DEV * PITCH, 128),
+        far_field_kernel, shape(DEV * KEPT, 128),
         (far, aperture, tb["l_plain"], tb["r_in"], tb["r_out"], tb["tw_u_rho"]),
         (pltpu.VMEM((256, 384), F32), pltpu.VMEM((3, 128, 256), F32)) + pair3,
     )
-    phase_back = exchange(phase_two, "cols").reshape(384, 768)
+    sent, phase_back = lax.optimization_barrier((sent, phase_back))
+    near = exchange(sent.reshape(DEV, KEPT, 128), both).reshape(DEV * KEPT, 128)
     b_integral = phase_one + phase_back
-    near = exchange(sent.reshape(DEV, PITCH, 128), both).reshape(DEV * PITCH, 128)
     sent = call(
-        leave_kernel, shape(8, 96, 768), (near, tb["l_plain"], tb["m_first"], tb["tw_u_a"]),
+        leave_kernel, shape(8, 96, 768), (near, tb["l_kept"], tb["l_moved"], tb["m_first"], tb["tw_u_a"]),
         (pltpu.VMEM((256, 768), F32),) + pair6,
     )
     out = exchange(sent, "cols")

time: 286 us -> 285 us (level)
  blocking collectives: 81.4 us -> 115 us
  waiting for transfers between devices: 103 us -> 72.1 us
  Pallas kernels: 60.2 us -> 36.5 us
  local copies, waits for them, and re-layouts: 9.72 us -> 26.5 us
    all_to_all x2 -> x3, blocking collectives: 81.4 us -> 115 us  [exchange(): return lax.all_to_all(x, axis, split_axis=0, concat_axis=0, tiled=True)]
    all_to_all x5 -> x4, waiting for transfers between devices: 103 us -> 72 us  [exchange(): return lax.all_to_all(x, axis, split_axis=0, concat_axis=0, tiled=True)]
    pallas_call x6, Pallas kernels: 60.2 us -> 36.5 us  [call(): pl.pallas_call(kernel, out_shape=outs, scratch_shapes=list(scratch), comp...]
    unnamed x7 -> x62, local copies, waits for them, and re-layouts: 7.23 us -> 19.9 us
    ppermute x0 -> x3, starting transfers between devices: none -> 7.17 us  [make_aperture(): lax.ppermute(turned[40:48], ('rows', 'cols'), pairs)]
    all_to_all x5 -> x4, starting transfers between devices: 22.9 us -> 17.6 us  [exchange(): return lax.all_to_all(x, axis, split_axis=0, concat_axis=0, tiled=True)]
    slice x0 -> x3, local copies, waits for them, and re-layouts: none -> 2.86 us  [the longest x1 1.62 us: make_aperture(): turned[40:48]]
  transfers between devices with their start and end apart: 5 -> 7, of which waited for: 5 -> 4; matrix products, arithmetic and copies ran while one was open for 3% -> 3% of each run, Pallas kernels for 8% -> 5%
where the time goes in v2:
time: 285 us; the launch traced here: 281 us
  blocking collectives  115 us (40%)
  waiting for transfers between devices  72.1 us (25%)
  Pallas kernels  36.5 us (13%)
  local copies, waits for them, and re-layouts  26.5 us (9%)
  starting transfers between devices  24.8 us (9%)
  between operations  3.46 us (1%)
    all_to_all x3, blocking collectives, exchange(): return lax.all_to_all(x, axis, split_axis=0, concat_axis=0, tiled=True)  115 us
    all_to_all x4, waiting for transfers between devices, exchange(): return lax.all_to_all(x, axis, split_axis=0, concat_axis=0, tiled=True)  72 us
    pallas_call x6, Pallas kernels, call(): pl.pallas_call(kernel, out_shape=outs, scratch_shapes=list(scratch), comp...  36.5 us
    unnamed x62, local copies, waits for them, and re-layouts  19.9 us
    all_to_all x4, starting transfers between devices, exchange(): return lax.all_to_all(x, axis, split_axis=0, concat_axis=0, tiled=True)  17.6 us
    ppermute x3, starting transfers between devices, make_aperture(): lax.ppermute(turned[40:48], ('rows', 'cols'), pairs)  7.17 us
  transfers between devices with their start and end apart: 7, of which 4 were waited for; matrix products, arithmetic and copies ran while one was open for 3% of the time, Pallas kernels for 5%

profile of v2, /device:TPU:1, one launch (start us, length us, event | category | flops | bytes accessed | tf_op | source)
XLA Modules:
  0.0 281.4 jit_solution(5610419966210757576)
XLA Ops:
  0.6 0.1 fusion.2.ax_ref
  0.8 1.3 copy-done.6
  2.1 1.3 copy-done.16
  3.4 1.3 copy-done.17
  4.6 2.7 shard_map.220
  7.3 40.2 %all_to_all.35.in_ref = f32[16,96,384]{2,1,0:T(8,128)S(1)} all-to-all(f32[16,96,384]{2,1,0:T(8,128)S(1)} %get-tuple-element.47), channel_id=1, replica_groups=mesh['rows'=16,'cols'=8] {'rows'}, dimensions={0} | all-to-all | bytes 4718592 | tf_op jit(solution)/shard_map/all_to_all | solution.py:393
  47.6 4.5 %all-to-all-start.2 = ((f32[8,48,768]{2,1,0:T(8,128)}), f32[8,48,768]{2,1,0:T(8,128)S(1)}, u32[]{:S(2)}, u32[]{:S(2)}) async-start(f32[8,48,768]{2,1,0:T(8,128)} %bitcast.26), calls=%async_computation.2 | async-start | bytes 2359296 | tf_op jit(solution)/shard_map/all_to_all | solution.py:393
  52.0 0.9 copy-done.8
  53.0 0.8 copy-done.28
  53.8 3.4 %shard_map.221 = f32[5120,128]{1,0:T(8,128)S(1)} custom-call(f32[16,96,384]{2,1,0:T(8,128)S(1)} %all_to_all.35.in_ref, bf16[2,256,256]{2,1,0:T(8,128)(2,1)S(1)} %copy-done.8, f32[2,48,1,128]{3,2,1,0:T(1,128)S(1)} %copy-done.28), custom_call_target="tpu_custom_call" | custom-call | bytes 5292032 | tf_op jit(solution)/shard_map/pallas_call | solution.py:378
  57.2 1.5 copy-done
  58.6 10.6 %all-to-all-done.2.kerr_ref = f32[8,48,768]{2,1,0:T(8,128)S(1)} async-done(((f32[8,48,768]{2,1,0:T(8,128)}), f32[8,48,768]{2,1,0:T(8,128)S(1)}, u32[]{:S(2)}, u32[]{:S(2)}) %all-to-all-start.2) | async-done | bytes 1179680 | tf_op jit(solution)/shard_map/all_to_all | solution.py:393
  69.3 1.0 copy-done.4
  70.3 4.5 %all-to-all-start.1 = ((f32[128,40,128]{2,1,0:T(8,128)}), f32[128,40,128]{2,1,0:T(8,128)S(1)}, u32[]{:S(2)}, u32[]{:S(2)}) async-start(f32[128,40,128]{2,1,0:T(8,128)} %bitcast.22), calls=%async_computation.1 | async-start | bytes 5242880 | tf_op jit(solution)/shard_map/all_to_all | solution.py:393
  74.8 0.1 fusion.17
  74.9 0.8 reshape.379.ax_ref
  75.7 33.9 %all-to-all-done.1 = f32[128,40,128]{2,1,0:T(8,128)S(1)} async-done(((f32[128,40,128]{2,1,0:T(8,128)}), f32[128,40,128]{2,1,0:T(8,128)S(1)}, u32[]{:S(2)}, u32[]{:S(2)}) %all-to-all-start.1) | async-done | bytes 2621472 | tf_op jit(solution)/shard_map/all_to_all | solution.py:393
  109.6 1.4 copy-done.2
  111.0 1.3 copy-done.5
  112.3 0.9 copy-done.9
  113.3 1.4 copy-done.12
  114.7 1.1 copy-done.20
  115.8 0.9 copy-done.21
  116.7 1.0 copy-done.23
  117.7 0.9 copy-done.27
  118.7 12.6 %shard_map.222 = (f32[4096,128]{1,0:T(8,128)S(1)}, f32[8,48,768]{2,1,0:T(8,128)S(1)}) custom-call(f32[5120,128]{1,0:T(8,128)S(1)} %bitcast.21, f32[8,48,768]{2,1,0:T(8,128)S(1)} %copy-done.5, f32[384,1]{1,0:T(8,128)S(1)} %copy-done.21, f32[6,128,128]{2,1,0:T(8,128)S(1)} %copy-done.23, bf16[2,256,256]{2,1,0:T(8,128)(2,1)S(1)} %copy-done.27, ...), custom_call_target="tpu_custom_call" | custom-call | bytes 12715520 | tf_op jit(solution)/shard_map/pallas_call | solution.py:378
  131.3 34.8 %all_to_all.36 = f32[128,32,128]{2,1,0:T(8,128)S(1)} all-to-all(f32[128,32,128]{2,1,0:T(8,128)S(1)} %bitcast.27), channel_id=1, replica_groups=mesh['rows'=16,'cols'=8] {'rows','cols'}, dimensions={0} | all-to-all | bytes 4194304 | tf_op jit(solution)/shard_map/all_to_all | solution.py:393
  166.1 4.4 %all-to-all-start.4 = ((f32[8,48,768]{2,1,0:T(8,128)}), f32[8,48,768]{2,1,0:T(8,128)}, u32[]{:S(2)}, u32[]{:S(2)}) async-start(f32[8,48,768]{2,1,0:T(8,128)} %copy-done.15), calls=%async_computation.4 | async-start | bytes 2359296 | tf_op jit(solution)/shard_map/all_to_all | solution.py:393
  170.5 1.6 slice.56
  172.1 4.5 %collective-permute-start = (s32[8,6144]{1,0:T(8,128)}, s32[8,6144]{1,0:T(8,128)S(1)}, u32[]{:S(2)}, u32[]{:S(2)}) collective-permute-start(s32[8,6144]{1,0:T(8,128)} %slice.56), channel_id=1, source_target_pairs={{0,44},{1,45},{2,46},{3,47},{4,48},{5,49},{6,50},{7,51},{8,52},{9,... | collective-permute-start | bytes 589832 | tf_op jit(solution)/shard_map/ppermute | solution.py:399
  176.6 1.3 collective-permute-start.1
  178.0 1.3 collective-permute-start.2
  179.4 0.7 dynamic_slice.10
  180.1 0.6 slice.52
  181.9 0.6 dynamic_slice.11
  183.2 0.6 slice.53
  184.6 0.1 rem.76
  184.8 1.3 copy-done.11
  186.1 1.6 shard_map.223.ph_ref
  187.7 0.1 copy-done.22
  187.8 9.4 %shard_map.224 = f32[4096,128]{1,0:T(8,128)S(1)} custom-call(f32[4096,128]{1,0:T(8,128)S(1)} %bitcast.24, f32[2,3,5,128,128]{4,3,2,1,0:T(8,128)S(1)} %shard_map.223.ph_ref, bf16[2,256,256]{2,1,0:T(8,128)(2,1)S(1)} %copy-done.10, bf16[2,3,256,256]{3,2,1,0:T(8,128)(2,1)S(1)} %copy-done.18, bf16[2,3,256,256]{3,2,1,0:T(8,128)(2,1)S(1)} %copy-done.19, ...), custom_call_target="tpu_custom_call" | custom-call | bytes 8388608 | tf_op jit(solution)/shard_map/pallas_call | solution.py:378
  197.3 1.3 copy-done.1
  198.6 40.1 %all_to_all.37 = f32[128,32,128]{2,1,0:T(8,128)S(1)} all-to-all(f32[128,32,128]{2,1,0:T(8,128)} %bitcast.25), channel_id=1, replica_groups=mesh['rows'=16,'cols'=8] {'rows','cols'}, dimensions={0} | all-to-all | bytes 4194304 | tf_op jit(solution)/shard_map/all_to_all | solution.py:393
  238.7 6.9 %shard_map.225 = f32[8,96,768]{2,1,0:T(8,128)} custom-call(f32[4096,128]{1,0:T(8,128)S(1)} %bitcast.23, bf16[2,256,256]{2,1,0:T(8,128)(2,1)S(1)} %copy-done.25, bf16[2,256,176]{2,1,0:T(8,128)(2,1)S(1)} %copy-done.26, bf16[2,6,256,256]{3,2,1,0:T(8,128)(2,1)S(1)} %copy-done.3, f32[2,6,128,128]{3,2,1,0:T(8,128)S(1)} %copy-done.7), custom_call_target="tpu_custom_call" | custom-call | bytes 7258112 | tf_op jit(solution)/shard_map/pallas_call | solution.py:378
  245.7 4.2 %all-to-all-start.6 = ((f32[8,96,768]{2,1,0:T(8,128)}), f32[8,96,768]{2,1,0:T(8,128)S(1)}, u32[]{:S(2)}, u32[]{:S(2)}) async-start(f32[8,96,768]{2,1,0:T(8,128)} %shard_map.225), calls=%async_computation.6 | async-start | bytes 4718592 | tf_op jit(solution)/shard_map/all_to_all | solution.py:393
  249.9 2.4 add.281
  252.4 27.4 %all-to-all-done.6 = f32[8,96,768]{2,1,0:T(8,128)S(1)} async-done(((f32[8,96,768]{2,1,0:T(8,128)}), f32[8,96,768]{2,1,0:T(8,128)S(1)}, u32[]{:S(2)}, u32[]{:S(2)}) %all-to-all-start.6) | async-done | bytes 2359328 | tf_op jit(solution)/shard_map/all_to_all | solution.py:393
  279.8 1.6 fusion.21
  (59 shorter events, 0.4 us)
Async XLA Ops:
  0.8 1.3 copy-start.6
  2.1 1.3 copy-start.16
  3.4 1.3 copy-start.17
  7.3 40.3 %copy-start.13 = (f32[384,768]{1,0:T(8,128)}, f32[384,768]{1,0:T(8,128)S(1)}, u32[]{:S(2)}) copy-start(f32[384,768]{1,0:T(8,128)S(1)} %get-tuple-element.53) | copy-start | bytes 3538948
  47.6 21.7 %all-to-all-start.2 = ((f32[8,48,768]{2,1,0:T(8,128)}), f32[8,48,768]{2,1,0:T(8,128)S(1)}, u32[]{:S(2)}, u32[]{:S(2)}) async-start(f32[8,48,768]{2,1,0:T(8,128)} %bitcast.26), calls=%async_computation.2 | async-start | bytes 2359296 | tf_op jit(solution)/shard_map/all_to_all | solution.py:393
  52.0 0.9 copy-start.8
  53.0 0.8 copy-start.28
  57.2 1.5 copy-start
  69.2 1.0 copy-start.4
  70.3 39.4 %copy-start.7 = (f32[2,6,128,128]{3,2,1,0:T(8,128)S(1)}, f32[2,6,128,128]{3,2,1,0:T(8,128)}, u32[]{:S(2)}) copy-start(f32[2,6,128,128]{3,2,1,0:T(8,128)} %constant.204.clone.tw_ref) | copy-start | bytes 2359300
  70.3 39.4 %all-to-all-start.1 = ((f32[128,40,128]{2,1,0:T(8,128)}), f32[128,40,128]{2,1,0:T(8,128)S(1)}, u32[]{:S(2)}, u32[]{:S(2)}) async-start(f32[128,40,128]{2,1,0:T(8,128)} %bitcast.22), calls=%async_computation.1 | async-start | bytes 5242880 | tf_op jit(solution)/shard_map/all_to_all | solution.py:393
  109.6 1.4 copy-start.2
  111.0 1.3 copy-start.5
  112.3 0.9 copy-start.9
  113.3 1.4 copy-start.12
  114.7 1.1 copy-start.20
  115.8 0.9 copy-start.21
  116.7 1.0 copy-start.23
  117.7 0.9 copy-start.27
  131.2 34.9 %copy-start.15 = (f32[8,48,768]{2,1,0:T(8,128)}, f32[8,48,768]{2,1,0:T(8,128)S(1)}, u32[]{:S(2)}) copy-start(f32[8,48,768]{2,1,0:T(8,128)S(1)} %get-tuple-element.51) | copy-start | bytes 3538948
  166.1 13.3 %copy-start.30 = (s32[40]{0:T(128)S(1)}, s32[40]{0:T(128)}, u32[]{:S(2)}) copy-start(s32[40]{0:T(128)} %constant.211.clone) | copy-start | bytes 484
  166.1 15.8 %copy-start.29 = (s32[8]{0:T(128)S(1)}, s32[8]{0:T(128)}, u32[]{:S(2)}) copy-start(s32[8]{0:T(128)} %constant.212.clone) | copy-start | bytes 100
  166.1 18.7 %copy-start.24 = (f32[2,3,128,128]{3,2,1,0:T(8,128)S(1)}, f32[2,3,128,128]{3,2,1,0:T(8,128)}, u32[]{:S(2)}) copy-start(f32[2,3,128,128]{3,2,1,0:T(8,128)} %constant.209.clone.hx_ref) | copy-start | bytes 1179652
  166.1 32.5 %all-to-all-start.4 = ((f32[8,48,768]{2,1,0:T(8,128)}), f32[8,48,768]{2,1,0:T(8,128)}, u32[]{:S(2)}, u32[]{:S(2)}) async-start(f32[8,48,768]{2,1,0:T(8,128)} %copy-done.15), calls=%async_computation.4 | async-start | bytes 2359296 | tf_op jit(solution)/shard_map/all_to_all | solution.py:393
  172.1 12.6 %collective-permute-start = (s32[8,6144]{1,0:T(8,128)}, s32[8,6144]{1,0:T(8,128)S(1)}, u32[]{:S(2)}, u32[]{:S(2)}) collective-permute-start(s32[8,6144]{1,0:T(8,128)} %slice.56), channel_id=1, source_target_pairs={{0,44},{1,45},{2,46},{3,47},{4,48},{5,49},{6,50},{7,51},{8,52},{9,... | collective-permute-start | bytes 589832 | tf_op jit(solution)/shard_map/ppermute | solution.py:399
  176.6 8.2 %collective-permute-start.1 = (s32[8,6144]{1,0:T(8,128)}, s32[8,6144]{1,0:T(8,128)}, u32[]{:S(2)}, u32[]{:S(2)}) collective-permute-start(s32[8,6144]{1,0:T(8,128)} %slice.56), channel_id=1, source_target_pairs={{88,44},{89,45},{90,46},{91,47},{92,48},{93,49},{94,50},{95,51},{9... | collective-permute-start | bytes 589832 | tf_op jit(solution)/shard_map/ppermute | solution.py:399
  178.0 6.8 %collective-permute-start.2 = (s32[8,6144]{1,0:T(8,128)}, s32[8,6144]{1,0:T(8,128)}, u32[]{:S(2)}, u32[]{:S(2)}) collective-permute-start(s32[8,6144]{1,0:T(8,128)} %slice.56), channel_id=1, source_target_pairs={{40,44},{41,45},{42,46},{43,47},{84,48},{85,49},{86,50},{87,51}} | collective-permute-start | bytes 589832 | tf_op jit(solution)/shard_map/ppermute | solution.py:399
  184.8 1.3 copy-start.11
  186.1 1.6 copy-start.10
  186.1 1.6 copy-start.18
  186.1 1.6 copy-start.19
  186.1 1.7 copy-start.22
  197.3 1.4 copy-start.1
  198.6 40.1 %copy-start.3 = (bf16[2,6,256,256]{3,2,1,0:T(8,128)(2,1)S(1)}, bf16[2,6,256,256]{3,2,1,0:T(8,128)(2,1)}, u32[]{:S(2)}) copy-start(bf16[2,6,256,256]{3,2,1,0:T(8,128)(2,1)} %constant.202.clone.m_ref) | copy-start | bytes 4718596
  198.6 40.1 %copy-start.25 = (bf16[2,256,256]{2,1,0:T(8,128)(2,1)S(1)}, bf16[2,256,256]{2,1,0:T(8,128)(2,1)}, u32[]{:S(2)}) copy-start(bf16[2,256,256]{2,1,0:T(8,128)(2,1)} %constant.200.clone.l_ref) | copy-start | bytes 786436
  198.6 40.1 %copy-start.26 = (bf16[2,256,176]{2,1,0:T(8,128)(2,1)S(1)}, bf16[2,256,176]{2,1,0:T(8,128)(2,1)}, u32[]{:S(2)}) copy-start(bf16[2,256,176]{2,1,0:T(8,128)(2,1)} %constant.201.clone.lm_ref) | copy-start | bytes 540676
  245.7 4.2 %copy-start.14 = (f32[384,768]{1,0:T(8,128)S(1)}, f32[384,768]{1,0:T(8,128)}, u32[]{:S(2)}) copy-start(f32[384,768]{1,0:T(8,128)} %copy-done.13) | copy-start | bytes 3538948
  245.7 34.1 %all-to-all-start.6 = ((f32[8,96,768]{2,1,0:T(8,128)}), f32[8,96,768]{2,1,0:T(8,128)S(1)}, u32[]{:S(2)}, u32[]{:S(2)}) async-start(f32[8,96,768]{2,1,0:T(8,128)} %shard_map.225), calls=%async_computation.6 | async-start | bytes 4718592 | tf_op jit(solution)/shard_map/all_to_all | solution.py:393

commit v3 on v2

--- a/solution.py
+++ b/solution.py
@@ -55,27 +55,35 @@
     lane_q, lane_8 = r128 // 8, r128 % 8
     row_8, row_q = r128 // 16, r128 % 16
     same = (row_q[:, None] == lane_q[None, :]).astype(np.float64)
-    g6 = np.arange(6)[:, None, None]
-    first = same * root(48, lane_8[None, None, :] * g6 + 6 * row_8[None, :, None] * lane_8[None, None, :]) * s48
-    t["m_first"] = np.stack([halves(real_form(m)) for m in first], 1)
-    second = same.T * root(48, g6 * lane_8[None, :, None] + 6 * row_8[None, None, :] * lane_8[None, :, None]) * s48
-    t["m_second"] = np.stack([halves(real_form(m)) for m in second], 1)
-    a = lane_8[None, :] + 8 * np.arange(6)[:, None]
-    tw = root(N, r128[None, :, None] * a[:, None, :])
-    t["tw_u_a"] = planes(tw)
-    t["tw_a_u"] = planes(tw.transpose(0, 2, 1))
+    eight = same * root(8, row_8[:, None] * lane_8[None, :]) * s48
+    t["m_first"] = halves(real_form(eight))
+    t["m_second"] = halves(real_form(eight.T))
+    six = np.arange(6)
+    t["v_6"] = planes(root(48, six[:, None, None] * lane_8[None, None, :]))
+    t["v_6_rows"] = planes(root(48, six[:, None, None] * (np.arange(16) % 8)[None, :, None]) * np.ones((1, 1, 128)))
+    a = lane_8[None, :] + 8 * six[:, None]
+    t["tw_u_a"] = planes(root(N, r128[None, :, None] * a[:, None, :]))
+    a = np.arange(16)[None, :] % 8 + 8 * six[:, None]
+    t["tw_a_u"] = planes(root(N, r128[None, None, :] * a[:, :, None]))
     keep = (lane_8[:, None] == lane_8[None, :]).astype(np.float64)
-    v3 = np.arange(3)[:, None, None]
-    into = keep * root(48, lane_q[None, :, None] * v3 + 3 * lane_q[None, :, None] * lane_q[None, None, :]) * s48
-    t["r_in"] = np.stack([halves(real_form(m.T).T) for m in into], 1)
-    back = keep * root(48, lane_q[None, None, :] * v3 + 3 * lane_q[None, :, None] * lane_q[None, None, :]) * s48
-    t["r_out"] = np.stack([halves(real_form(m.T).T) for m in back], 1)
+    sixteen = keep * root(16, lane_q[:, None] * lane_q[None, :]) * s48
+    t["r_16"] = halves(real_form(sixteen).T)
+    t["v_3"] = planes(root(48, np.arange(3)[:, None, None] * lane_q[None, None, :]))
     rho = lane_q[None, :] + 16 * np.arange(3)[:, None]
     t["tw_u_rho"] = planes(root(N, r128[None, :, None] * rho[:, None, :]))
     kx = r128[None, :, None] + 128 * (np.arange(3)[:, None, None] + 3 * lane_q[None, None, :])
     t["h_x"] = planes(root(2 * N, kx * kx))
-    y = r128[None, None, :] + 128 * (np.arange(6)[:, None, None] + 6 * row_8[None, :, None])
+    y = r128[None, None, :] + 128 * (six[:, None, None] + 6 * np.arange(8)[None, :, None])
     t["chirp_y"] = (math.pi / N * ((y * y + N) % (2 * N) - N)).astype(np.float32)
+    taken = np.zeros(DEV, np.int32)
+    ky = 48 * np.arange(DEV)[:, None] + 8 * np.arange(6)[None, :]
+    for slot, m in enumerate(MOVED):
+        for place, b in enumerate(m):
+            taken[EDGE + place] = slot + 1
+            ky[EDGE + place, slot] = 48 * b + 40
+    t["taken"] = taken
+    ky = ky[:, :, None] + lane_8[None, None, :]
+    t["h_y"] = planes(root(2 * N, ky * ky)).transpose(1, 0, 2, 3)
     return t
 
 
@@ -83,7 +91,9 @@
 
 
 def chirp_angle(index):
-    return math.pi / N * ((index * index + N) % (2 * N) - N).astype(F32)
+    square = index * index
+    turns = (square.astype(F32) * (0.5 / N)).astype(jnp.int32)
+    return (math.pi / N) * (square - 2 * N * turns).astype(F32)
 
 
 def sin_cos(angle):
@@ -186,13 +196,17 @@
     return out
 
 
-def enter_kernel(re_ref, im_ref, kerr_ref, ax_ref, ay_ref, out_ref, phase_ref):
+def enter_kernel(me_ref, re_ref, im_ref, kerr_ref, out_ref, phase_ref):
+    top = (me_ref[0] // 8) * 384 + pl.program_id(0) * 128
+    left = (me_ref[0] % 8) * 768
+    ax = chirp_angle(top + lax.broadcasted_iota(jnp.int32, (128, 128), 0))
     for lb in range(6):
+        ay = chirp_angle(left + 128 * lb + lax.broadcasted_iota(jnp.int32, (1, 128), 1))
         cols = slice(128 * lb, 128 * lb + 128)
         re, im = re_ref[:, cols], im_ref[:, cols]
         phase = kerr_ref[:, cols] * (re * re + im * im)
         phase_ref[:, cols] = phase
-        s, c = sin_cos(phase + (ax_ref[...] + ay_ref[:, cols]))
+        s, c = sin_cos(phase + (ax + ay))
         both = turn((re, im), (c, s))
         for p in range(2):
             turned = both[p].T
@@ -201,7 +215,8 @@
                 out_ref[l // 48, pl.ds(48 * p + l % 48, 16), :] = turned[16 * i:16 * i + 16]
 
 
-def columns_kernel(in_ref, l_ref, tw_ref, out_ref, z_ref, high_ref, low_ref):
+def columns_kernel(in_ref, tw_ref, l_ref, out_ref, z_ref, high_ref, low_ref):
+
     def body(lh, _):
         low = pl.ds(pl.multiple_of(8 * lh, 8), 8)
         high = pl.ds(pl.multiple_of(48 + 8 * lh, 8), 8)
@@ -244,7 +259,7 @@
     out_ref[:, :data.shape[1]] = dot_left(table, split(data), NN)
 
 
-def after_senders(tw_ref, y_ref, high_ref, low_ref):
+def after_senders(tw_ref, v_ref, y_ref, high_ref, low_ref):
     for u in range(0, 128, 16):
         z = []
         for t in range(6):
@@ -252,6 +267,7 @@
             w = (tw_ref[0, t, u:u + 16, :], tw_ref[1, t, u:u + 16, :])
             z.append(turn((y_ref[u:u + 16, lanes], y_ref[128 + u:144 + u, lanes]), w))
         z = dft6(z)
+        z = [z[0]] + [turn(z[t], (v_ref[0, t], v_ref[1, t])) for t in range(1, 6)]
         for t in range(6):
             for p in range(2):
                 h, l = split(z[t][p])
@@ -259,26 +275,29 @@
                 low_ref[t, u:u + 16, 128 * p:128 * p + 128] = l
 
 
-def rows_kernel(in_ref, kerr_ref, ax_ref, ay_ref, l_ref, m_ref, m2_ref, l2_ref, tw_ref, tw2_ref,
+def rows_kernel(me_ref, in_ref, kerr_ref, l_ref, tw_ref, v_ref, m_ref, ay_ref, m2_ref, v2_ref, tw2_ref, l2_ref,
                 out_ref, phase_ref, y_ref, w_ref, high_ref, low_ref):
+
     def body(j, _):
         over_senders(in_ref, [(12 * j + t, 12 * j + 6 + t) for t in range(6)], PITCH, (l_ref[0], l_ref[1]), y_ref)
-        after_senders(tw_ref, y_ref, high_ref, low_ref)
+        after_senders(tw_ref, v_ref, y_ref, high_ref, low_ref)
         rows = pl.ds(pl.multiple_of(16 * j, 16), 16)
-        ax = ax_ref[pl.ds(pl.multiple_of(128 * j, 128), 128), :]
+        ax = chirp_angle(48 * me_ref[0] + 16 * j + lax.broadcasted_iota(jnp.int32, (128, 128), 0) % 16)
         for t in range(6):
-            z = dot_left((m_ref[0, t], m_ref[1, t]), (high_ref[t], low_ref[t]), NT)
+            z = dot_left((m_ref[0], m_ref[1]), (high_ref[t], low_ref[t]), NT)
             re, im = z[:128], z[128:]
             lanes = slice(128 * t, 128 * t + 128)
             phase = kerr_ref[:, rows, lanes].reshape(128, 128) * (re * re + im * im)
             phase_ref[:, rows, lanes] = phase.reshape(8, 16, 128)
-            s, c = sin_cos(phase + (ax + ay_ref[t]))
+            ay = jnp.concatenate([jnp.broadcast_to(ay_ref[t, k:k + 1, :], (16, 128)) for k in range(8)], 0)
+            s, c = sin_cos(phase + (ax + ay))
             both = jnp.concatenate(turn((im, -re), (c, s)), 0)
-            w_ref[t] = dot_left((m2_ref[0, t], m2_ref[1, t]), split(both), NN)
+            w_ref[t] = dot_left((m2_ref[0], m2_ref[1]), split(both), NN)
         for r in range(0, 128, 16):
-            z = dft6([(w_ref[t, r:r + 16, :], w_ref[t, 128 + r:144 + r, :]) for t in range(6)])
+            z = [(w_ref[t, r:r + 16, :], w_ref[t, 128 + r:144 + r, :]) for t in range(6)]
+            z = dft6([z[0]] + [turn(z[t], (v2_ref[0, t], v2_ref[1, t])) for t in range(1, 6)])
             for t in range(6):
-                q = turn(z[t], (tw2_ref[0, t, r:r + 16, :], tw2_ref[1, t, r:r + 16, :]))
+                q = turn(z[t], (tw2_ref[0, t], tw2_ref[1, t]))
                 for p in range(2):
                     h, l = split(q[p])
                     high_ref[t, r:r + 16, 128 * p:128 * p + 128] = h
@@ -301,7 +320,8 @@
     lax.fori_loop(0, 3, body, 0)
 
 
-def far_field_kernel(in_ref, ph_ref, l_ref, r_ref, r2_ref, tw_ref, out_ref, y_ref, w_ref, high_ref, low_ref):
+def far_field_kernel(in_ref, ph_ref, l_ref, tw_ref, v_ref, r_ref, out_ref, y_ref, w_ref, high_ref, low_ref):
+
     def body(g, _):
         over_senders(in_ref, [(6 * g + 2 * j, 6 * g + 2 * j + 1) for j in range(3)], KEPT, (l_ref[0], l_ref[1]), y_ref)
         for u in range(0, 128, 16):
@@ -311,17 +331,19 @@
                 w = (tw_ref[0, t, u:u + 16, :], tw_ref[1, t, u:u + 16, :])
                 z.append(turn((y_ref[u:u + 16, lanes], y_ref[128 + u:144 + u, lanes]), w))
             z = dft3(*z)
+            z = [z[0]] + [turn(z[t], (v_ref[0, t], v_ref[1, t])) for t in range(1, 3)]
             for t in range(3):
                 for p in range(2):
                     h, l = split(z[t][p])
                     high_ref[t, u:u + 16, 128 * p:128 * p + 128] = h
                     low_ref[t, u:u + 16, 128 * p:128 * p + 128] = l
         for t in range(3):
-            z = dot_right((high_ref[t], low_ref[t]), (r_ref[0, t], r_ref[1, t]), NN)
+            z = dot_right((high_ref[t], low_ref[t]), (r_ref[0], r_ref[1]), NN)
             z = turn((z[:, :128], z[:, 128:]), (ph_ref[0, t, g], ph_ref[1, t, g]))
-            w_ref[t] = dot_right(split(jnp.concatenate(z, 1)), (r2_ref[0, t], r2_ref[1, t]), NN)
+            w_ref[t] = dot_right(split(jnp.concatenate(z, 1)), (r_ref[0], r_ref[1]), NN)
         for u in range(0, 128, 16):
-            z = dft3(*[(w_ref[t, u:u + 16, :128], w_ref[t, u:u + 16, 128:]) for t in range(3)])
+            z = [(w_ref[t, u:u + 16, :128], w_ref[t, u:u + 16, 128:]) for t in range(3)]
+            z = dft3(z[0], *[turn(z[t], (v_ref[0, t], v_ref[1, t])) for t in range(1, 3)])
             for t in range(3):
                 q = turn(z[t], (tw_ref[0, t, u:u + 16, :], tw_ref[1, t, u:u + 16, :]))
                 for p in range(2):
@@ -335,15 +357,16 @@
     lax.fori_loop(0, 5, body, 0)
 
 
-def leave_kernel(in_ref, l_ref, lm_ref, m_ref, tw_ref, out_ref, y_ref, high_ref, low_ref):
+def leave_kernel(in_ref, l_ref, lm_ref, tw_ref, v_ref, m_ref, out_ref, y_ref, high_ref, low_ref):
+
     def body(j, _):
         row = 2 * j
         over_senders(in_ref, [(6 * t + row, 6 * t + row + 1) for t in range(5)], KEPT, (l_ref[0], l_ref[1]), y_ref)
         moved = [gather_rows(in_ref, 6 * slot + row + p, KEPT, len(MOVED[slot]), EDGE) for p in range(2) for slot in range(3)]
         y_ref[:, 640:] = dot_left((lm_ref[0], lm_ref[1]), split(jnp.concatenate(moved, 0)), NN)
-        after_senders(tw_ref, y_ref, high_ref, low_ref)
+        after_senders(tw_ref, v_ref, y_ref, high_ref, low_ref)
         for t in range(6):
-            z = dot_left((m_ref[0, t], m_ref[1, t]), (high_ref[t], low_ref[t]), NT)
+            z = dot_left((m_ref[0], m_ref[1]), (high_ref[t], low_ref[t]), NT)
             for p in range(2):
                 rows = pl.ds(pl.multiple_of(48 * p + 16 * j, 16), 16)
                 out_ref[:, rows, 128 * t:128 * t + 128] = z[128 * p:128 * p + 128].reshape(8, 16, 128)
@@ -372,16 +395,18 @@
     return math.prod(a.shape) * jnp.dtype(a.dtype).itemsize
 
 
-def call(kernel, outs, args, scratch=(), spec=None):
+def call(kernel, outs, args, scratch=(), spec=None, limit=None):
     size = sum(nbytes(a) for a in args) + sum(nbytes(o) for o in jax.tree.leaves(outs))
     held = sum(math.prod(r.shape) * jnp.dtype(r.dtype).itemsize for r in scratch)
+    if spec is None:
+        spec = dict(in_specs=[pl.BlockSpec(memory_space=pltpu.SMEM if a.size == 1 else pltpu.VMEM) for a in args])
     return pl.pallas_call(
         kernel,
         out_shape=outs,
         scratch_shapes=list(scratch),
-        compiler_params=pltpu.CompilerParams(vmem_limit_bytes=size + held + 8 * 2**20),
+        compiler_params=pltpu.CompilerParams(vmem_limit_bytes=limit or size + held + 8 * 2**20),
         cost_estimate=pl.CostEstimate(flops=0, bytes_accessed=size, transcendentals=0),
-        **(spec or {}),
+        **spec,
     )(*args)
 
 
@@ -393,75 +418,64 @@
     return lax.all_to_all(x, axis, split_axis=0, concat_axis=0, tiled=True)
 
 
-def make_aperture(pinhole, me, tb):
-    turned = pinhole.T
+def move_groups(turned):
     moves = [[(int(b), EDGE + i) for i, b in enumerate(m)] for m in MOVED]
-    moved = [lax.ppermute(turned[40:48], ("rows", "cols"), pairs) for pairs in moves]
-    place = me - EDGE
-    inside = (place >= 0) & (place < DEV - 2 * EDGE)
-    taken = jnp.where(inside, 2 + (place < len(MOVED[2])).astype(jnp.int32), 0)
-    ky = 48 * me + 8 * jnp.arange(6, dtype=jnp.int32)
-    for slot, m in enumerate(MOVED):
-        source = jnp.asarray(m, jnp.int32)[jnp.clip(place, 0, len(m) - 1)]
-        ky = ky.at[slot].set(jnp.where(taken > slot, 48 * source + 40, ky[slot]))
-    ky = ky[:, None, None] + jnp.arange(8, dtype=jnp.int32)[None, None, :]
-    angle = -chirp_angle(jnp.broadcast_to(ky, (6, 16, 8)).reshape(6, 128))
-    h_y = jnp.stack([jnp.cos(angle), jnp.sin(angle)])
-    whole = pl.BlockSpec(memory_space=pltpu.VMEM)
-    return call(
-        aperture_kernel, shape(2, 3, 5, 128, 128), (taken.reshape(1), turned, *moved, tb["h_x"], h_y),
-        spec=dict(in_specs=[pl.BlockSpec(memory_space=pltpu.SMEM)] + [whole] * 6),
-    )
+    return [lax.ppermute(turned[40:48], ("rows", "cols"), pairs) for pairs in moves]
+
+
+def make_aperture(turned, moved, me, tb):
+    taken = lax.dynamic_slice_in_dim(tb["taken"], me, 1)
+    h_y = lax.dynamic_index_in_dim(tb["h_y"], me, 0, keepdims=False)
+    return call(aperture_kernel, shape(2, 3, 5, 128, 128), (taken, turned, *moved, tb["h_x"], h_y))
 
 
 def per_device(field_real, field_imag, kerr_map, pinhole):
     tb = {k: jnp.asarray(v) for k, v in TABLES.items()}
-    row_at, col_at = lax.axis_index("rows"), lax.axis_index("cols")
     me = lax.axis_index(("rows", "cols"))
+    place = me.reshape(1)
     both = ("rows", "cols")
-    ints = lambda n: jnp.arange(n, dtype=jnp.int32)
-    kerr_rows = exchange(kerr_map.reshape(8, 48, 768), "cols")
-    ax0 = chirp_angle(row_at * 384 + ints(384)).reshape(384, 1)
-    ay0 = chirp_angle(col_at * 768 + ints(768)).reshape(1, 768)
     strip = pl.BlockSpec((128, 768), lambda i: (i, 0))
     enter = dict(
         grid=(3,),
-        in_specs=[strip, strip, strip, pl.BlockSpec((128, 1), lambda i: (i, 0)), pl.BlockSpec((1, 768), lambda i: (0, 0))],
+        in_specs=[pl.BlockSpec(memory_space=pltpu.SMEM), strip, strip, strip],
         out_specs=(pl.BlockSpec((16, 96, 128), lambda i: (0, 0, i)), strip),
     )
     sent, phase_one = call(
-        enter_kernel, (shape(16, 96, 384), shape(384, 768)), (field_real, field_imag, kerr_map, ax0, ay0), spec=enter
-    )
+        enter_kernel, (shape(16, 96, 384), shape(384, 768)), (place, field_real, field_imag, kerr_map), spec=enter, limit=60 * 2**20
+    )
+    sent, turned = lax.optimization_barrier((sent, pinhole.T))
     cols = exchange(sent, "rows")
+    moved = move_groups(turned)
+    cols, kerr_part, turned, *moved = lax.optimization_barrier((cols, kerr_map.reshape(8, 48, 768), turned, *moved))
+    kerr_rows = exchange(kerr_part, "cols")
+    aperture = make_aperture(turned, moved, me, tb)
     sent = call(
-        columns_kernel, shape(DEV * PITCH, 128), (cols, tb["l_plain"], tb["tw_rho_j"]),
+        columns_kernel, shape(DEV * PITCH, 128), (cols, tb["tw_rho_j"], tb["l_plain"]),
         (pltpu.VMEM((3, 16, 2, 8, 128), F32), pltpu.VMEM((384, 256), BF16), pltpu.VMEM((384, 256), BF16)),
     )
+    sent, kerr_rows, aperture = lax.optimization_barrier((sent, kerr_rows, aperture))
     rows = exchange(sent.reshape(DEV, PITCH, 128), both).reshape(DEV * PITCH, 128)
-    ax1 = chirp_angle(me * 48 + 16 * ints(3)[:, None, None] + ints(16)[None, None, :])
-    ax1 = jnp.broadcast_to(ax1, (3, 8, 16)).reshape(384, 1)
     pair6 = (pltpu.VMEM((6, 128, 256), BF16), pltpu.VMEM((6, 128, 256), BF16))
     sent, phase_two = call(
         rows_kernel, (shape(DEV * KEPT, 128), shape(8, 48, 768)),
-        (rows, kerr_rows, ax1, tb["chirp_y"], tb["l_mixed"], tb["m_first"], tb["m_second"], tb["l_plain"],
-         tb["tw_u_a"], tb["tw_a_u"]),
+        (place, rows, kerr_rows, tb["l_mixed"], tb["tw_u_a"], tb["v_6"], tb["m_first"], tb["chirp_y"], tb["m_second"], tb["v_6_rows"], tb["tw_a_u"],
+         tb["l_plain"]),
         (pltpu.VMEM((256, 768), F32), pltpu.VMEM((6, 256, 128), F32)) + pair6,
     )
     far = exchange(sent.reshape(DEV, KEPT, 128), both).reshape(DEV * KEPT, 128)
     far, phase_two = lax.optimization_barrier((far, phase_two))
     phase_back = exchange(phase_two, "cols").reshape(384, 768)
-    aperture = make_aperture(pinhole, me, tb)
     pair3 = (pltpu.VMEM((3, 128, 256), BF16), pltpu.VMEM((3, 128, 256), BF16))
     sent = call(
         far_field_kernel, shape(DEV * KEPT, 128),
-        (far, aperture, tb["l_plain"], tb["r_in"], tb["r_out"], tb["tw_u_rho"]),
+        (far, aperture, tb["l_plain"], tb["tw_u_rho"], tb["v_3"], tb["r_16"]),
         (pltpu.VMEM((256, 384), F32), pltpu.VMEM((3, 128, 256), F32)) + pair3,
     )
     sent, phase_back = lax.optimization_barrier((sent, phase_back))
     near = exchange(sent.reshape(DEV, KEPT, 128), both).reshape(DEV * KEPT, 128)
     b_integral = phase_one + phase_back
     sent = call(
-        leave_kernel, shape(8, 96, 768), (near, tb["l_kept"], tb["l_moved"], tb["m_first"], tb["tw_u_a"]),
+        leave_kernel, shape(8, 96, 768), (near, tb["l_kept"], tb["l_moved"], tb["tw_u_a"], tb["v_6"], tb["m_first"]),
         (pltpu.VMEM((256, 768), F32),) + pair6,
     )
     out = exchange(sent, "cols")

time: 285 us -> 265 us (0.930)
  local copies, waits for them, and re-layouts: 26.5 us -> 12.2 us
  waiting for transfers between devices: 72.1 us -> 63 us
  starting transfers between devices: 24.8 us -> 29.6 us
  Pallas kernels: 36.5 us -> 40.5 us
    all_to_all x4, waiting for transfers between devices: 72 us -> 42.3 us  [exchange(): return lax.all_to_all(x, axis, split_axis=0, concat_axis=0, tiled=True)]
    ppermute x3, waiting for transfers between devices: 0.07 us -> 20.7 us  [move_groups(): lax.ppermute(turned[40:48], ('rows', 'cols'), pairs)]
    unnamed x62 -> x56, local copies, waits for them, and re-layouts: 19.9 us -> 8.37 us
    all_to_all x4, starting transfers between devices: 17.6 us -> 22.4 us  [exchange(): return lax.all_to_all(x, axis, split_axis=0, concat_axis=0, tiled=True)]
    pallas_call x6, Pallas kernels: 36.5 us -> 40.5 us  [call(): pl.pallas_call(kernel, out_shape=outs, scratch_shapes=list(scratch), comp...]
  transfers between devices with their start and end apart: 7 -> 7, of which waited for: 4 -> 5; matrix products, arithmetic and copies ran while one was open for 3% -> 2% of each run, Pallas kernels for 5% -> 5%
where the time goes in v3:
time: 265 us; the launch traced here: 262 us
  blocking collectives  113 us (43%)
  waiting for transfers between devices  63 us (24%)
  Pallas kernels  40.5 us (15%)
  starting transfers between devices  29.6 us (11%)
  local copies, waits for them, and re-layouts  12.2 us (5%)
    all_to_all x3, blocking collectives, exchange(): return lax.all_to_all(x, axis, split_axis=0, concat_axis=0, tiled=True)  113 us
    all_to_all x4, waiting for transfers between devices, exchange(): return lax.all_to_all(x, axis, split_axis=0, concat_axis=0, tiled=True)  42.3 us
    pallas_call x6, Pallas kernels, call(): pl.pallas_call(kernel, out_shape=outs, scratch_shapes=list(scratch), comp...  40.5 us
    all_to_all x4, starting transfers between devices, exchange(): return lax.all_to_all(x, axis, split_axis=0, concat_axis=0, tiled=True)  22.4 us
    ppermute x3, waiting for transfers between devices, move_groups(): lax.ppermute(turned[40:48], ('rows', 'cols'), pairs)  20.7 us
    unnamed x56, local copies, waits for them, and re-layouts  8.37 us
    ppermute x3, starting transfers between devices, move_groups(): lax.ppermute(turned[40:48], ('rows', 'cols'), pairs)  7.18 us
  transfers between devices with their start and end apart: 7, of which 5 were waited for; matrix products, arithmetic and copies ran while one was open for 2% of the time, Pallas kernels for 5%

profile of v3, /device:TPU:1, one launch (start us, length us, event | category | flops | bytes accessed | tf_op | source)
XLA Modules:
  0.0 261.6 jit_solution(222481890098480097)
XLA Ops:
  0.6 5.4 %shard_map.229 = (f32[16,96,384]{2,1,0:T(8,128)}, f32[384,768]{1,0:T(8,128)}) custom-call(s32[1]{0:T(128)} %bitcast.me_ref, f32[384,768]{1,0:T(8,128)} %re_ref.1, f32[384,768]{1,0:T(8,128)} %im_ref.1, f32[384,768]{1,0:T(8,128)} %kerr_ref.1), custom_call_target="tpu_custom_call" | custom-call | bytes 7077892 | tf_op jit(solution)/shard_map/pallas_call | solution.py:403
  6.0 9.3 %all-to-all-start = ((f32[16,96,384]{2,1,0:T(8,128)}), f32[16,96,384]{2,1,0:T(8,128)S(1)}, u32[]{:S(2)}, u32[]{:S(2)}) async-start(f32[16,96,384]{2,1,0:T(8,128)} %get-tuple-element.23), calls=%async_computation | async-start | bytes 4718592 | tf_op jit(solution)/shard_map/all_to_all | solution.py:418
  15.3 0.9 slice.11
  16.3 0.7 collective-permute-start.2
  16.9 0.7 collective-permute-start.1
  17.6 5.8 %collective-permute-start = (s32[8,6144]{1,0:T(8,128)S(1)}, s32[8,6144]{1,0:T(8,128)S(1)}, u32[]{:S(2)}, u32[]{:S(2)}) collective-permute-start(s32[8,6144]{1,0:T(8,128)S(1)} %slice.11), channel_id=1, source_target_pairs={{0,44},{1,45},{2,46},{3,47},{4,48},{5,49},{6,50},{7,51},{8,52},{9,... | collective-permute-start | bytes 589832 | tf_op jit(solution)/shard_map/ppermute | solution.py:423
  23.5 0.0 collective-permute-done.2.m2_ref
  23.5 0.0 collective-permute-done.1.m1_ref
  23.5 20.6 %collective-permute-done.m0_ref = s32[8,6144]{1,0:T(8,128)S(1)} collective-permute-done((s32[8,6144]{1,0:T(8,128)S(1)}, s32[8,6144]{1,0:T(8,128)S(1)}, u32[]{:S(2)}, u32[]{:S(2)}) %collective-permute-start) | collective-permute-done | bytes 196640 | tf_op jit(solution)/shard_map/ppermute | solution.py:423
  44.1 2.6 all-to-all-done.in_ref
  46.7 1.4 copy-done
  48.1 4.5 %all-to-all-start.1 = ((f32[8,48,768]{2,1,0:T(8,128)}), f32[8,48,768]{2,1,0:T(8,128)}, u32[]{:S(2)}, u32[]{:S(2)}) async-start(f32[8,48,768]{2,1,0:T(8,128)} %bitcast.22), calls=%async_computation.1 | async-start | bytes 2359296 | tf_op jit(solution)/shard_map/all_to_all | solution.py:418
  52.6 0.0 copy-done.27
  52.6 0.6 dynamic_slice.7.at_ref
  53.2 0.7 dynamic-slice_bitcast_fusion.hy_ref
  53.9 0.0 copy-done.6
  53.9 0.0 copy-done.22
  53.9 1.7 copy-done.1
  55.6 3.4 %shard_map.230 = f32[5120,128]{1,0:T(8,128)S(1)} custom-call(f32[16,96,384]{2,1,0:T(8,128)S(1)} %copy-done.1, f32[2,48,1,128]{3,2,1,0:T(1,128)S(1)} %copy-done.22, bf16[2,256,256]{2,1,0:T(8,128)(2,1)S(1)} %copy-done.6), custom_call_target="tpu_custom_call" | custom-call | bytes 5292032 | tf_op jit(solution)/shard_map/pallas_call | solution.py:403
  58.9 0.0 copy-done.9
  59.0 0.0 copy-done.14
  59.0 1.0 shard_map.231.ph_ref
  60.0 0.0 copy-start.3
  60.0 1.3 copy-done.3
  61.3 8.6 %all-to-all-done.1.kerr_ref = f32[8,48,768]{2,1,0:T(8,128)} async-done(((f32[8,48,768]{2,1,0:T(8,128)}), f32[8,48,768]{2,1,0:T(8,128)}, u32[]{:S(2)}, u32[]{:S(2)}) %all-to-all-start.1) | async-done | bytes 1179680 | tf_op jit(solution)/shard_map/all_to_all | solution.py:418
  69.9 0.0 copy-start.19
  70.0 0.0 copy-start.20
  70.0 0.0 copy-start.21
  70.0 0.0 copy-start.23
  70.0 0.0 copy-start.24
  70.0 43.4 %all_to_all.35 = f32[128,40,128]{2,1,0:T(8,128)S(1)} all-to-all(f32[128,40,128]{2,1,0:T(8,128)S(1)} %bitcast.14), channel_id=1, replica_groups=mesh['rows'=16,'cols'=8] {'rows','cols'}, dimensions={0} | all-to-all | bytes 5242880 | tf_op jit(solution)/shard_map/all_to_all | solution.py:418
  113.4 0.0 copy-done.5
  113.5 14.1 %shard_map.232 = (f32[4096,128]{1,0:T(8,128)S(1)}, f32[8,48,768]{2,1,0:T(8,128)S(1)}) custom-call(s32[1]{0:T(128)} %bitcast.me_ref, f32[5120,128]{1,0:T(8,128)S(1)} %bitcast.15, f32[8,48,768]{2,1,0:T(8,128)} %all-to-all-done.1.kerr_ref, bf16[2,256,256]{2,1,0:T(8,128)(2,1)S(1)} %copy-done.19, f32[2,6,128,128]{3,2,1,0:T(8,128)S(1)} %copy-done.5, ...), custom_call_target="tpu_custom_call" | custom-call | bytes 9140228 | tf_op jit(solution)/shard_map/pallas_call | solution.py:403
  127.6 0.0 copy-start.10
  127.6 34.8 %all_to_all.36 = f32[128,32,128]{2,1,0:T(8,128)S(1)} all-to-all(f32[128,32,128]{2,1,0:T(8,128)S(1)} %bitcast.19), channel_id=1, replica_groups=mesh['rows'=16,'cols'=8] {'rows','cols'}, dimensions={0} | all-to-all | bytes 4194304 | tf_op jit(solution)/shard_map/all_to_all | solution.py:418
  162.4 4.4 %all-to-all-start.4 = ((f32[8,48,768]{2,1,0:T(8,128)}), f32[8,48,768]{2,1,0:T(8,128)}, u32[]{:S(2)}, u32[]{:S(2)}) async-start(f32[8,48,768]{2,1,0:T(8,128)} %copy-done.10), calls=%async_computation.4 | async-start | bytes 2359296 | tf_op jit(solution)/shard_map/all_to_all | solution.py:418
  166.9 1.5 copy-done.4
  168.4 1.0 copy-done.13
  169.4 9.6 %shard_map.233 = f32[4096,128]{1,0:T(8,128)S(1)} custom-call(f32[4096,128]{1,0:T(8,128)S(1)} %bitcast.17, f32[2,3,5,128,128]{4,3,2,1,0:T(8,128)S(1)} %copy-done.4, bf16[2,256,256]{2,1,0:T(8,128)(2,1)S(1)} %copy-done.8, f32[2,3,128,128]{3,2,1,0:T(8,128)S(1)} %copy-done.13, f32[2,3,1,128]{3,2,1,0:T(1,128)S(1)} %copy-done.25, bf16[2,256,256]{2,1,0:T(8,128)(2,1)S(1)} %copy-done.17), custom_call_target="tpu_custom_call" | custom-call | bytes 7080960 | tf_op jit(solution)/shard_map/pallas_call | solution.py:403
  179.0 1.3 copy-done.2
  180.4 3.7 %all-to-all-done.4 = f32[8,48,768]{2,1,0:T(8,128)} async-done(((f32[8,48,768]{2,1,0:T(8,128)}), f32[8,48,768]{2,1,0:T(8,128)}, u32[]{:S(2)}, u32[]{:S(2)}) %all-to-all-start.4) | async-done | bytes 1179680 | tf_op jit(solution)/shard_map/all_to_all | solution.py:418
  184.1 34.7 %all_to_all.37 = f32[128,32,128]{2,1,0:T(8,128)S(1)} all-to-all(f32[128,32,128]{2,1,0:T(8,128)} %bitcast.18), channel_id=1, replica_groups=mesh['rows'=16,'cols'=8] {'rows','cols'}, dimensions={0} | all-to-all | bytes 4194304 | tf_op jit(solution)/shard_map/all_to_all | solution.py:418
  218.8 7.1 %shard_map.234 = f32[8,96,768]{2,1,0:T(8,128)} custom-call(f32[4096,128]{1,0:T(8,128)S(1)} %bitcast.16, bf16[2,256,256]{2,1,0:T(8,128)(2,1)S(1)} %copy-done.16, bf16[2,256,176]{2,1,0:T(8,128)(2,1)S(1)} %copy-done.15, f32[2,6,128,128]{3,2,1,0:T(8,128)S(1)} %copy-done.5, f32[2,6,1,128]{3,2,1,0:T(1,128)S(1)} %copy-done.24, bf16[2,256,256]{2,1,0:T(8,128)(2,1)S(1)} %copy-done.12), custom_call_target="tpu_custom_call" | custom-call | bytes 5953536 | tf_op jit(solution)/shard_map/pallas_call | solution.py:403
  225.9 4.2 %all-to-all-start.6 = ((f32[8,96,768]{2,1,0:T(8,128)}), f32[8,96,768]{2,1,0:T(8,128)S(1)}, u32[]{:S(2)}, u32[]{:S(2)}) async-start(f32[8,96,768]{2,1,0:T(8,128)} %shard_map.234), calls=%async_computation.6 | async-start | bytes 4718592 | tf_op jit(solution)/shard_map/all_to_all | solution.py:418
  230.1 0.0 copy-done.26
  230.1 2.4 add.13
  232.6 27.4 %all-to-all-done.6 = f32[8,96,768]{2,1,0:T(8,128)S(1)} async-done(((f32[8,96,768]{2,1,0:T(8,128)}), f32[8,96,768]{2,1,0:T(8,128)S(1)}, u32[]{:S(2)}, u32[]{:S(2)}) %all-to-all-start.6) | async-done | bytes 2359328 | tf_op jit(solution)/shard_map/all_to_all | solution.py:418
  260.0 1.6 fusion
  (36 shorter events, 0.1 us)
Async XLA Ops:
  6.0 40.7 %all-to-all-start = ((f32[16,96,384]{2,1,0:T(8,128)}), f32[16,96,384]{2,1,0:T(8,128)S(1)}, u32[]{:S(2)}, u32[]{:S(2)}) async-start(f32[16,96,384]{2,1,0:T(8,128)} %get-tuple-element.23), calls=%async_computation | async-start | bytes 4718592 | tf_op jit(solution)/shard_map/all_to_all | solution.py:418
  16.3 7.2 %collective-permute-start.2 = (s32[8,6144]{1,0:T(8,128)S(1)}, s32[8,6144]{1,0:T(8,128)S(1)}, u32[]{:S(2)}, u32[]{:S(2)}) collective-permute-start(s32[8,6144]{1,0:T(8,128)S(1)} %slice.11), channel_id=1, source_target_pairs={{40,44},{41,45},{42,46},{43,47},{84,48},{85,49},{86,50},{87,51}} | collective-permute-start | bytes 589832 | tf_op jit(solution)/shard_map/ppermute | solution.py:423
  16.9 6.5 %collective-permute-start.1 = (s32[8,6144]{1,0:T(8,128)S(1)}, s32[8,6144]{1,0:T(8,128)S(1)}, u32[]{:S(2)}, u32[]{:S(2)}) collective-permute-start(s32[8,6144]{1,0:T(8,128)S(1)} %slice.11), channel_id=1, source_target_pairs={{88,44},{89,45},{90,46},{91,47},{92,48},{93,49},{94,50},{95,51},{9... | collective-permute-start | bytes 589832 | tf_op jit(solution)/shard_map/ppermute | solution.py:423
  17.6 26.5 %collective-permute-start = (s32[8,6144]{1,0:T(8,128)S(1)}, s32[8,6144]{1,0:T(8,128)S(1)}, u32[]{:S(2)}, u32[]{:S(2)}) collective-permute-start(s32[8,6144]{1,0:T(8,128)S(1)} %slice.11), channel_id=1, source_target_pairs={{0,44},{1,45},{2,46},{3,47},{4,48},{5,49},{6,50},{7,51},{8,52},{9,... | collective-permute-start | bytes 589832 | tf_op jit(solution)/shard_map/ppermute | solution.py:423
  46.7 1.4 copy-start
  46.7 5.9 %copy-start.27 = (s32[128]{0:T(128)S(1)}, s32[128]{0:T(128)}, u32[]{:S(2)}) copy-start(s32[128]{0:T(128)} %constant.71.clone) | copy-start | bytes 1540
  46.7 7.2 %copy-start.6 = (bf16[2,256,256]{2,1,0:T(8,128)(2,1)S(1)}, bf16[2,256,256]{2,1,0:T(8,128)(2,1)}, u32[]{:S(2)}) copy-start(bf16[2,256,256]{2,1,0:T(8,128)(2,1)} %constant.57.clone.l_ref.l2_ref) | copy-start | bytes 786436
  46.7 7.2 %copy-start.22 = (f32[2,48,1,128]{3,2,1,0:T(1,128)S(1)}, f32[2,48,1,128]{3,2,1,0:T(1,128)}, u32[]{:S(2)}) copy-start(f32[2,48,1,128]{3,2,1,0:T(1,128)} %constant.55.clone.tw_ref) | copy-start | bytes 147460
  48.1 21.8 %all-to-all-start.1 = ((f32[8,48,768]{2,1,0:T(8,128)}), f32[8,48,768]{2,1,0:T(8,128)}, u32[]{:S(2)}, u32[]{:S(2)}) async-start(f32[8,48,768]{2,1,0:T(8,128)} %bitcast.22), calls=%async_computation.1 | async-start | bytes 2359296 | tf_op jit(solution)/shard_map/all_to_all | solution.py:418
  53.9 1.7 copy-start.1
  55.6 3.4 %copy-start.9 = (s32[6144,48]{0,1:T(8,128)S(1)}, s32[6144,48]{0,1:T(8,128)}, u32[]{:S(2)}) copy-start(s32[6144,48]{0,1:T(8,128)} %param.25) | copy-start | bytes 3538948
  55.6 3.4 %copy-start.14 = (f32[2,3,128,128]{3,2,1,0:T(8,128)S(1)}, f32[2,3,128,128]{3,2,1,0:T(8,128)}, u32[]{:S(2)}) copy-start(f32[2,3,128,128]{3,2,1,0:T(8,128)} %constant.69.clone.hx_ref) | copy-start | bytes 1179652
  60.0 1.3 copy-start.3
  69.9 43.5 %copy-start.5 = (f32[2,6,128,128]{3,2,1,0:T(8,128)S(1)}, f32[2,6,128,128]{3,2,1,0:T(8,128)}, u32[]{:S(2)}) copy-start(f32[2,6,128,128]{3,2,1,0:T(8,128)} %constant.64.clone.tw_ref) | copy-start | bytes 2359300
  69.9 43.5 %copy-start.7 = (bf16[2,256,256]{2,1,0:T(8,128)(2,1)S(1)}, bf16[2,256,256]{2,1,0:T(8,128)(2,1)}, u32[]{:S(2)}) copy-start(bf16[2,256,256]{2,1,0:T(8,128)(2,1)} %constant.57.clone.l_ref.l2_ref) | copy-start | bytes 786436
  69.9 43.5 %copy-start.11 = (bf16[2,256,256]{2,1,0:T(8,128)(2,1)S(1)}, bf16[2,256,256]{2,1,0:T(8,128)(2,1)}, u32[]{:S(2)}) copy-start(bf16[2,256,256]{2,1,0:T(8,128)(2,1)} %constant.60.clone.m_ref) | copy-start | bytes 786436
  69.9 43.5 %copy-start.18 = (bf16[2,256,256]{2,1,0:T(8,128)(2,1)S(1)}, bf16[2,256,256]{2,1,0:T(8,128)(2,1)}, u32[]{:S(2)}) copy-start(bf16[2,256,256]{2,1,0:T(8,128)(2,1)} %constant.61.clone.m2_ref) | copy-start | bytes 786436
  69.9 43.5 %copy-start.19 = (bf16[2,256,256]{2,1,0:T(8,128)(2,1)S(1)}, bf16[2,256,256]{2,1,0:T(8,128)(2,1)}, u32[]{:S(2)}) copy-start(bf16[2,256,256]{2,1,0:T(8,128)(2,1)} %constant.56.clone.l_ref) | copy-start | bytes 786436
  70.0 43.5 %copy-start.20 = (f32[2,6,16,128]{3,2,1,0:T(8,128)S(1)}, f32[2,6,16,128]{3,2,1,0:T(8,128)}, u32[]{:S(2)}) copy-start(f32[2,6,16,128]{3,2,1,0:T(8,128)} %constant.65.clone.tw2_ref) | copy-start | bytes 294916
  70.0 43.5 %copy-start.21 = (f32[2,6,16,128]{3,2,1,0:T(8,128)S(1)}, f32[2,6,16,128]{3,2,1,0:T(8,128)}, u32[]{:S(2)}) copy-start(f32[2,6,16,128]{3,2,1,0:T(8,128)} %constant.63.clone.v2_ref) | copy-start | bytes 294916
  70.0 43.5 %copy-start.23 = (f32[6,8,128]{2,1,0:T(8,128)S(1)}, f32[6,8,128]{2,1,0:T(8,128)}, u32[]{:S(2)}) copy-start(f32[6,8,128]{2,1,0:T(8,128)} %constant.70.clone.ay_ref) | copy-start | bytes 73732
  70.0 43.5 %copy-start.24 = (f32[2,6,1,128]{3,2,1,0:T(1,128)S(1)}, f32[2,6,1,128]{3,2,1,0:T(1,128)}, u32[]{:S(2)}) copy-start(f32[2,6,1,128]{3,2,1,0:T(1,128)} %constant.62.clone.v_ref) | copy-start | bytes 18436
  127.6 34.8 %copy-start.10 = (f32[8,48,768]{2,1,0:T(8,128)}, f32[8,48,768]{2,1,0:T(8,128)S(1)}, u32[]{:S(2)}) copy-start(f32[8,48,768]{2,1,0:T(8,128)S(1)} %get-tuple-element.37) | copy-start | bytes 3538948
  162.4 4.4 %copy-start.8 = (bf16[2,256,256]{2,1,0:T(8,128)(2,1)S(1)}, bf16[2,256,256]{2,1,0:T(8,128)(2,1)}, u32[]{:S(2)}) copy-start(bf16[2,256,256]{2,1,0:T(8,128)(2,1)} %constant.57.clone.l_ref.l2_ref) | copy-start | bytes 786436
  162.4 4.4 %copy-start.17 = (bf16[2,256,256]{2,1,0:T(8,128)(2,1)S(1)}, bf16[2,256,256]{2,1,0:T(8,128)(2,1)}, u32[]{:S(2)}) copy-start(bf16[2,256,256]{2,1,0:T(8,128)(2,1)} %constant.66.clone.r_ref) | copy-start | bytes 786436
  162.4 4.4 %copy-start.25 = (f32[2,3,1,128]{3,2,1,0:T(1,128)S(1)}, f32[2,3,1,128]{3,2,1,0:T(1,128)}, u32[]{:S(2)}) copy-start(f32[2,3,1,128]{3,2,1,0:T(1,128)} %constant.67.clone.v_ref) | copy-start | bytes 9220
  162.4 21.6 %all-to-all-start.4 = ((f32[8,48,768]{2,1,0:T(8,128)}), f32[8,48,768]{2,1,0:T(8,128)}, u32[]{:S(2)}, u32[]{:S(2)}) async-start(f32[8,48,768]{2,1,0:T(8,128)} %copy-done.10), calls=%async_computation.4 | async-start | bytes 2359296 | tf_op jit(solution)/shard_map/all_to_all | solution.py:418
  166.9 1.5 copy-start.4
  168.4 1.0 copy-start.13
  179.0 1.4 copy-start.2
  184.1 34.7 %copy-start.12 = (bf16[2,256,256]{2,1,0:T(8,128)(2,1)S(1)}, bf16[2,256,256]{2,1,0:T(8,128)(2,1)}, u32[]{:S(2)}) copy-start(bf16[2,256,256]{2,1,0:T(8,128)(2,1)} %constant.60.clone.m_ref) | copy-start | bytes 786436
  184.1 34.7 %copy-start.15 = (bf16[2,256,176]{2,1,0:T(8,128)(2,1)S(1)}, bf16[2,256,176]{2,1,0:T(8,128)(2,1)}, u32[]{:S(2)}) copy-start(bf16[2,256,176]{2,1,0:T(8,128)(2,1)} %constant.59.clone.lm_ref) | copy-start | bytes 540676
  184.1 34.7 %copy-start.16 = (bf16[2,256,256]{2,1,0:T(8,128)(2,1)S(1)}, bf16[2,256,256]{2,1,0:T(8,128)(2,1)}, u32[]{:S(2)}) copy-start(bf16[2,256,256]{2,1,0:T(8,128)(2,1)} %constant.58.clone.l_ref) | copy-start | bytes 786436
  225.9 4.2 %copy-start.26 = (f32[384,768]{1,0:T(8,128)S(1)}, f32[384,768]{1,0:T(8,128)}, u32[]{:S(2)}) copy-start(f32[384,768]{1,0:T(8,128)} %get-tuple-element.39) | copy-start | bytes 3538948
  225.9 34.1 %all-to-all-start.6 = ((f32[8,96,768]{2,1,0:T(8,128)}), f32[8,96,768]{2,1,0:T(8,128)S(1)}, u32[]{:S(2)}, u32[]{:S(2)}) async-start(f32[8,96,768]{2,1,0:T(8,128)} %shard_map.234), calls=%async_computation.6 | async-start | bytes 4718592 | tf_op jit(solution)/shard_map/all_to_all | solution.py:418

commit v4 on v3

--- a/solution.py
+++ b/solution.py
@@ -259,6 +259,10 @@
     out_ref[:, :data.shape[1]] = dot_left(table, split(data), NN)
 
 
+def flat(high_ref, low_ref):
+    return high_ref[...].reshape(768, 256), low_ref[...].reshape(768, 256)
+
+
 def after_senders(tw_ref, v_ref, y_ref, high_ref, low_ref):
     for u in range(0, 128, 16):
         z = []
@@ -276,25 +280,29 @@
 
 
 def rows_kernel(me_ref, in_ref, kerr_ref, l_ref, tw_ref, v_ref, m_ref, ay_ref, m2_ref, v2_ref, tw2_ref, l2_ref,
-                out_ref, phase_ref, y_ref, w_ref, high_ref, low_ref):
+                out_ref, phase_ref, y_ref, w_ref, e_high_ref, e_low_ref, high_ref, low_ref):
 
     def body(j, _):
         over_senders(in_ref, [(12 * j + t, 12 * j + 6 + t) for t in range(6)], PITCH, (l_ref[0], l_ref[1]), y_ref)
         after_senders(tw_ref, v_ref, y_ref, high_ref, low_ref)
         rows = pl.ds(pl.multiple_of(16 * j, 16), 16)
         ax = chirp_angle(48 * me_ref[0] + 16 * j + lax.broadcasted_iota(jnp.int32, (128, 128), 0) % 16)
+        y_ref[...] = dot_left((m_ref[0], m_ref[1]), flat(high_ref, low_ref), NT)
         for t in range(6):
-            z = dot_left((m_ref[0], m_ref[1]), (high_ref[t], low_ref[t]), NT)
-            re, im = z[:128], z[128:]
             lanes = slice(128 * t, 128 * t + 128)
+            re, im = y_ref[:128, lanes], y_ref[128:, lanes]
             phase = kerr_ref[:, rows, lanes].reshape(128, 128) * (re * re + im * im)
             phase_ref[:, rows, lanes] = phase.reshape(8, 16, 128)
             ay = jnp.concatenate([jnp.broadcast_to(ay_ref[t, k:k + 1, :], (16, 128)) for k in range(8)], 0)
             s, c = sin_cos(phase + (ax + ay))
-            both = jnp.concatenate(turn((im, -re), (c, s)), 0)
-            w_ref[t] = dot_left((m2_ref[0], m2_ref[1]), split(both), NN)
+            both = turn((im, -re), (c, s))
+            for p in range(2):
+                h, l = split(both[p])
+                e_high_ref[128 * p:128 * p + 128, lanes] = h
+                e_low_ref[128 * p:128 * p + 128, lanes] = l
+        w_ref[...] = dot_left((m2_ref[0], m2_ref[1]), (e_high_ref[...], e_low_ref[...]), NN)
         for r in range(0, 128, 16):
-            z = [(w_ref[t, r:r + 16, :], w_ref[t, 128 + r:144 + r, :]) for t in range(6)]
+            z = [(w_ref[r:r + 16, 128 * t:128 * t + 128], w_ref[128 + r:144 + r, 128 * t:128 * t + 128]) for t in range(6)]
             z = dft6([z[0]] + [turn(z[t], (v2_ref[0, t], v2_ref[1, t])) for t in range(1, 6)])
             for t in range(6):
                 q = turn(z[t], (tw2_ref[0, t], tw2_ref[1, t]))
@@ -302,19 +310,18 @@
                     h, l = split(q[p])
                     high_ref[t, r:r + 16, 128 * p:128 * p + 128] = h
                     low_ref[t, r:r + 16, 128 * p:128 * p + 128] = l
+        y_ref[...] = dot_left((l2_ref[0], l2_ref[1]), flat(high_ref, low_ref), NT)
         for t in range(6):
-            res = dot_left((l2_ref[0], l2_ref[1]), (high_ref[t], low_ref[t]), NT)
             for p in range(2):
                 row = 2 * j + p
                 if t < 5:
-                    out_ref[pl.ds(6 * t + row, 128, stride=KEPT), :] = res[128 * p:128 * p + 128]
+                    out_ref[pl.ds(6 * t + row, 128, stride=KEPT), :] = y_ref[128 * p:128 * p + 128, 128 * t:128 * t + 128]
                 else:
-                    y_ref[128 * p:128 * p + 128, :128] = res[128 * p:128 * p + 128]
                     for slot in range(2):
                         b = 128 * p + int(MOVED[slot][0])
-                        out_ref[pl.ds(EDGE * KEPT + 6 * slot + row, 40, stride=KEPT), :] = y_ref[b:b + 40, :128]
-                    out_ref[pl.ds(EDGE * KEPT + 12 + row, 4, stride=KEPT), :] = y_ref[128 * p + 40:128 * p + 44, :128]
-                    out_ref[pl.ds((EDGE + 4) * KEPT + 12 + row, 4, stride=KEPT), :] = y_ref[128 * p + 84:128 * p + 88, :128]
+                        out_ref[pl.ds(EDGE * KEPT + 6 * slot + row, 40, stride=KEPT), :] = y_ref[b:b + 40, 640:]
+                    out_ref[pl.ds(EDGE * KEPT + 12 + row, 4, stride=KEPT), :] = y_ref[128 * p + 40:128 * p + 44, 640:]
+                    out_ref[pl.ds((EDGE + 4) * KEPT + 12 + row, 4, stride=KEPT), :] = y_ref[128 * p + 84:128 * p + 88, 640:]
         return 0
 
     lax.fori_loop(0, 3, body, 0)
@@ -365,11 +372,10 @@
         moved = [gather_rows(in_ref, 6 * slot + row + p, KEPT, len(MOVED[slot]), EDGE) for p in range(2) for slot in range(3)]
         y_ref[:, 640:] = dot_left((lm_ref[0], lm_ref[1]), split(jnp.concatenate(moved, 0)), NN)
         after_senders(tw_ref, v_ref, y_ref, high_ref, low_ref)
-        for t in range(6):
-            z = dot_left((m_ref[0], m_ref[1]), (high_ref[t], low_ref[t]), NT)
-            for p in range(2):
-                rows = pl.ds(pl.multiple_of(48 * p + 16 * j, 16), 16)
-                out_ref[:, rows, 128 * t:128 * t + 128] = z[128 * p:128 * p + 128].reshape(8, 16, 128)
+        z = dot_left((m_ref[0], m_ref[1]), flat(high_ref, low_ref), NT)
+        for p in range(2):
+            rows = pl.ds(pl.multiple_of(48 * p + 16 * j, 16), 16)
+            out_ref[:, rows, :] = z[128 * p:128 * p + 128].reshape(8, 16, 768)
         return 0
 
     lax.fori_loop(0, 3, body, 0)
@@ -443,24 +449,22 @@
     sent, phase_one = call(
         enter_kernel, (shape(16, 96, 384), shape(384, 768)), (place, field_real, field_imag, kerr_map), spec=enter, limit=60 * 2**20
     )
-    sent, turned = lax.optimization_barrier((sent, pinhole.T))
+    kerr_rows = exchange(kerr_map.reshape(8, 48, 768), "cols")
+    turned = pinhole.T
+    aperture = make_aperture(turned, move_groups(turned), me, tb)
+    sent, kerr_rows, aperture = lax.optimization_barrier((sent, kerr_rows, aperture))
     cols = exchange(sent, "rows")
-    moved = move_groups(turned)
-    cols, kerr_part, turned, *moved = lax.optimization_barrier((cols, kerr_map.reshape(8, 48, 768), turned, *moved))
-    kerr_rows = exchange(kerr_part, "cols")
-    aperture = make_aperture(turned, moved, me, tb)
     sent = call(
         columns_kernel, shape(DEV * PITCH, 128), (cols, tb["tw_rho_j"], tb["l_plain"]),
         (pltpu.VMEM((3, 16, 2, 8, 128), F32), pltpu.VMEM((384, 256), BF16), pltpu.VMEM((384, 256), BF16)),
     )
-    sent, kerr_rows, aperture = lax.optimization_barrier((sent, kerr_rows, aperture))
     rows = exchange(sent.reshape(DEV, PITCH, 128), both).reshape(DEV * PITCH, 128)
     pair6 = (pltpu.VMEM((6, 128, 256), BF16), pltpu.VMEM((6, 128, 256), BF16))
     sent, phase_two = call(
         rows_kernel, (shape(DEV * KEPT, 128), shape(8, 48, 768)),
         (place, rows, kerr_rows, tb["l_mixed"], tb["tw_u_a"], tb["v_6"], tb["m_first"], tb["chirp_y"], tb["m_second"], tb["v_6_rows"], tb["tw_a_u"],
          tb["l_plain"]),
-        (pltpu.VMEM((256, 768), F32), pltpu.VMEM((6, 256, 128), F32)) + pair6,
+        (pltpu.VMEM((256, 768), F32), pltpu.VMEM((256, 768), F32), pltpu.VMEM((256, 768), BF16), pltpu.VMEM((256, 768), BF16)) + pair6,
     )
     far = exchange(sent.reshape(DEV, KEPT, 128), both).reshape(DEV * KEPT, 128)
     far, phase_two = lax.optimization_barrier((far, phase_two))

time: 265 us -> 255 us (0.962)
  blocking collectives: 113 us -> 149 us
  waiting for transfers between devices: 63 us -> 30.2 us
  starting transfers between devices: 29.6 us -> 23.9 us
  Pallas kernels: 40.5 us -> 36.6 us
  local copies, waits for them, and re-layouts: 12.2 us -> 9.09 us
    all_to_all x3 -> x4, blocking collectives: 113 us -> 149 us  [exchange(): return lax.all_to_all(x, axis, split_axis=0, concat_axis=0, tiled=True)]
    ppermute x3, waiting for transfers between devices: 20.7 us -> 0.01 us  [move_groups(): lax.ppermute(turned[40:48], ('rows', 'cols'), pairs)]
    all_to_all x4 -> x3, waiting for transfers between devices: 42.3 us -> 30.2 us  [exchange(): return lax.all_to_all(x, axis, split_axis=0, concat_axis=0, tiled=True)]
    all_to_all x4 -> x3, starting transfers between devices: 22.4 us -> 15 us  [exchange(): return lax.all_to_all(x, axis, split_axis=0, concat_axis=0, tiled=True)]
    pallas_call x6, Pallas kernels: 40.5 us -> 36.6 us  [call(): pl.pallas_call(kernel, out_shape=outs, scratch_shapes=list(scratch), comp...]
    unnamed x56 -> x46, local copies, waits for them, and re-layouts: 8.37 us -> 6.21 us
  transfers between devices with their start and end apart: 7 -> 6, of which waited for: 5 -> 2; matrix products, arithmetic and copies ran while one was open for 2% -> 1% of each run, Pallas kernels for 5% -> 6%
where the time goes in v4:
time: 255 us; the launch traced here: 252 us
  blocking collectives  149 us (58%)
  Pallas kernels  36.6 us (14%)
  waiting for transfers between devices  30.2 us (12%)
  starting transfers between devices  23.9 us (9%)
  local copies, waits for them, and re-layouts  9.09 us (4%)
    all_to_all x4, blocking collectives, exchange(): return lax.all_to_all(x, axis, split_axis=0, concat_axis=0, tiled=True)  149 us
    pallas_call x6, Pallas kernels, call(): pl.pallas_call(kernel, out_shape=outs, scratch_shapes=list(scratch), comp...  36.6 us
    all_to_all x3, waiting for transfers between devices, exchange(): return lax.all_to_all(x, axis, split_axis=0, concat_axis=0, tiled=True)  30.2 us
    all_to_all x3, starting transfers between devices, exchange(): return lax.all_to_all(x, axis, split_axis=0, concat_axis=0, tiled=True)  15 us
    ppermute x3, starting transfers between devices, move_groups(): lax.ppermute(turned[40:48], ('rows', 'cols'), pairs)  8.91 us
    unnamed x46, local copies, waits for them, and re-layouts  6.21 us
  transfers between devices with their start and end apart: 6, of which 2 were waited for; matrix products, arithmetic and copies ran while one was open for 1% of the time, Pallas kernels for 6%

profile of v4, /device:TPU:1, one launch (start us, length us, event | category | flops | bytes accessed | tf_op | source)
XLA Modules:
  0.0 251.7 jit_solution(5713604440423684804)
XLA Ops:
  0.6 0.0 copy-start.5
  0.6 0.0 copy-start.22
  0.7 6.3 %all-to-all-start = ((f32[8,48,768]{2,1,0:T(8,128)}), f32[8,48,768]{2,1,0:T(8,128)S(1)}, u32[]{:S(2)}, u32[]{:S(2)}) async-start(f32[8,48,768]{2,1,0:T(8,128)} %bitcast.22), calls=%async_computation | async-start | bytes 2359296 | tf_op jit(solution)/shard_map/all_to_all | solution.py:424
  7.0 0.7 collective-permute-start.2
  7.7 0.7 collective-permute-start.1
  8.4 7.6 %collective-permute-start = (s32[8,6144]{1,0:T(8,128)S(1)}, s32[8,6144]{1,0:T(8,128)S(1)}, u32[]{:S(2)}, u32[]{:S(2)}) collective-permute-start(s32[8,6144]{1,0:T(8,128)S(1)} %slice.14), channel_id=1, source_target_pairs={{0,44},{1,45},{2,46},{3,47},{4,48},{5,49},{6,50},{7,51},{8,52},{9,... | collective-permute-start | bytes 589832 | tf_op jit(solution)/shard_map/ppermute | solution.py:429
  16.0 0.0 copy-done.22
  16.0 0.6 dynamic_slice.7.at_ref
  16.6 5.4 %shard_map.229 = (f32[16,96,384]{2,1,0:T(8,128)}, f32[384,768]{1,0:T(8,128)}) custom-call(s32[1]{0:T(128)} %bitcast.me_ref, f32[384,768]{1,0:T(8,128)} %re_ref.1, f32[384,768]{1,0:T(8,128)} %im_ref.1, f32[384,768]{1,0:T(8,128)} %kerr_ref.1), custom_call_target="tpu_custom_call" | custom-call | bytes 7077892 | tf_op jit(solution)/shard_map/pallas_call | solution.py:409
  22.0 0.7 dynamic-slice_bitcast_fusion.hy_ref
  22.7 0.0 collective-permute-done.2.m2_ref
  22.7 0.0 collective-permute-done.1.m1_ref
  22.7 0.0 collective-permute-done.m0_ref
  22.7 1.0 shard_map.230.ph_ref
  23.7 1.3 copy-done.1
  25.0 0.0 all-to-all-done.kerr_ref
  25.0 38.8 %all_to_all.35.in_ref = f32[16,96,384]{2,1,0:T(8,128)S(1)} all-to-all(f32[16,96,384]{2,1,0:T(8,128)} %get-tuple-element.15), channel_id=1, replica_groups=mesh['rows'=16,'cols'=8] {'rows'}, dimensions={0} | all-to-all | bytes 4718592 | tf_op jit(solution)/shard_map/all_to_all | solution.py:424
  63.8 0.0 copy-done.17
  63.8 3.4 %shard_map.231 = f32[5120,128]{1,0:T(8,128)S(1)} custom-call(f32[16,96,384]{2,1,0:T(8,128)S(1)} %all_to_all.35.in_ref, f32[2,48,1,128]{3,2,1,0:T(1,128)S(1)} %copy-done.17, bf16[2,256,256]{2,1,0:T(8,128)(2,1)S(1)} %copy-done.4), custom_call_target="tpu_custom_call" | custom-call | bytes 5292032 | tf_op jit(solution)/shard_map/pallas_call | solution.py:409
  67.2 0.0 copy-start.3
  67.2 0.0 copy-start.7
  67.2 0.0 copy-start.13
  67.2 0.0 copy-start.14
  67.3 0.0 copy-start.15
  67.3 0.0 copy-start.16
  67.3 0.0 copy-start.18
  67.3 0.0 copy-start.19
  67.3 40.1 %all_to_all.36 = f32[128,40,128]{2,1,0:T(8,128)S(1)} all-to-all(f32[128,40,128]{2,1,0:T(8,128)S(1)} %bitcast.15), channel_id=1, replica_groups=mesh['rows'=16,'cols'=8] {'rows','cols'}, dimensions={0} | all-to-all | bytes 5242880 | tf_op jit(solution)/shard_map/all_to_all | solution.py:424
  107.4 0.0 copy-done.13
  107.5 10.7 %shard_map.232 = (f32[4096,128]{1,0:T(8,128)S(1)}, f32[8,48,768]{2,1,0:T(8,128)S(1)}) custom-call(s32[1]{0:T(128)} %bitcast.me_ref, f32[5120,128]{1,0:T(8,128)S(1)} %bitcast.14, f32[8,48,768]{2,1,0:T(8,128)S(1)} %all-to-all-done.kerr_ref, bf16[2,256,256]{2,1,0:T(8,128)(2,1)S(1)} %copy-done.14, f32[2,6,128,128]{3,2,1,0:T(8,128)S(1)} %copy-done.3, ...), custom_call_target="tpu_custom_call" | custom-call | bytes 9140228 | tf_op jit(solution)/shard_map/pallas_call | solution.py:409
  118.1 0.0 copy-start.6
  118.1 34.8 %all_to_all.37 = f32[128,32,128]{2,1,0:T(8,128)S(1)} all-to-all(f32[128,32,128]{2,1,0:T(8,128)S(1)} %bitcast.19), channel_id=1, replica_groups=mesh['rows'=16,'cols'=8] {'rows','cols'}, dimensions={0} | all-to-all | bytes 4194304 | tf_op jit(solution)/shard_map/all_to_all | solution.py:424
  153.0 0.0 copy-done.6
  153.0 4.4 %all-to-all-start.4 = ((f32[8,48,768]{2,1,0:T(8,128)}), f32[8,48,768]{2,1,0:T(8,128)}, u32[]{:S(2)}, u32[]{:S(2)}) async-start(f32[8,48,768]{2,1,0:T(8,128)} %copy-done.6), calls=%async_computation.4 | async-start | bytes 2359296 | tf_op jit(solution)/shard_map/all_to_all | solution.py:424
  157.4 1.5 copy-done.2
  158.9 1.0 copy-done.8
  159.9 0.9 copy-done.12
  160.9 9.6 %shard_map.233 = f32[4096,128]{1,0:T(8,128)S(1)} custom-call(f32[4096,128]{1,0:T(8,128)S(1)} %bitcast.17, f32[2,3,5,128,128]{4,3,2,1,0:T(8,128)S(1)} %copy-done.2, bf16[2,256,256]{2,1,0:T(8,128)(2,1)S(1)} %copy-done.4, f32[2,3,128,128]{3,2,1,0:T(8,128)S(1)} %copy-done.8, f32[2,3,1,128]{3,2,1,0:T(1,128)S(1)} %copy-done.20, bf16[2,256,256]{2,1,0:T(8,128)(2,1)S(1)} %copy-done.12), custom_call_target="tpu_custom_call" | custom-call | bytes 7080960 | tf_op jit(solution)/shard_map/pallas_call | solution.py:409
  170.5 0.0 copy-start
  170.5 1.3 copy-done
  171.9 2.7 %all-to-all-done.4 = f32[8,48,768]{2,1,0:T(8,128)} async-done(((f32[8,48,768]{2,1,0:T(8,128)}), f32[8,48,768]{2,1,0:T(8,128)}, u32[]{:S(2)}, u32[]{:S(2)}) %all-to-all-start.4) | async-done | bytes 1179680 | tf_op jit(solution)/shard_map/all_to_all | solution.py:424
  174.6 34.8 %all_to_all.38 = f32[128,32,128]{2,1,0:T(8,128)S(1)} all-to-all(f32[128,32,128]{2,1,0:T(8,128)} %bitcast.18), channel_id=1, replica_groups=mesh['rows'=16,'cols'=8] {'rows','cols'}, dimensions={0} | all-to-all | bytes 4194304 | tf_op jit(solution)/shard_map/all_to_all | solution.py:424
  209.5 6.6 %shard_map.234 = f32[8,96,768]{2,1,0:T(8,128)} custom-call(f32[4096,128]{1,0:T(8,128)S(1)} %bitcast.16, bf16[2,256,256]{2,1,0:T(8,128)(2,1)S(1)} %copy-done.11, bf16[2,256,176]{2,1,0:T(8,128)(2,1)S(1)} %copy-done.10, f32[2,6,128,128]{3,2,1,0:T(8,128)S(1)} %copy-done.3, f32[2,6,1,128]{3,2,1,0:T(1,128)S(1)} %copy-done.19, bf16[2,256,256]{2,1,0:T(8,128)(2,1)S(1)} %copy-done.7), custom_call_target="tpu_custom_call" | custom-call | bytes 5953536 | tf_op jit(solution)/shard_map/pallas_call | solution.py:409
  216.0 4.2 %all-to-all-start.6 = ((f32[8,96,768]{2,1,0:T(8,128)}), f32[8,96,768]{2,1,0:T(8,128)S(1)}, u32[]{:S(2)}, u32[]{:S(2)}) async-start(f32[8,96,768]{2,1,0:T(8,128)} %shard_map.234), calls=%async_computation.6 | async-start | bytes 4718592 | tf_op jit(solution)/shard_map/all_to_all | solution.py:424
  220.3 0.0 copy-done.21
  220.3 2.4 add.13
  222.7 27.4 %all-to-all-done.6 = f32[8,96,768]{2,1,0:T(8,128)S(1)} async-done(((f32[8,96,768]{2,1,0:T(8,128)}), f32[8,96,768]{2,1,0:T(8,128)S(1)}, u32[]{:S(2)}, u32[]{:S(2)}) %all-to-all-start.6) | async-done | bytes 2359328 | tf_op jit(solution)/shard_map/all_to_all | solution.py:424
  250.1 1.6 fusion
  (25 shorter events, 0.1 us)
Async XLA Ops:
  0.6 6.4 %copy-start.5 = (s32[6144,48]{0,1:T(8,128)S(1)}, s32[6144,48]{0,1:T(8,128)}, u32[]{:S(2)}) copy-start(s32[6144,48]{0,1:T(8,128)} %param.25) | copy-start | bytes 3538948
  0.6 15.3 %copy-start.22 = (s32[128]{0:T(128)S(1)}, s32[128]{0:T(128)}, u32[]{:S(2)}) copy-start(s32[128]{0:T(128)} %constant.71.clone) | copy-start | bytes 1540
  0.7 24.3 %all-to-all-start = ((f32[8,48,768]{2,1,0:T(8,128)}), f32[8,48,768]{2,1,0:T(8,128)S(1)}, u32[]{:S(2)}, u32[]{:S(2)}) async-start(f32[8,48,768]{2,1,0:T(8,128)} %bitcast.22), calls=%async_computation | async-start | bytes 2359296 | tf_op jit(solution)/shard_map/all_to_all | solution.py:424
  7.0 15.6 %collective-permute-start.2 = (s32[8,6144]{1,0:T(8,128)S(1)}, s32[8,6144]{1,0:T(8,128)S(1)}, u32[]{:S(2)}, u32[]{:S(2)}) collective-permute-start(s32[8,6144]{1,0:T(8,128)S(1)} %slice.14), channel_id=1, source_target_pairs={{40,44},{41,45},{42,46},{43,47},{84,48},{85,49},{86,50},{87,51}} | collective-permute-start | bytes 589832 | tf_op jit(solution)/shard_map/ppermute | solution.py:429
  7.7 15.0 %collective-permute-start.1 = (s32[8,6144]{1,0:T(8,128)S(1)}, s32[8,6144]{1,0:T(8,128)S(1)}, u32[]{:S(2)}, u32[]{:S(2)}) collective-permute-start(s32[8,6144]{1,0:T(8,128)S(1)} %slice.14), channel_id=1, source_target_pairs={{88,44},{89,45},{90,46},{91,47},{92,48},{93,49},{94,50},{95,51},{9... | collective-permute-start | bytes 589832 | tf_op jit(solution)/shard_map/ppermute | solution.py:429
  8.4 14.3 %collective-permute-start = (s32[8,6144]{1,0:T(8,128)S(1)}, s32[8,6144]{1,0:T(8,128)S(1)}, u32[]{:S(2)}, u32[]{:S(2)}) collective-permute-start(s32[8,6144]{1,0:T(8,128)S(1)} %slice.14), channel_id=1, source_target_pairs={{0,44},{1,45},{2,46},{3,47},{4,48},{5,49},{6,50},{7,51},{8,52},{9,... | collective-permute-start | bytes 589832 | tf_op jit(solution)/shard_map/ppermute | solution.py:429
  16.6 6.1 %copy-start.9 = (f32[2,3,128,128]{3,2,1,0:T(8,128)S(1)}, f32[2,3,128,128]{3,2,1,0:T(8,128)}, u32[]{:S(2)}) copy-start(f32[2,3,128,128]{3,2,1,0:T(8,128)} %constant.69.clone.hx_ref) | copy-start | bytes 1179652
  23.7 1.3 copy-start.1
  25.0 38.9 %copy-start.4 = (bf16[2,256,256]{2,1,0:T(8,128)(2,1)S(1)}, bf16[2,256,256]{2,1,0:T(8,128)(2,1)}, u32[]{:S(2)}) copy-start(bf16[2,256,256]{2,1,0:T(8,128)(2,1)} %constant.57.clone.l_ref.l2_ref) | copy-start | bytes 786436
  25.0 38.9 %copy-start.17 = (f32[2,48,1,128]{3,2,1,0:T(1,128)S(1)}, f32[2,48,1,128]{3,2,1,0:T(1,128)}, u32[]{:S(2)}) copy-start(f32[2,48,1,128]{3,2,1,0:T(1,128)} %constant.55.clone.tw_ref) | copy-start | bytes 147460
  67.2 40.2 %copy-start.3 = (f32[2,6,128,128]{3,2,1,0:T(8,128)S(1)}, f32[2,6,128,128]{3,2,1,0:T(8,128)}, u32[]{:S(2)}) copy-start(f32[2,6,128,128]{3,2,1,0:T(8,128)} %constant.64.clone.tw_ref) | copy-start | bytes 2359300
  67.2 40.2 %copy-start.7 = (bf16[2,256,256]{2,1,0:T(8,128)(2,1)S(1)}, bf16[2,256,256]{2,1,0:T(8,128)(2,1)}, u32[]{:S(2)}) copy-start(bf16[2,256,256]{2,1,0:T(8,128)(2,1)} %constant.60.clone.m_ref) | copy-start | bytes 786436
  67.2 40.2 %copy-start.13 = (bf16[2,256,256]{2,1,0:T(8,128)(2,1)S(1)}, bf16[2,256,256]{2,1,0:T(8,128)(2,1)}, u32[]{:S(2)}) copy-start(bf16[2,256,256]{2,1,0:T(8,128)(2,1)} %constant.61.clone.m2_ref) | copy-start | bytes 786436
  67.2 40.2 %copy-start.14 = (bf16[2,256,256]{2,1,0:T(8,128)(2,1)S(1)}, bf16[2,256,256]{2,1,0:T(8,128)(2,1)}, u32[]{:S(2)}) copy-start(bf16[2,256,256]{2,1,0:T(8,128)(2,1)} %constant.56.clone.l_ref) | copy-start | bytes 786436
  67.3 40.2 %copy-start.15 = (f32[2,6,16,128]{3,2,1,0:T(8,128)S(1)}, f32[2,6,16,128]{3,2,1,0:T(8,128)}, u32[]{:S(2)}) copy-start(f32[2,6,16,128]{3,2,1,0:T(8,128)} %constant.65.clone.tw2_ref) | copy-start | bytes 294916
  67.3 40.2 %copy-start.16 = (f32[2,6,16,128]{3,2,1,0:T(8,128)S(1)}, f32[2,6,16,128]{3,2,1,0:T(8,128)}, u32[]{:S(2)}) copy-start(f32[2,6,16,128]{3,2,1,0:T(8,128)} %constant.63.clone.v2_ref) | copy-start | bytes 294916
  67.3 40.2 %copy-start.18 = (f32[6,8,128]{2,1,0:T(8,128)S(1)}, f32[6,8,128]{2,1,0:T(8,128)}, u32[]{:S(2)}) copy-start(f32[6,8,128]{2,1,0:T(8,128)} %constant.70.clone.ay_ref) | copy-start | bytes 73732
  67.3 40.2 %copy-start.19 = (f32[2,6,1,128]{3,2,1,0:T(1,128)S(1)}, f32[2,6,1,128]{3,2,1,0:T(1,128)}, u32[]{:S(2)}) copy-start(f32[2,6,1,128]{3,2,1,0:T(1,128)} %constant.62.clone.v_ref) | copy-start | bytes 18436
  118.1 34.9 %copy-start.6 = (f32[8,48,768]{2,1,0:T(8,128)}, f32[8,48,768]{2,1,0:T(8,128)S(1)}, u32[]{:S(2)}) copy-start(f32[8,48,768]{2,1,0:T(8,128)S(1)} %get-tuple-element.21) | copy-start | bytes 3538948
  153.0 4.4 %copy-start.20 = (f32[2,3,1,128]{3,2,1,0:T(1,128)S(1)}, f32[2,3,1,128]{3,2,1,0:T(1,128)}, u32[]{:S(2)}) copy-start(f32[2,3,1,128]{3,2,1,0:T(1,128)} %constant.67.clone.v_ref) | copy-start | bytes 9220
  153.0 21.6 %all-to-all-start.4 = ((f32[8,48,768]{2,1,0:T(8,128)}), f32[8,48,768]{2,1,0:T(8,128)}, u32[]{:S(2)}, u32[]{:S(2)}) async-start(f32[8,48,768]{2,1,0:T(8,128)} %copy-done.6), calls=%async_computation.4 | async-start | bytes 2359296 | tf_op jit(solution)/shard_map/all_to_all | solution.py:424
  157.4 1.5 copy-start.2
  158.9 1.0 copy-start.8
  159.9 0.9 copy-start.12
  170.5 1.4 copy-start
  174.6 34.8 %copy-start.10 = (bf16[2,256,176]{2,1,0:T(8,128)(2,1)S(1)}, bf16[2,256,176]{2,1,0:T(8,128)(2,1)}, u32[]{:S(2)}) copy-start(bf16[2,256,176]{2,1,0:T(8,128)(2,1)} %constant.59.clone.lm_ref) | copy-start | bytes 540676
  174.6 34.8 %copy-start.11 = (bf16[2,256,256]{2,1,0:T(8,128)(2,1)S(1)}, bf16[2,256,256]{2,1,0:T(8,128)(2,1)}, u32[]{:S(2)}) copy-start(bf16[2,256,256]{2,1,0:T(8,128)(2,1)} %constant.58.clone.l_ref) | copy-start | bytes 786436
  216.0 4.2 %copy-start.21 = (f32[384,768]{1,0:T(8,128)S(1)}, f32[384,768]{1,0:T(8,128)}, u32[]{:S(2)}) copy-start(f32[384,768]{1,0:T(8,128)} %get-tuple-element.23) | copy-start | bytes 3538948
  216.0 34.1 %all-to-all-start.6 = ((f32[8,96,768]{2,1,0:T(8,128)}), f32[8,96,768]{2,1,0:T(8,128)S(1)}, u32[]{:S(2)}, u32[]{:S(2)}) async-start(f32[8,96,768]{2,1,0:T(8,128)} %shard_map.234), calls=%async_computation.6 | async-start | bytes 4718592 | tf_op jit(solution)/shard_map/all_to_all | solution.py:424

commit v5 on v4

--- a/solution.py
+++ b/solution.py
@@ -259,6 +259,15 @@
     out_ref[:, :data.shape[1]] = dot_left(table, split(data), NN)
 
 
+def skewed(steps, count):
+    live = []
+    for at in range(count):
+        live.append(steps(at))
+        live = [g for g in live if next(g, None)]
+    while live:
+        live = [g for g in live if next(g, None)]
+
+
 def flat(high_ref, low_ref):
     return high_ref[...].reshape(768, 256), low_ref[...].reshape(768, 256)
 
@@ -280,14 +289,19 @@
 
 
 def rows_kernel(me_ref, in_ref, kerr_ref, l_ref, tw_ref, v_ref, m_ref, ay_ref, m2_ref, v2_ref, tw2_ref, l2_ref,
-                out_ref, phase_ref, y_ref, w_ref, e_high_ref, e_low_ref, high_ref, low_ref):
-
-    def body(j, _):
+                out_ref, phase_ref, y_all, w_all, e_high_all, e_low_all, high_all, low_all):
+
+    def steps(j):
+        y_ref, w_ref, high_ref, low_ref = y_all.at[j], w_all.at[j], high_all.at[j], low_all.at[j]
+        e_high_ref, e_low_ref = e_high_all.at[j], e_low_all.at[j]
         over_senders(in_ref, [(12 * j + t, 12 * j + 6 + t) for t in range(6)], PITCH, (l_ref[0], l_ref[1]), y_ref)
+        yield True
         after_senders(tw_ref, v_ref, y_ref, high_ref, low_ref)
-        rows = pl.ds(pl.multiple_of(16 * j, 16), 16)
+        yield True
+        rows = pl.ds(16 * j, 16)
         ax = chirp_angle(48 * me_ref[0] + 16 * j + lax.broadcasted_iota(jnp.int32, (128, 128), 0) % 16)
         y_ref[...] = dot_left((m_ref[0], m_ref[1]), flat(high_ref, low_ref), NT)
+        yield True
         for t in range(6):
             lanes = slice(128 * t, 128 * t + 128)
             re, im = y_ref[:128, lanes], y_ref[128:, lanes]
@@ -300,7 +314,9 @@
                 h, l = split(both[p])
                 e_high_ref[128 * p:128 * p + 128, lanes] = h
                 e_low_ref[128 * p:128 * p + 128, lanes] = l
+        yield True
         w_ref[...] = dot_left((m2_ref[0], m2_ref[1]), (e_high_ref[...], e_low_ref[...]), NN)
+        yield True
         for r in range(0, 128, 16):
             z = [(w_ref[r:r + 16, 128 * t:128 * t + 128], w_ref[128 + r:144 + r, 128 * t:128 * t + 128]) for t in range(6)]
             z = dft6([z[0]] + [turn(z[t], (v2_ref[0, t], v2_ref[1, t])) for t in range(1, 6)])
@@ -310,7 +326,9 @@
                     h, l = split(q[p])
                     high_ref[t, r:r + 16, 128 * p:128 * p + 128] = h
                     low_ref[t, r:r + 16, 128 * p:128 * p + 128] = l
+        yield True
         y_ref[...] = dot_left((l2_ref[0], l2_ref[1]), flat(high_ref, low_ref), NT)
+        yield True
         for t in range(6):
             for p in range(2):
                 row = 2 * j + p
@@ -322,9 +340,8 @@
                         out_ref[pl.ds(EDGE * KEPT + 6 * slot + row, 40, stride=KEPT), :] = y_ref[b:b + 40, 640:]
                     out_ref[pl.ds(EDGE * KEPT + 12 + row, 4, stride=KEPT), :] = y_ref[128 * p + 40:128 * p + 44, 640:]
                     out_ref[pl.ds((EDGE + 4) * KEPT + 12 + row, 4, stride=KEPT), :] = y_ref[128 * p + 84:128 * p + 88, 640:]
-        return 0
-
-    lax.fori_loop(0, 3, body, 0)
+
+    skewed(steps, 3)
 
 
 def far_field_kernel(in_ref, ph_ref, l_ref, tw_ref, v_ref, r_ref, out_ref, y_ref, w_ref, high_ref, low_ref):
@@ -364,21 +381,25 @@
     lax.fori_loop(0, 5, body, 0)
 
 
-def leave_kernel(in_ref, l_ref, lm_ref, tw_ref, v_ref, m_ref, out_ref, y_ref, high_ref, low_ref):
-
-    def body(j, _):
+def leave_kernel(in_ref, one_ref, two_ref, l_ref, lm_ref, tw_ref, v_ref, m_ref, out_ref, sum_ref, y_all, high_all, low_all):
+    sum_ref[...] = one_ref[...] + two_ref[...]
+
+
+    def steps(j):
+        y_ref, high_ref, low_ref = y_all.at[j], high_all.at[j], low_all.at[j]
         row = 2 * j
         over_senders(in_ref, [(6 * t + row, 6 * t + row + 1) for t in range(5)], KEPT, (l_ref[0], l_ref[1]), y_ref)
         moved = [gather_rows(in_ref, 6 * slot + row + p, KEPT, len(MOVED[slot]), EDGE) for p in range(2) for slot in range(3)]
         y_ref[:, 640:] = dot_left((lm_ref[0], lm_ref[1]), split(jnp.concatenate(moved, 0)), NN)
+        yield True
         after_senders(tw_ref, v_ref, y_ref, high_ref, low_ref)
+        yield True
         z = dot_left((m_ref[0], m_ref[1]), flat(high_ref, low_ref), NT)
         for p in range(2):
-            rows = pl.ds(pl.multiple_of(48 * p + 16 * j, 16), 16)
+            rows = pl.ds(48 * p + 16 * j, 16)
             out_ref[:, rows, :] = z[128 * p:128 * p + 128].reshape(8, 16, 768)
-        return 0
-
-    lax.fori_loop(0, 3, body, 0)
+
+    skewed(steps, 3)
 
 
 def aperture_kernel(at_ref, pin_ref, m0_ref, m1_ref, m2_ref, hx_ref, hy_ref, out_ref):
@@ -459,12 +480,13 @@
         (pltpu.VMEM((3, 16, 2, 8, 128), F32), pltpu.VMEM((384, 256), BF16), pltpu.VMEM((384, 256), BF16)),
     )
     rows = exchange(sent.reshape(DEV, PITCH, 128), both).reshape(DEV * PITCH, 128)
-    pair6 = (pltpu.VMEM((6, 128, 256), BF16), pltpu.VMEM((6, 128, 256), BF16))
+    pair6 = (pltpu.VMEM((3, 6, 128, 256), BF16), pltpu.VMEM((3, 6, 128, 256), BF16))
     sent, phase_two = call(
         rows_kernel, (shape(DEV * KEPT, 128), shape(8, 48, 768)),
         (place, rows, kerr_rows, tb["l_mixed"], tb["tw_u_a"], tb["v_6"], tb["m_first"], tb["chirp_y"], tb["m_second"], tb["v_6_rows"], tb["tw_a_u"],
          tb["l_plain"]),
-        (pltpu.VMEM((256, 768), F32), pltpu.VMEM((256, 768), F32), pltpu.VMEM((256, 768), BF16), pltpu.VMEM((256, 768), BF16)) + pair6,
+        (pltpu.VMEM((3, 256, 768), F32), pltpu.VMEM((3, 256, 768), F32), pltpu.VMEM((3, 256, 768), BF16),
+         pltpu.VMEM((3, 256, 768), BF16)) + pair6,
     )
     far = exchange(sent.reshape(DEV, KEPT, 128), both).reshape(DEV * KEPT, 128)
     far, phase_two = lax.optimization_barrier((far, phase_two))
@@ -477,10 +499,9 @@
     )
     sent, phase_back = lax.optimization_barrier((sent, phase_back))
     near = exchange(sent.reshape(DEV, KEPT, 128), both).reshape(DEV * KEPT, 128)
-    b_integral = phase_one + phase_back
-    sent = call(
-        leave_kernel, shape(8, 96, 768), (near, tb["l_kept"], tb["l_moved"], tb["tw_u_a"], tb["v_6"], tb["m_first"]),
-        (pltpu.VMEM((256, 768), F32),) + pair6,
+    sent, b_integral = call(
+        leave_kernel, (shape(8, 96, 768), shape(384, 768)), (near, phase_one, phase_back, tb["l_kept"], tb["l_moved"], tb["tw_u_a"], tb["v_6"], tb["m_first"]),
+        (pltpu.VMEM((3, 256, 768), F32),) + pair6,
     )
     out = exchange(sent, "cols")
     return (out[:, :48].reshape(384, 768), out[:, 48:].reshape(384, 768), b_integral)

time: 255 us -> 248 us (0.973); the launches traced: 252 us -> 248 us
  blocking collectives: 149 us -> 182 us
  waiting for transfers between devices: 30.2 us -> 2.7 us
  starting transfers between devices: 23.9 us -> 19.5 us
  Pallas kernels: 36.6 us -> 33.4 us
    all_to_all x4 -> x5, blocking collectives: 149 us -> 182 us  [exchange(): return lax.all_to_all(x, axis, split_axis=0, concat_axis=0, tiled=True)]
    all_to_all x3 -> x2, waiting for transfers between devices: 30.2 us -> 2.69 us  [exchange(): return lax.all_to_all(x, axis, split_axis=0, concat_axis=0, tiled=True)]
    all_to_all x3 -> x2, starting transfers between devices: 15 us -> 10.6 us  [exchange(): return lax.all_to_all(x, axis, split_axis=0, concat_axis=0, tiled=True)]
    pallas_call x6, Pallas kernels: 36.6 us -> 33.4 us  [call(): pl.pallas_call(kernel, out_shape=outs, scratch_shapes=list(scratch), comp...]
    unnamed x46 -> x50, local copies, waits for them, and re-layouts: 6.21 us -> 6.21 us
  transfers between devices with their start and end apart: 6 -> 5, of which waited for: 2 -> 1; matrix products, arithmetic and copies ran while one was open for 1% -> 1% of each run, Pallas kernels for 6% -> 7%
where the time goes in v5:
time: 248 us
  blocking collectives  182 us (73%)
  Pallas kernels  33.4 us (13%)
  starting transfers between devices  19.5 us (8%)
  local copies, waits for them, and re-layouts  9.06 us (4%)
  waiting for transfers between devices  2.7 us (1%)
    all_to_all x5, blocking collectives, exchange(): return lax.all_to_all(x, axis, split_axis=0, concat_axis=0, tiled=True)  182 us
    pallas_call x6, Pallas kernels, call(): pl.pallas_call(kernel, out_shape=outs, scratch_shapes=list(scratch), comp...  33.4 us
    all_to_all x2, starting transfers between devices, exchange(): return lax.all_to_all(x, axis, split_axis=0, concat_axis=0, tiled=True)  10.6 us
    ppermute x3, starting transfers between devices, move_groups(): lax.ppermute(turned[40:48], ('rows', 'cols'), pairs)  8.91 us
    unnamed x50, local copies, waits for them, and re-layouts  6.21 us
  transfers between devices with their start and end apart: 5, of which 1 were waited for; matrix products, arithmetic and copies ran while one was open for 1% of the time, Pallas kernels for 7%

profile of v5, /device:TPU:1, one launch (start us, length us, event | category | flops | bytes accessed | tf_op | source)
XLA Modules:
  0.0 247.6 jit_solution(3140457345433574633)
XLA Ops:
  0.6 0.0 copy-start.6
  0.6 0.0 copy-start.24
  0.7 6.3 %all-to-all-start = ((f32[8,48,768]{2,1,0:T(8,128)}), f32[8,48,768]{2,1,0:T(8,128)S(1)}, u32[]{:S(2)}, u32[]{:S(2)}) async-start(f32[8,48,768]{2,1,0:T(8,128)} %bitcast.23), calls=%async_computation | async-start | bytes 2359296 | tf_op jit(solution)/shard_map/all_to_all | solution.py:445
  7.0 0.0 copy-done.6
  7.0 0.7 collective-permute-start.2
  7.7 0.7 collective-permute-start.1
  8.4 7.6 %collective-permute-start = (s32[8,6144]{1,0:T(8,128)S(1)}, s32[8,6144]{1,0:T(8,128)S(1)}, u32[]{:S(2)}, u32[]{:S(2)}) collective-permute-start(s32[8,6144]{1,0:T(8,128)S(1)} %slice.14), channel_id=1, source_target_pairs={{0,44},{1,45},{2,46},{3,47},{4,48},{5,49},{6,50},{7,51},{8,52},{9,... | collective-permute-start | bytes 589832 | tf_op jit(solution)/shard_map/ppermute | solution.py:450
  16.0 0.0 copy-done.24
  16.0 0.6 dynamic_slice.7.at_ref
  16.6 5.4 %shard_map.229 = (f32[16,96,384]{2,1,0:T(8,128)}, f32[384,768]{1,0:T(8,128)}) custom-call(s32[1]{0:T(128)} %bitcast.me_ref, f32[384,768]{1,0:T(8,128)} %re_ref.1, f32[384,768]{1,0:T(8,128)} %im_ref.1, f32[384,768]{1,0:T(8,128)} %kerr_ref.1), custom_call_target="tpu_custom_call" | custom-call | bytes 7077892 | tf_op jit(solution)/shard_map/pallas_call | solution.py:430
  22.0 0.7 dynamic-slice_bitcast_fusion.hy_ref
  22.7 0.0 collective-permute-done.2.m2_ref
  22.7 0.0 collective-permute-done.1.m1_ref
  22.7 0.0 collective-permute-done.m0_ref
  22.7 0.0 copy-done.12
  22.7 1.0 shard_map.230.ph_ref
  23.7 0.0 copy-start.1
  23.7 1.3 copy-done.1
  25.0 0.0 all-to-all-done.kerr_ref
  25.0 38.8 %all_to_all.35.in_ref = f32[16,96,384]{2,1,0:T(8,128)S(1)} all-to-all(f32[16,96,384]{2,1,0:T(8,128)} %get-tuple-element.17), channel_id=1, replica_groups=mesh['rows'=16,'cols'=8] {'rows'}, dimensions={0} | all-to-all | bytes 4718592 | tf_op jit(solution)/shard_map/all_to_all | solution.py:445
  63.8 0.0 copy-done.20
  63.8 3.4 %shard_map.231 = f32[5120,128]{1,0:T(8,128)S(1)} custom-call(f32[16,96,384]{2,1,0:T(8,128)S(1)} %all_to_all.35.in_ref, f32[2,48,1,128]{3,2,1,0:T(1,128)S(1)} %copy-done.20, bf16[2,256,256]{2,1,0:T(8,128)(2,1)S(1)} %copy-done.5), custom_call_target="tpu_custom_call" | custom-call | bytes 5292032 | tf_op jit(solution)/shard_map/pallas_call | solution.py:430
  67.2 0.0 copy-start.3
  67.3 0.0 copy-start.9
  67.3 0.0 copy-start.16
  67.3 0.0 copy-start.17
  67.3 0.0 copy-start.18
  67.3 0.0 copy-start.19
  67.3 0.0 copy-start.21
  67.3 0.0 copy-start.22
  67.3 40.1 %all_to_all.36 = f32[128,40,128]{2,1,0:T(8,128)S(1)} all-to-all(f32[128,40,128]{2,1,0:T(8,128)S(1)} %bitcast.15), channel_id=1, replica_groups=mesh['rows'=16,'cols'=8] {'rows','cols'}, dimensions={0} | all-to-all | bytes 5242880 | tf_op jit(solution)/shard_map/all_to_all | solution.py:445
  107.4 0.0 copy-done.3
  107.4 0.0 copy-done.16
  107.5 8.7 %shard_map.232 = (f32[4096,128]{1,0:T(8,128)S(1)}, f32[8,48,768]{2,1,0:T(8,128)S(1)}) custom-call(s32[1]{0:T(128)} %bitcast.me_ref, f32[5120,128]{1,0:T(8,128)S(1)} %bitcast.14, f32[8,48,768]{2,1,0:T(8,128)S(1)} %all-to-all-done.kerr_ref, bf16[2,256,256]{2,1,0:T(8,128)(2,1)S(1)} %copy-done.17, f32[2,6,128,128]{3,2,1,0:T(8,128)S(1)} %copy-done.3, ...), custom_call_target="tpu_custom_call" | custom-call | bytes 9140228 | tf_op jit(solution)/shard_map/pallas_call | solution.py:430
  116.2 0.0 copy-start.7
  116.2 34.8 %all_to_all.37 = f32[128,32,128]{2,1,0:T(8,128)S(1)} all-to-all(f32[128,32,128]{2,1,0:T(8,128)S(1)} %bitcast.20), channel_id=1, replica_groups=mesh['rows'=16,'cols'=8] {'rows','cols'}, dimensions={0} | all-to-all | bytes 4194304 | tf_op jit(solution)/shard_map/all_to_all | solution.py:445
  151.1 4.2 %all-to-all-start.4 = ((f32[8,48,768]{2,1,0:T(8,128)}), f32[8,48,768]{2,1,0:T(8,128)S(1)}, u32[]{:S(2)}, u32[]{:S(2)}) async-start(f32[8,48,768]{2,1,0:T(8,128)} %copy-done.7), calls=%async_computation.4 | async-start | bytes 2359296 | tf_op jit(solution)/shard_map/all_to_all | solution.py:445
  155.3 1.5 copy-done.2
  156.8 1.0 copy-done.11
  157.8 0.9 copy-done.15
  158.8 9.7 %shard_map.233 = f32[4096,128]{1,0:T(8,128)S(1)} custom-call(f32[4096,128]{1,0:T(8,128)S(1)} %bitcast.17, f32[2,3,5,128,128]{4,3,2,1,0:T(8,128)S(1)} %copy-done.2, bf16[2,256,256]{2,1,0:T(8,128)(2,1)S(1)} %copy-done.5, f32[2,3,128,128]{3,2,1,0:T(8,128)S(1)} %copy-done.11, f32[2,3,1,128]{3,2,1,0:T(1,128)S(1)} %copy-done.23, bf16[2,256,256]{2,1,0:T(8,128)(2,1)S(1)} %copy-done.15), custom_call_target="tpu_custom_call" | custom-call | bytes 7080960 | tf_op jit(solution)/shard_map/pallas_call | solution.py:430
  168.5 1.3 copy-done
  169.8 2.7 %all-to-all-done.4 = f32[8,48,768]{2,1,0:T(8,128)S(1)} async-done(((f32[8,48,768]{2,1,0:T(8,128)}), f32[8,48,768]{2,1,0:T(8,128)S(1)}, u32[]{:S(2)}, u32[]{:S(2)}) %all-to-all-start.4) | async-done | bytes 1179680 | tf_op jit(solution)/shard_map/all_to_all | solution.py:445
  172.5 0.0 copy-start.14
  172.5 34.4 %all_to_all.38 = f32[128,32,128]{2,1,0:T(8,128)S(1)} all-to-all(f32[128,32,128]{2,1,0:T(8,128)} %bitcast.18), channel_id=1, replica_groups=mesh['rows'=16,'cols'=8] {'rows','cols'}, dimensions={0} | all-to-all | bytes 4194304 | tf_op jit(solution)/shard_map/all_to_all | solution.py:445
  207.0 5.2 %shard_map.234 = (f32[8,96,768]{2,1,0:T(8,128)S(1)}, f32[384,768]{1,0:T(8,128)}) custom-call(f32[4096,128]{1,0:T(8,128)S(1)} %bitcast.16, f32[384,768]{1,0:T(8,128)S(1)} %copy-done.8, f32[384,768]{1,0:T(8,128)S(1)} %bitcast.19, bf16[2,256,256]{2,1,0:T(8,128)(2,1)S(1)} %copy-done.14, bf16[2,256,176]{2,1,0:T(8,128)(2,1)S(1)} %copy-done.13, ...), custom_call_target="tpu_custom_call" | custom-call | bytes 9492480 | tf_op jit(solution)/shard_map/pallas_call | solution.py:430
  212.2 33.9 %all_to_all.39 = f32[8,96,768]{2,1,0:T(8,128)S(1)} all-to-all(f32[8,96,768]{2,1,0:T(8,128)S(1)} %get-tuple-element.27), channel_id=1, replica_groups=mesh['rows'=16,'cols'=8] {'cols'}, dimensions={0} | all-to-all | bytes 4718592 | tf_op jit(solution)/shard_map/all_to_all | solution.py:445
  246.1 1.6 fusion
  (27 shorter events, 0.1 us)
Async XLA Ops:
  0.6 6.4 %copy-start.6 = (s32[6144,48]{0,1:T(8,128)S(1)}, s32[6144,48]{0,1:T(8,128)}, u32[]{:S(2)}) copy-start(s32[6144,48]{0,1:T(8,128)} %param.25) | copy-start | bytes 3538948
  0.6 15.3 %copy-start.24 = (s32[128]{0:T(128)S(1)}, s32[128]{0:T(128)}, u32[]{:S(2)}) copy-start(s32[128]{0:T(128)} %constant.71.clone) | copy-start | bytes 1540
  0.7 24.4 %all-to-all-start = ((f32[8,48,768]{2,1,0:T(8,128)}), f32[8,48,768]{2,1,0:T(8,128)S(1)}, u32[]{:S(2)}, u32[]{:S(2)}) async-start(f32[8,48,768]{2,1,0:T(8,128)} %bitcast.23), calls=%async_computation | async-start | bytes 2359296 | tf_op jit(solution)/shard_map/all_to_all | solution.py:445
  7.0 15.7 %collective-permute-start.2 = (s32[8,6144]{1,0:T(8,128)S(1)}, s32[8,6144]{1,0:T(8,128)S(1)}, u32[]{:S(2)}, u32[]{:S(2)}) collective-permute-start(s32[8,6144]{1,0:T(8,128)S(1)} %slice.14), channel_id=1, source_target_pairs={{40,44},{41,45},{42,46},{43,47},{84,48},{85,49},{86,50},{87,51}} | collective-permute-start | bytes 589832 | tf_op jit(solution)/shard_map/ppermute | solution.py:450
  7.7 15.0 %collective-permute-start.1 = (s32[8,6144]{1,0:T(8,128)S(1)}, s32[8,6144]{1,0:T(8,128)S(1)}, u32[]{:S(2)}, u32[]{:S(2)}) collective-permute-start(s32[8,6144]{1,0:T(8,128)S(1)} %slice.14), channel_id=1, source_target_pairs={{88,44},{89,45},{90,46},{91,47},{92,48},{93,49},{94,50},{95,51},{9... | collective-permute-start | bytes 589832 | tf_op jit(solution)/shard_map/ppermute | solution.py:450
  8.4 14.3 %collective-permute-start = (s32[8,6144]{1,0:T(8,128)S(1)}, s32[8,6144]{1,0:T(8,128)S(1)}, u32[]{:S(2)}, u32[]{:S(2)}) collective-permute-start(s32[8,6144]{1,0:T(8,128)S(1)} %slice.14), channel_id=1, source_target_pairs={{0,44},{1,45},{2,46},{3,47},{4,48},{5,49},{6,50},{7,51},{8,52},{9,... | collective-permute-start | bytes 589832 | tf_op jit(solution)/shard_map/ppermute | solution.py:450
  16.6 6.1 %copy-start.12 = (f32[2,3,128,128]{3,2,1,0:T(8,128)S(1)}, f32[2,3,128,128]{3,2,1,0:T(8,128)}, u32[]{:S(2)}) copy-start(f32[2,3,128,128]{3,2,1,0:T(8,128)} %constant.69.clone.hx_ref) | copy-start | bytes 1179652
  23.7 1.3 copy-start.1
  25.0 38.8 %copy-start.5 = (bf16[2,256,256]{2,1,0:T(8,128)(2,1)S(1)}, bf16[2,256,256]{2,1,0:T(8,128)(2,1)}, u32[]{:S(2)}) copy-start(bf16[2,256,256]{2,1,0:T(8,128)(2,1)} %constant.57.clone.l_ref.l2_ref) | copy-start | bytes 786436
  25.0 38.8 %copy-start.20 = (f32[2,48,1,128]{3,2,1,0:T(1,128)S(1)}, f32[2,48,1,128]{3,2,1,0:T(1,128)}, u32[]{:S(2)}) copy-start(f32[2,48,1,128]{3,2,1,0:T(1,128)} %constant.55.clone.tw_ref) | copy-start | bytes 147460
  67.2 40.2 %copy-start.3 = (f32[2,6,128,128]{3,2,1,0:T(8,128)S(1)}, f32[2,6,128,128]{3,2,1,0:T(8,128)}, u32[]{:S(2)}) copy-start(f32[2,6,128,128]{3,2,1,0:T(8,128)} %constant.64.clone.tw_ref) | copy-start | bytes 2359300
  67.3 40.2 %copy-start.9 = (bf16[2,256,256]{2,1,0:T(8,128)(2,1)S(1)}, bf16[2,256,256]{2,1,0:T(8,128)(2,1)}, u32[]{:S(2)}) copy-start(bf16[2,256,256]{2,1,0:T(8,128)(2,1)} %constant.60.clone.m_ref) | copy-start | bytes 786436
  67.3 40.2 %copy-start.16 = (bf16[2,256,256]{2,1,0:T(8,128)(2,1)S(1)}, bf16[2,256,256]{2,1,0:T(8,128)(2,1)}, u32[]{:S(2)}) copy-start(bf16[2,256,256]{2,1,0:T(8,128)(2,1)} %constant.61.clone.m2_ref) | copy-start | bytes 786436
  67.3 40.2 %copy-start.17 = (bf16[2,256,256]{2,1,0:T(8,128)(2,1)S(1)}, bf16[2,256,256]{2,1,0:T(8,128)(2,1)}, u32[]{:S(2)}) copy-start(bf16[2,256,256]{2,1,0:T(8,128)(2,1)} %constant.56.clone.l_ref) | copy-start | bytes 786436
  67.3 40.2 %copy-start.18 = (f32[2,6,16,128]{3,2,1,0:T(8,128)S(1)}, f32[2,6,16,128]{3,2,1,0:T(8,128)}, u32[]{:S(2)}) copy-start(f32[2,6,16,128]{3,2,1,0:T(8,128)} %constant.65.clone.tw2_ref) | copy-start | bytes 294916
  67.3 40.2 %copy-start.19 = (f32[2,6,16,128]{3,2,1,0:T(8,128)S(1)}, f32[2,6,16,128]{3,2,1,0:T(8,128)}, u32[]{:S(2)}) copy-start(f32[2,6,16,128]{3,2,1,0:T(8,128)} %constant.63.clone.v2_ref) | copy-start | bytes 294916
  67.3 40.2 %copy-start.21 = (f32[6,8,128]{2,1,0:T(8,128)S(1)}, f32[6,8,128]{2,1,0:T(8,128)}, u32[]{:S(2)}) copy-start(f32[6,8,128]{2,1,0:T(8,128)} %constant.70.clone.ay_ref) | copy-start | bytes 73732
  67.3 40.2 %copy-start.22 = (f32[2,6,1,128]{3,2,1,0:T(1,128)S(1)}, f32[2,6,1,128]{3,2,1,0:T(1,128)}, u32[]{:S(2)}) copy-start(f32[2,6,1,128]{3,2,1,0:T(1,128)} %constant.62.clone.v_ref) | copy-start | bytes 18436
  116.2 34.9 %copy-start.7 = (f32[8,48,768]{2,1,0:T(8,128)}, f32[8,48,768]{2,1,0:T(8,128)S(1)}, u32[]{:S(2)}) copy-start(f32[8,48,768]{2,1,0:T(8,128)S(1)} %get-tuple-element.23) | copy-start | bytes 3538948
  151.0 4.2 %copy-start.23 = (f32[2,3,1,128]{3,2,1,0:T(1,128)S(1)}, f32[2,3,1,128]{3,2,1,0:T(1,128)}, u32[]{:S(2)}) copy-start(f32[2,3,1,128]{3,2,1,0:T(1,128)} %constant.67.clone.v_ref) | copy-start | bytes 9220
  151.1 21.5 %all-to-all-start.4 = ((f32[8,48,768]{2,1,0:T(8,128)}), f32[8,48,768]{2,1,0:T(8,128)S(1)}, u32[]{:S(2)}, u32[]{:S(2)}) async-start(f32[8,48,768]{2,1,0:T(8,128)} %copy-done.7), calls=%async_computation.4 | async-start | bytes 2359296 | tf_op jit(solution)/shard_map/all_to_all | solution.py:445
  155.3 1.5 copy-start.2
  156.8 1.0 copy-start.11
  157.8 0.9 copy-start.15
  168.5 1.3 copy-start
  172.5 34.4 %copy-start.4 = (f32[2,6,128,128]{3,2,1,0:T(8,128)S(1)}, f32[2,6,128,128]{3,2,1,0:T(8,128)}, u32[]{:S(2)}) copy-start(f32[2,6,128,128]{3,2,1,0:T(8,128)} %constant.64.clone.tw_ref) | copy-start | bytes 2359300
  172.5 34.4 %copy-start.8 = (f32[384,768]{1,0:T(8,128)S(1)}, f32[384,768]{1,0:T(8,128)}, u32[]{:S(2)}) copy-start(f32[384,768]{1,0:T(8,128)} %get-tuple-element.25.one_ref) | copy-start | bytes 3538948
  172.5 34.4 %copy-start.10 = (bf16[2,256,256]{2,1,0:T(8,128)(2,1)S(1)}, bf16[2,256,256]{2,1,0:T(8,128)(2,1)}, u32[]{:S(2)}) copy-start(bf16[2,256,256]{2,1,0:T(8,128)(2,1)} %constant.60.clone.m_ref) | copy-start | bytes 786436
  172.5 34.4 %copy-start.13 = (bf16[2,256,176]{2,1,0:T(8,128)(2,1)S(1)}, bf16[2,256,176]{2,1,0:T(8,128)(2,1)}, u32[]{:S(2)}) copy-start(bf16[2,256,176]{2,1,0:T(8,128)(2,1)} %constant.59.clone.lm_ref) | copy-start | bytes 540676
  172.5 34.4 %copy-start.14 = (bf16[2,256,256]{2,1,0:T(8,128)(2,1)S(1)}, bf16[2,256,256]{2,1,0:T(8,128)(2,1)}, u32[]{:S(2)}) copy-start(bf16[2,256,256]{2,1,0:T(8,128)(2,1)} %constant.58.clone.l_ref) | copy-start | bytes 786436

commit v6 on v5

--- a/solution.py
+++ b/solution.py
@@ -215,39 +215,44 @@
                 out_ref[l // 48, pl.ds(48 * p + l % 48, 16), :] = turned[16 * i:16 * i + 16]
 
 
-def columns_kernel(in_ref, tw_ref, l_ref, out_ref, z_ref, high_ref, low_ref):
-
-    def body(lh, _):
-        low = pl.ds(pl.multiple_of(8 * lh, 8), 8)
-        high = pl.ds(pl.multiple_of(48 + 8 * lh, 8), 8)
-        for j3 in range(3):
-            lanes = slice(128 * j3, 128 * j3 + 128)
-            at = [(n + 5 * j3) % 16 for n in range(16)]
-            z = dft16([(in_ref[r, low, lanes], in_ref[r, high, lanes]) for r in at])
-            for k in range(16):
-                z_ref[j3, k, 0] = z[k][0]
-                z_ref[j3, k, 1] = z[k][1]
-        for k in range(0, 16, 2):
-            found = {}
-            for m in (k, k + 1):
-                z = dft3(*[(z_ref[j3, m, 0], z_ref[j3, m, 1]) for j3 in range(3)])
-                for k3 in range(3):
-                    rho = next(r for r in range(48) if r % 16 == m and r % 3 == k3)
-                    found[rho] = turn(z[k3], (tw_ref[0, rho], tw_ref[1, rho]))
-            for rho in sorted(found):
-                if rho % 2 == 0:
-                    rows = slice(8 * rho, 8 * rho + 16)
-                    for p in range(2):
-                        h, l = split(jnp.concatenate([found[rho][p], found[rho + 1][p]], 0))
-                        high_ref[rows, 128 * p:128 * p + 128] = h
-                        low_ref[rows, 128 * p:128 * p + 128] = l
+def columns_kernel(in_ref, tw_ref, l_ref, out_ref, z_all, high_all, low_all):
+    def steps(at):
+        z_ref, high_ref, low_ref = z_all.at[at], high_all.at[at], low_all.at[at]
+        for half in range(2):
+            low = 8 * (2 * at + half)
+            for j3 in range(3):
+                lanes = slice(128 * j3, 128 * j3 + 128)
+                order = [(n + 5 * j3) % 16 for n in range(16)]
+                z = dft16([(in_ref[r, low:low + 8, lanes], in_ref[r, 48 + low:56 + low, lanes]) for r in order])
+                for k in range(16):
+                    z_ref[half, j3, k, 0] = z[k][0]
+                    z_ref[half, j3, k, 1] = z[k][1]
+        yield True
+        for half in range(2):
+            for k in range(0, 16, 2):
+                found = {}
+                for m in (k, k + 1):
+                    z = dft3(*[(z_ref[half, j3, m, 0], z_ref[half, j3, m, 1]) for j3 in range(3)])
+                    for k3 in range(3):
+                        rho = next(r for r in range(48) if r % 16 == m and r % 3 == k3)
+                        found[rho] = turn(z[k3], (tw_ref[0, rho], tw_ref[1, rho]))
+                for rho in sorted(found):
+                    if rho % 2 == 0:
+                        rows = slice(384 * half + 8 * rho, 384 * half + 8 * rho + 16)
+                        for p in range(2):
+                            h, l = split(jnp.concatenate([found[rho][p], found[rho + 1][p]], 0))
+                            high_ref[rows, 128 * p:128 * p + 128] = h
+                            low_ref[rows, 128 * p:128 * p + 128] = l
+        yield True
         res = dot_left((l_ref[0], l_ref[1]), (high_ref[...], low_ref[...]), NT)
-        for j in range(3):
-            for p in range(2):
-                out_ref[pl.ds(12 * j + 6 * p + lh, 128, stride=PITCH), :] = res[128 * p:128 * p + 128, 128 * j:128 * j + 128]
-        return 0
-
-    lax.fori_loop(0, 6, body, 0)
+        for half in range(2):
+            for j in range(3):
+                lanes = slice(384 * half + 128 * j, 384 * half + 128 * j + 128)
+                for p in range(2):
+                    start = 12 * j + 6 * p + 2 * at + half
+                    out_ref[pl.ds(start, 128, stride=PITCH), :] = res[128 * p:128 * p + 128, lanes]
+
+    skewed(steps, 3)
 
 
 def gather_rows(in_ref, row, pitch, count=128, first=0):
@@ -477,7 +482,7 @@
     cols = exchange(sent, "rows")
     sent = call(
         columns_kernel, shape(DEV * PITCH, 128), (cols, tb["tw_rho_j"], tb["l_plain"]),
-        (pltpu.VMEM((3, 16, 2, 8, 128), F32), pltpu.VMEM((384, 256), BF16), pltpu.VMEM((384, 256), BF16)),
+        (pltpu.VMEM((3, 2, 3, 16, 2, 8, 128), F32), pltpu.VMEM((3, 768, 256), BF16), pltpu.VMEM((3, 768, 256), BF16)),
     )
     rows = exchange(sent.reshape(DEV, PITCH, 128), both).reshape(DEV * PITCH, 128)
     pair6 = (pltpu.VMEM((3, 6, 128, 256), BF16), pltpu.VMEM((3, 6, 128, 256), BF16))

time: 248 us -> 247 us (level)
  no operation moved by 1% of the time
where the time goes in v6:
time: 247 us; the launch traced here: 246 us
  blocking collectives  182 us (74%)
  Pallas kernels  32.3 us (13%)
  starting transfers between devices  19.5 us (8%)
  local copies, waits for them, and re-layouts  9.06 us (4%)
  waiting for transfers between devices  2.69 us (1%)
    all_to_all x5, blocking collectives, exchange(): return lax.all_to_all(x, axis, split_axis=0, concat_axis=0, tiled=True)  182 us
    pallas_call x6, Pallas kernels, call(): pl.pallas_call(kernel, out_shape=outs, scratch_shapes=list(scratch), comp...  32.3 us
    all_to_all x2, starting transfers between devices, exchange(): return lax.all_to_all(x, axis, split_axis=0, concat_axis=0, tiled=True)  10.6 us
    ppermute x3, starting transfers between devices, move_groups(): lax.ppermute(turned[40:48], ('rows', 'cols'), pairs)  8.91 us
    unnamed x50, local copies, waits for them, and re-layouts  6.21 us
  transfers between devices with their start and end apart: 5, of which 1 were waited for; matrix products, arithmetic and copies ran while one was open for 1% of the time, Pallas kernels for 7%

profile of v6, /device:TPU:1, one launch (start us, length us, event | category | flops | bytes accessed | tf_op | source)
XLA Modules:
  0.0 246.5 jit_solution(6344293474473208150)
XLA Ops:
  0.6 0.0 copy-start.6
  0.6 0.0 copy-start.24
  0.7 6.3 %all-to-all-start = ((f32[8,48,768]{2,1,0:T(8,128)}), f32[8,48,768]{2,1,0:T(8,128)S(1)}, u32[]{:S(2)}, u32[]{:S(2)}) async-start(f32[8,48,768]{2,1,0:T(8,128)} %bitcast.23), calls=%async_computation | async-start | bytes 2359296 | tf_op jit(solution)/shard_map/all_to_all | solution.py:450
  7.0 0.0 copy-done.6
  7.0 0.7 collective-permute-start.2
  7.7 0.7 collective-permute-start.1
  8.4 7.6 %collective-permute-start = (s32[8,6144]{1,0:T(8,128)S(1)}, s32[8,6144]{1,0:T(8,128)S(1)}, u32[]{:S(2)}, u32[]{:S(2)}) collective-permute-start(s32[8,6144]{1,0:T(8,128)S(1)} %slice.14), channel_id=1, source_target_pairs={{0,44},{1,45},{2,46},{3,47},{4,48},{5,49},{6,50},{7,51},{8,52},{9,... | collective-permute-start | bytes 589832 | tf_op jit(solution)/shard_map/ppermute | solution.py:455
  16.0 0.0 copy-done.24
  16.0 0.6 dynamic_slice.7.at_ref
  16.6 5.4 %shard_map.229 = (f32[16,96,384]{2,1,0:T(8,128)}, f32[384,768]{1,0:T(8,128)}) custom-call(s32[1]{0:T(128)} %bitcast.me_ref, f32[384,768]{1,0:T(8,128)} %re_ref.1, f32[384,768]{1,0:T(8,128)} %im_ref.1, f32[384,768]{1,0:T(8,128)} %kerr_ref.1), custom_call_target="tpu_custom_call" | custom-call | bytes 7077892 | tf_op jit(solution)/shard_map/pallas_call | solution.py:435
  22.0 0.7 dynamic-slice_bitcast_fusion.hy_ref
  22.7 0.0 collective-permute-done.2.m2_ref
  22.7 0.0 collective-permute-done.1.m1_ref
  22.7 0.0 collective-permute-done.m0_ref
  22.7 0.0 copy-done.12
  22.7 1.0 shard_map.230.ph_ref
  23.7 0.0 copy-start.1
  23.7 1.3 copy-done.1
  25.0 0.0 all-to-all-done.kerr_ref
  25.0 38.8 %all_to_all.35.in_ref = f32[16,96,384]{2,1,0:T(8,128)S(1)} all-to-all(f32[16,96,384]{2,1,0:T(8,128)} %get-tuple-element.17), channel_id=1, replica_groups=mesh['rows'=16,'cols'=8] {'rows'}, dimensions={0} | all-to-all | bytes 4718592 | tf_op jit(solution)/shard_map/all_to_all | solution.py:450
  63.8 0.0 copy-done.20
  63.8 2.2 shard_map.231
  66.1 0.0 copy-start.3
  66.1 0.0 copy-start.9
  66.1 0.0 copy-start.16
  66.1 0.0 copy-start.17
  66.1 0.0 copy-start.18
  66.2 0.0 copy-start.19
  66.2 0.0 copy-start.21
  66.2 0.0 copy-start.22
  66.2 40.1 %all_to_all.36 = f32[128,40,128]{2,1,0:T(8,128)S(1)} all-to-all(f32[128,40,128]{2,1,0:T(8,128)S(1)} %bitcast.15), channel_id=1, replica_groups=mesh['rows'=16,'cols'=8] {'rows','cols'}, dimensions={0} | all-to-all | bytes 5242880 | tf_op jit(solution)/shard_map/all_to_all | solution.py:450
  106.3 0.0 copy-done.9
  106.3 8.7 %shard_map.232 = (f32[4096,128]{1,0:T(8,128)S(1)}, f32[8,48,768]{2,1,0:T(8,128)S(1)}) custom-call(s32[1]{0:T(128)} %bitcast.me_ref, f32[5120,128]{1,0:T(8,128)S(1)} %bitcast.14, f32[8,48,768]{2,1,0:T(8,128)S(1)} %all-to-all-done.kerr_ref, bf16[2,256,256]{2,1,0:T(8,128)(2,1)S(1)} %copy-done.17, f32[2,6,128,128]{3,2,1,0:T(8,128)S(1)} %copy-done.3, ...), custom_call_target="tpu_custom_call" | custom-call | bytes 9140228 | tf_op jit(solution)/shard_map/pallas_call | solution.py:435
  115.0 0.0 copy-start.7
  115.0 34.9 %all_to_all.37 = f32[128,32,128]{2,1,0:T(8,128)S(1)} all-to-all(f32[128,32,128]{2,1,0:T(8,128)S(1)} %bitcast.20), channel_id=1, replica_groups=mesh['rows'=16,'cols'=8] {'rows','cols'}, dimensions={0} | all-to-all | bytes 4194304 | tf_op jit(solution)/shard_map/all_to_all | solution.py:450
  149.9 0.0 copy-done.7
  149.9 4.2 %all-to-all-start.4 = ((f32[8,48,768]{2,1,0:T(8,128)}), f32[8,48,768]{2,1,0:T(8,128)S(1)}, u32[]{:S(2)}, u32[]{:S(2)}) async-start(f32[8,48,768]{2,1,0:T(8,128)} %copy-done.7), calls=%async_computation.4 | async-start | bytes 2359296 | tf_op jit(solution)/shard_map/all_to_all | solution.py:450
  154.1 1.5 copy-done.2
  155.7 1.0 copy-done.11
  156.7 0.9 copy-done.15
  157.6 9.7 %shard_map.233 = f32[4096,128]{1,0:T(8,128)S(1)} custom-call(f32[4096,128]{1,0:T(8,128)S(1)} %bitcast.17, f32[2,3,5,128,128]{4,3,2,1,0:T(8,128)S(1)} %copy-done.2, bf16[2,256,256]{2,1,0:T(8,128)(2,1)S(1)} %copy-done.5, f32[2,3,128,128]{3,2,1,0:T(8,128)S(1)} %copy-done.11, f32[2,3,1,128]{3,2,1,0:T(1,128)S(1)} %copy-done.23, bf16[2,256,256]{2,1,0:T(8,128)(2,1)S(1)} %copy-done.15), custom_call_target="tpu_custom_call" | custom-call | bytes 7080960 | tf_op jit(solution)/shard_map/pallas_call | solution.py:435
  167.3 1.3 copy-done
  168.7 2.7 %all-to-all-done.4 = f32[8,48,768]{2,1,0:T(8,128)S(1)} async-done(((f32[8,48,768]{2,1,0:T(8,128)}), f32[8,48,768]{2,1,0:T(8,128)S(1)}, u32[]{:S(2)}, u32[]{:S(2)}) %all-to-all-start.4) | async-done | bytes 1179680 | tf_op jit(solution)/shard_map/all_to_all | solution.py:450
  171.4 0.0 copy-start.14
  171.4 34.4 %all_to_all.38 = f32[128,32,128]{2,1,0:T(8,128)S(1)} all-to-all(f32[128,32,128]{2,1,0:T(8,128)} %bitcast.18), channel_id=1, replica_groups=mesh['rows'=16,'cols'=8] {'rows','cols'}, dimensions={0} | all-to-all | bytes 4194304 | tf_op jit(solution)/shard_map/all_to_all | solution.py:450
  205.8 5.2 %shard_map.234 = (f32[8,96,768]{2,1,0:T(8,128)S(1)}, f32[384,768]{1,0:T(8,128)}) custom-call(f32[4096,128]{1,0:T(8,128)S(1)} %bitcast.16, f32[384,768]{1,0:T(8,128)S(1)} %copy-done.8, f32[384,768]{1,0:T(8,128)S(1)} %bitcast.19, bf16[2,256,256]{2,1,0:T(8,128)(2,1)S(1)} %copy-done.14, bf16[2,256,176]{2,1,0:T(8,128)(2,1)S(1)} %copy-done.13, ...), custom_call_target="tpu_custom_call" | custom-call | bytes 9492480 | tf_op jit(solution)/shard_map/pallas_call | solution.py:435
  211.0 33.9 %all_to_all.39 = f32[8,96,768]{2,1,0:T(8,128)S(1)} all-to-all(f32[8,96,768]{2,1,0:T(8,128)S(1)} %get-tuple-element.27), channel_id=1, replica_groups=mesh['rows'=16,'cols'=8] {'cols'}, dimensions={0} | all-to-all | bytes 4718592 | tf_op jit(solution)/shard_map/all_to_all | solution.py:450
  244.9 1.6 fusion
  (27 shorter events, 0.1 us)
Async XLA Ops:
  0.6 6.4 %copy-start.6 = (s32[6144,48]{0,1:T(8,128)S(1)}, s32[6144,48]{0,1:T(8,128)}, u32[]{:S(2)}) copy-start(s32[6144,48]{0,1:T(8,128)} %param.25) | copy-start | bytes 3538948
  0.6 15.3 %copy-start.24 = (s32[128]{0:T(128)S(1)}, s32[128]{0:T(128)}, u32[]{:S(2)}) copy-start(s32[128]{0:T(128)} %constant.71.clone) | copy-start | bytes 1540
  0.7 24.4 %all-to-all-start = ((f32[8,48,768]{2,1,0:T(8,128)}), f32[8,48,768]{2,1,0:T(8,128)S(1)}, u32[]{:S(2)}, u32[]{:S(2)}) async-start(f32[8,48,768]{2,1,0:T(8,128)} %bitcast.23), calls=%async_computation | async-start | bytes 2359296 | tf_op jit(solution)/shard_map/all_to_all | solution.py:450
  7.0 15.7 %collective-permute-start.2 = (s32[8,6144]{1,0:T(8,128)S(1)}, s32[8,6144]{1,0:T(8,128)S(1)}, u32[]{:S(2)}, u32[]{:S(2)}) collective-permute-start(s32[8,6144]{1,0:T(8,128)S(1)} %slice.14), channel_id=1, source_target_pairs={{40,44},{41,45},{42,46},{43,47},{84,48},{85,49},{86,50},{87,51}} | collective-permute-start | bytes 589832 | tf_op jit(solution)/shard_map/ppermute | solution.py:455
  7.7 15.0 %collective-permute-start.1 = (s32[8,6144]{1,0:T(8,128)S(1)}, s32[8,6144]{1,0:T(8,128)S(1)}, u32[]{:S(2)}, u32[]{:S(2)}) collective-permute-start(s32[8,6144]{1,0:T(8,128)S(1)} %slice.14), channel_id=1, source_target_pairs={{88,44},{89,45},{90,46},{91,47},{92,48},{93,49},{94,50},{95,51},{9... | collective-permute-start | bytes 589832 | tf_op jit(solution)/shard_map/ppermute | solution.py:455
  8.4 14.3 %collective-permute-start = (s32[8,6144]{1,0:T(8,128)S(1)}, s32[8,6144]{1,0:T(8,128)S(1)}, u32[]{:S(2)}, u32[]{:S(2)}) collective-permute-start(s32[8,6144]{1,0:T(8,128)S(1)} %slice.14), channel_id=1, source_target_pairs={{0,44},{1,45},{2,46},{3,47},{4,48},{5,49},{6,50},{7,51},{8,52},{9,... | collective-permute-start | bytes 589832 | tf_op jit(solution)/shard_map/ppermute | solution.py:455
  16.6 6.1 %copy-start.12 = (f32[2,3,128,128]{3,2,1,0:T(8,128)S(1)}, f32[2,3,128,128]{3,2,1,0:T(8,128)}, u32[]{:S(2)}) copy-start(f32[2,3,128,128]{3,2,1,0:T(8,128)} %constant.69.clone.hx_ref) | copy-start | bytes 1179652
  23.7 1.3 copy-start.1
  25.0 38.8 %copy-start.5 = (bf16[2,256,256]{2,1,0:T(8,128)(2,1)S(1)}, bf16[2,256,256]{2,1,0:T(8,128)(2,1)}, u32[]{:S(2)}) copy-start(bf16[2,256,256]{2,1,0:T(8,128)(2,1)} %constant.57.clone.l_ref.l2_ref) | copy-start | bytes 786436
  25.0 38.8 %copy-start.20 = (f32[2,48,1,128]{3,2,1,0:T(1,128)S(1)}, f32[2,48,1,128]{3,2,1,0:T(1,128)}, u32[]{:S(2)}) copy-start(f32[2,48,1,128]{3,2,1,0:T(1,128)} %constant.55.clone.tw_ref) | copy-start | bytes 147460
  66.1 40.2 %copy-start.3 = (f32[2,6,128,128]{3,2,1,0:T(8,128)S(1)}, f32[2,6,128,128]{3,2,1,0:T(8,128)}, u32[]{:S(2)}) copy-start(f32[2,6,128,128]{3,2,1,0:T(8,128)} %constant.64.clone.tw_ref) | copy-start | bytes 2359300
  66.1 40.2 %copy-start.9 = (bf16[2,256,256]{2,1,0:T(8,128)(2,1)S(1)}, bf16[2,256,256]{2,1,0:T(8,128)(2,1)}, u32[]{:S(2)}) copy-start(bf16[2,256,256]{2,1,0:T(8,128)(2,1)} %constant.60.clone.m_ref) | copy-start | bytes 786436
  66.1 40.2 %copy-start.16 = (bf16[2,256,256]{2,1,0:T(8,128)(2,1)S(1)}, bf16[2,256,256]{2,1,0:T(8,128)(2,1)}, u32[]{:S(2)}) copy-start(bf16[2,256,256]{2,1,0:T(8,128)(2,1)} %constant.61.clone.m2_ref) | copy-start | bytes 786436
  66.1 40.2 %copy-start.17 = (bf16[2,256,256]{2,1,0:T(8,128)(2,1)S(1)}, bf16[2,256,256]{2,1,0:T(8,128)(2,1)}, u32[]{:S(2)}) copy-start(bf16[2,256,256]{2,1,0:T(8,128)(2,1)} %constant.56.clone.l_ref) | copy-start | bytes 786436
  66.1 40.2 %copy-start.18 = (f32[2,6,16,128]{3,2,1,0:T(8,128)S(1)}, f32[2,6,16,128]{3,2,1,0:T(8,128)}, u32[]{:S(2)}) copy-start(f32[2,6,16,128]{3,2,1,0:T(8,128)} %constant.65.clone.tw2_ref) | copy-start | bytes 294916
  66.2 40.2 %copy-start.19 = (f32[2,6,16,128]{3,2,1,0:T(8,128)S(1)}, f32[2,6,16,128]{3,2,1,0:T(8,128)}, u32[]{:S(2)}) copy-start(f32[2,6,16,128]{3,2,1,0:T(8,128)} %constant.63.clone.v2_ref) | copy-start | bytes 294916
  66.2 40.1 %copy-start.21 = (f32[6,8,128]{2,1,0:T(8,128)S(1)}, f32[6,8,128]{2,1,0:T(8,128)}, u32[]{:S(2)}) copy-start(f32[6,8,128]{2,1,0:T(8,128)} %constant.70.clone.ay_ref) | copy-start | bytes 73732
  66.2 40.1 %copy-start.22 = (f32[2,6,1,128]{3,2,1,0:T(1,128)S(1)}, f32[2,6,1,128]{3,2,1,0:T(1,128)}, u32[]{:S(2)}) copy-start(f32[2,6,1,128]{3,2,1,0:T(1,128)} %constant.62.clone.v_ref) | copy-start | bytes 18436
  115.0 34.9 %copy-start.7 = (f32[8,48,768]{2,1,0:T(8,128)}, f32[8,48,768]{2,1,0:T(8,128)S(1)}, u32[]{:S(2)}) copy-start(f32[8,48,768]{2,1,0:T(8,128)S(1)} %get-tuple-element.23) | copy-start | bytes 3538948
  149.9 4.2 %copy-start.23 = (f32[2,3,1,128]{3,2,1,0:T(1,128)S(1)}, f32[2,3,1,128]{3,2,1,0:T(1,128)}, u32[]{:S(2)}) copy-start(f32[2,3,1,128]{3,2,1,0:T(1,128)} %constant.67.clone.v_ref) | copy-start | bytes 9220
  149.9 21.5 %all-to-all-start.4 = ((f32[8,48,768]{2,1,0:T(8,128)}), f32[8,48,768]{2,1,0:T(8,128)S(1)}, u32[]{:S(2)}, u32[]{:S(2)}) async-start(f32[8,48,768]{2,1,0:T(8,128)} %copy-done.7), calls=%async_computation.4 | async-start | bytes 2359296 | tf_op jit(solution)/shard_map/all_to_all | solution.py:450
  154.1 1.5 copy-start.2
  155.7 1.0 copy-start.11
  156.7 0.9 copy-start.15
  167.3 1.3 copy-start
  171.4 34.4 %copy-start.4 = (f32[2,6,128,128]{3,2,1,0:T(8,128)S(1)}, f32[2,6,128,128]{3,2,1,0:T(8,128)}, u32[]{:S(2)}) copy-start(f32[2,6,128,128]{3,2,1,0:T(8,128)} %constant.64.clone.tw_ref) | copy-start | bytes 2359300
  171.4 34.4 %copy-start.8 = (f32[384,768]{1,0:T(8,128)S(1)}, f32[384,768]{1,0:T(8,128)}, u32[]{:S(2)}) copy-start(f32[384,768]{1,0:T(8,128)} %get-tuple-element.25.one_ref) | copy-start | bytes 3538948
  171.4 34.4 %copy-start.10 = (bf16[2,256,256]{2,1,0:T(8,128)(2,1)S(1)}, bf16[2,256,256]{2,1,0:T(8,128)(2,1)}, u32[]{:S(2)}) copy-start(bf16[2,256,256]{2,1,0:T(8,128)(2,1)} %constant.60.clone.m_ref) | copy-start | bytes 786436
  171.4 34.4 %copy-start.13 = (bf16[2,256,176]{2,1,0:T(8,128)(2,1)S(1)}, bf16[2,256,176]{2,1,0:T(8,128)(2,1)}, u32[]{:S(2)}) copy-start(bf16[2,256,176]{2,1,0:T(8,128)(2,1)} %constant.59.clone.lm_ref) | copy-start | bytes 540676
  171.4 34.4 %copy-start.14 = (bf16[2,256,256]{2,1,0:T(8,128)(2,1)S(1)}, bf16[2,256,256]{2,1,0:T(8,128)(2,1)}, u32[]{:S(2)}) copy-start(bf16[2,256,256]{2,1,0:T(8,128)(2,1)} %constant.58.clone.l_ref) | copy-start | bytes 786436

commit v7 on v6

--- a/solution.py
+++ b/solution.py
@@ -74,7 +74,7 @@
     kx = r128[None, :, None] + 128 * (np.arange(3)[:, None, None] + 3 * lane_q[None, None, :])
     t["h_x"] = planes(root(2 * N, kx * kx))
     y = r128[None, None, :] + 128 * (six[:, None, None] + 6 * np.arange(8)[None, :, None])
-    t["chirp_y"] = (math.pi / N * ((y * y + N) % (2 * N) - N)).astype(np.float32)
+    t["chirp_y"] = (2.0 / N * ((y * y + N) % (2 * N) - N)).astype(np.float32)
     taken = np.zeros(DEV, np.int32)
     ky = 48 * np.arange(DEV)[:, None] + 8 * np.arange(6)[None, :]
     for slot, m in enumerate(MOVED):
@@ -93,14 +93,12 @@
 def chirp_angle(index):
     square = index * index
     turns = (square.astype(F32) * (0.5 / N)).astype(jnp.int32)
-    return (math.pi / N) * (square - 2 * N * turns).astype(F32)
+    return (2.0 / N) * (square - 2 * N * turns).astype(F32)
 
 
 def sin_cos(angle):
-    turns = jnp.floor(angle * (2.0 / math.pi) + 0.5)
-    r = angle - turns * 1.5703125
-    r = r - turns * 4.837512969970703e-4
-    r = r - turns * 7.549789948768648e-8
+    turns = jnp.floor(angle + 0.5)
+    r = (angle - turns) * (math.pi / 2)
     quarter = turns.astype(jnp.int32)
     r2 = r * r
     sine = r + r * r2 * (-1.6666654611e-1 + r2 * (8.3321608736e-3 + r2 * -1.9515295891e-4))
@@ -206,7 +204,7 @@
         re, im = re_ref[:, cols], im_ref[:, cols]
         phase = kerr_ref[:, cols] * (re * re + im * im)
         phase_ref[:, cols] = phase
-        s, c = sin_cos(phase + (ax + ay))
+        s, c = sin_cos(phase * (2.0 / math.pi) + (ax + ay))
         both = turn((re, im), (c, s))
         for p in range(2):
             turned = both[p].T
@@ -313,7 +311,7 @@
             phase = kerr_ref[:, rows, lanes].reshape(128, 128) * (re * re + im * im)
             phase_ref[:, rows, lanes] = phase.reshape(8, 16, 128)
             ay = jnp.concatenate([jnp.broadcast_to(ay_ref[t, k:k + 1, :], (16, 128)) for k in range(8)], 0)
-            s, c = sin_cos(phase + (ax + ay))
+            s, c = sin_cos(phase * (2.0 / math.pi) + (ax + ay))
             both = turn((im, -re), (c, s))
             for p in range(2):
                 h, l = split(both[p])

time: 247 us -> 247 us (level)
  no operation moved by 1% of the time
where the time goes in v7:
time: 247 us; the launch traced here: 246 us
  blocking collectives  182 us (74%)
  Pallas kernels  32.1 us (13%)
  starting transfers between devices  19.5 us (8%)
  local copies, waits for them, and re-layouts  9.06 us (4%)
  waiting for transfers between devices  2.68 us (1%)
    all_to_all x5, blocking collectives, exchange(): return lax.all_to_all(x, axis, split_axis=0, concat_axis=0, tiled=True)  182 us
    pallas_call x6, Pallas kernels, call(): pl.pallas_call(kernel, out_shape=outs, scratch_shapes=list(scratch), comp...  32.1 us
    all_to_all x2, starting transfers between devices, exchange(): return lax.all_to_all(x, axis, split_axis=0, concat_axis=0, tiled=True)  10.6 us
    ppermute x3, starting transfers between devices, move_groups(): lax.ppermute(turned[40:48], ('rows', 'cols'), pairs)  8.91 us
    unnamed x50, local copies, waits for them, and re-layouts  6.21 us
  transfers between devices with their start and end apart: 5, of which 1 were waited for; matrix products, arithmetic and copies ran while one was open for 1% of the time, Pallas kernels for 7%

profile of v7, /device:TPU:1, one launch (start us, length us, event | category | flops | bytes accessed | tf_op | source)
XLA Modules:
  0.0 246.3 jit_solution(7995035312520283475)
XLA Ops:
  0.6 0.0 copy-start.6
  0.6 0.0 copy-start.24
  0.7 6.3 %all-to-all-start = ((f32[8,48,768]{2,1,0:T(8,128)}), f32[8,48,768]{2,1,0:T(8,128)S(1)}, u32[]{:S(2)}, u32[]{:S(2)}) async-start(f32[8,48,768]{2,1,0:T(8,128)} %bitcast.23), calls=%async_computation | async-start | bytes 2359296 | tf_op jit(solution)/shard_map/all_to_all | solution.py:448
  7.0 0.0 copy-done.6
  7.0 0.7 collective-permute-start.2
  7.7 0.7 collective-permute-start.1
  8.4 7.6 %collective-permute-start = (s32[8,6144]{1,0:T(8,128)S(1)}, s32[8,6144]{1,0:T(8,128)S(1)}, u32[]{:S(2)}, u32[]{:S(2)}) collective-permute-start(s32[8,6144]{1,0:T(8,128)S(1)} %slice.14), channel_id=1, source_target_pairs={{0,44},{1,45},{2,46},{3,47},{4,48},{5,49},{6,50},{7,51},{8,52},{9,... | collective-permute-start | bytes 589832 | tf_op jit(solution)/shard_map/ppermute | solution.py:453
  16.0 0.0 copy-done.24
  16.0 0.6 dynamic_slice.7.at_ref
  16.6 5.4 %shard_map.229 = (f32[16,96,384]{2,1,0:T(8,128)}, f32[384,768]{1,0:T(8,128)}) custom-call(s32[1]{0:T(128)} %bitcast.me_ref, f32[384,768]{1,0:T(8,128)} %re_ref.1, f32[384,768]{1,0:T(8,128)} %im_ref.1, f32[384,768]{1,0:T(8,128)} %kerr_ref.1), custom_call_target="tpu_custom_call" | custom-call | bytes 7077892 | tf_op jit(solution)/shard_map/pallas_call | solution.py:433
  22.0 0.7 dynamic-slice_bitcast_fusion.hy_ref
  22.7 0.0 collective-permute-done.2.m2_ref
  22.7 0.0 collective-permute-done.1.m1_ref
  22.7 0.0 collective-permute-done.m0_ref
  22.7 0.0 copy-done.12
  22.7 1.0 shard_map.230.ph_ref
  23.7 0.0 copy-start.1
  23.7 1.3 copy-done.1
  25.0 0.0 all-to-all-done.kerr_ref
  25.0 38.9 %all_to_all.35.in_ref = f32[16,96,384]{2,1,0:T(8,128)S(1)} all-to-all(f32[16,96,384]{2,1,0:T(8,128)} %get-tuple-element.17), channel_id=1, replica_groups=mesh['rows'=16,'cols'=8] {'rows'}, dimensions={0} | all-to-all | bytes 4718592 | tf_op jit(solution)/shard_map/all_to_all | solution.py:448
  63.8 0.0 copy-done.20
  63.8 2.2 shard_map.231
  66.1 0.0 copy-start.3
  66.1 0.0 copy-start.9
  66.1 0.0 copy-start.16
  66.1 0.0 copy-start.17
  66.1 0.0 copy-start.18
  66.2 0.0 copy-start.19
  66.2 0.0 copy-start.21
  66.2 0.0 copy-start.22
  66.2 40.1 %all_to_all.36 = f32[128,40,128]{2,1,0:T(8,128)S(1)} all-to-all(f32[128,40,128]{2,1,0:T(8,128)S(1)} %bitcast.15), channel_id=1, replica_groups=mesh['rows'=16,'cols'=8] {'rows','cols'}, dimensions={0} | all-to-all | bytes 5242880 | tf_op jit(solution)/shard_map/all_to_all | solution.py:448
  106.3 0.0 copy-done.9
  106.3 8.5 %shard_map.232 = (f32[4096,128]{1,0:T(8,128)S(1)}, f32[8,48,768]{2,1,0:T(8,128)S(1)}) custom-call(s32[1]{0:T(128)} %bitcast.me_ref, f32[5120,128]{1,0:T(8,128)S(1)} %bitcast.14, f32[8,48,768]{2,1,0:T(8,128)S(1)} %all-to-all-done.kerr_ref, bf16[2,256,256]{2,1,0:T(8,128)(2,1)S(1)} %copy-done.17, f32[2,6,128,128]{3,2,1,0:T(8,128)S(1)} %copy-done.3, ...), custom_call_target="tpu_custom_call" | custom-call | bytes 9140228 | tf_op jit(solution)/shard_map/pallas_call | solution.py:433
  114.9 0.0 copy-start.7
  114.9 34.9 %all_to_all.37 = f32[128,32,128]{2,1,0:T(8,128)S(1)} all-to-all(f32[128,32,128]{2,1,0:T(8,128)S(1)} %bitcast.20), channel_id=1, replica_groups=mesh['rows'=16,'cols'=8] {'rows','cols'}, dimensions={0} | all-to-all | bytes 4194304 | tf_op jit(solution)/shard_map/all_to_all | solution.py:448
  149.8 0.0 copy-done.7
  149.8 4.2 %all-to-all-start.4 = ((f32[8,48,768]{2,1,0:T(8,128)}), f32[8,48,768]{2,1,0:T(8,128)S(1)}, u32[]{:S(2)}, u32[]{:S(2)}) async-start(f32[8,48,768]{2,1,0:T(8,128)} %copy-done.7), calls=%async_computation.4 | async-start | bytes 2359296 | tf_op jit(solution)/shard_map/all_to_all | solution.py:448
  154.0 1.5 copy-done.2
  155.6 1.0 copy-done.11
  156.6 0.9 copy-done.15
  157.5 9.7 %shard_map.233 = f32[4096,128]{1,0:T(8,128)S(1)} custom-call(f32[4096,128]{1,0:T(8,128)S(1)} %bitcast.17, f32[2,3,5,128,128]{4,3,2,1,0:T(8,128)S(1)} %copy-done.2, bf16[2,256,256]{2,1,0:T(8,128)(2,1)S(1)} %copy-done.5, f32[2,3,128,128]{3,2,1,0:T(8,128)S(1)} %copy-done.11, f32[2,3,1,128]{3,2,1,0:T(1,128)S(1)} %copy-done.23, bf16[2,256,256]{2,1,0:T(8,128)(2,1)S(1)} %copy-done.15), custom_call_target="tpu_custom_call" | custom-call | bytes 7080960 | tf_op jit(solution)/shard_map/pallas_call | solution.py:433
  167.2 1.3 copy-done
  168.6 2.7 %all-to-all-done.4 = f32[8,48,768]{2,1,0:T(8,128)S(1)} async-done(((f32[8,48,768]{2,1,0:T(8,128)}), f32[8,48,768]{2,1,0:T(8,128)S(1)}, u32[]{:S(2)}, u32[]{:S(2)}) %all-to-all-start.4) | async-done | bytes 1179680 | tf_op jit(solution)/shard_map/all_to_all | solution.py:448
  171.2 0.0 copy-start.14
  171.3 34.4 %all_to_all.38 = f32[128,32,128]{2,1,0:T(8,128)S(1)} all-to-all(f32[128,32,128]{2,1,0:T(8,128)} %bitcast.18), channel_id=1, replica_groups=mesh['rows'=16,'cols'=8] {'rows','cols'}, dimensions={0} | all-to-all | bytes 4194304 | tf_op jit(solution)/shard_map/all_to_all | solution.py:448
  205.7 5.2 %shard_map.234 = (f32[8,96,768]{2,1,0:T(8,128)S(1)}, f32[384,768]{1,0:T(8,128)}) custom-call(f32[4096,128]{1,0:T(8,128)S(1)} %bitcast.16, f32[384,768]{1,0:T(8,128)S(1)} %copy-done.8, f32[384,768]{1,0:T(8,128)S(1)} %bitcast.19, bf16[2,256,256]{2,1,0:T(8,128)(2,1)S(1)} %copy-done.14, bf16[2,256,176]{2,1,0:T(8,128)(2,1)S(1)} %copy-done.13, ...), custom_call_target="tpu_custom_call" | custom-call | bytes 9492480 | tf_op jit(solution)/shard_map/pallas_call | solution.py:433
  210.9 33.9 %all_to_all.39 = f32[8,96,768]{2,1,0:T(8,128)S(1)} all-to-all(f32[8,96,768]{2,1,0:T(8,128)S(1)} %get-tuple-element.27), channel_id=1, replica_groups=mesh['rows'=16,'cols'=8] {'cols'}, dimensions={0} | all-to-all | bytes 4718592 | tf_op jit(solution)/shard_map/all_to_all | solution.py:448
  244.8 1.6 fusion
  (27 shorter events, 0.1 us)
Async XLA Ops:
  0.6 6.4 %copy-start.6 = (s32[6144,48]{0,1:T(8,128)S(1)}, s32[6144,48]{0,1:T(8,128)}, u32[]{:S(2)}) copy-start(s32[6144,48]{0,1:T(8,128)} %param.25) | copy-start | bytes 3538948
  0.6 15.3 %copy-start.24 = (s32[128]{0:T(128)S(1)}, s32[128]{0:T(128)}, u32[]{:S(2)}) copy-start(s32[128]{0:T(128)} %constant.71.clone) | copy-start | bytes 1540
  0.7 24.3 %all-to-all-start = ((f32[8,48,768]{2,1,0:T(8,128)}), f32[8,48,768]{2,1,0:T(8,128)S(1)}, u32[]{:S(2)}, u32[]{:S(2)}) async-start(f32[8,48,768]{2,1,0:T(8,128)} %bitcast.23), calls=%async_computation | async-start | bytes 2359296 | tf_op jit(solution)/shard_map/all_to_all | solution.py:448
  7.0 15.6 %collective-permute-start.2 = (s32[8,6144]{1,0:T(8,128)S(1)}, s32[8,6144]{1,0:T(8,128)S(1)}, u32[]{:S(2)}, u32[]{:S(2)}) collective-permute-start(s32[8,6144]{1,0:T(8,128)S(1)} %slice.14), channel_id=1, source_target_pairs={{40,44},{41,45},{42,46},{43,47},{84,48},{85,49},{86,50},{87,51}} | collective-permute-start | bytes 589832 | tf_op jit(solution)/shard_map/ppermute | solution.py:453
  7.7 14.9 %collective-permute-start.1 = (s32[8,6144]{1,0:T(8,128)S(1)}, s32[8,6144]{1,0:T(8,128)S(1)}, u32[]{:S(2)}, u32[]{:S(2)}) collective-permute-start(s32[8,6144]{1,0:T(8,128)S(1)} %slice.14), channel_id=1, source_target_pairs={{88,44},{89,45},{90,46},{91,47},{92,48},{93,49},{94,50},{95,51},{9... | collective-permute-start | bytes 589832 | tf_op jit(solution)/shard_map/ppermute | solution.py:453
  8.4 14.3 %collective-permute-start = (s32[8,6144]{1,0:T(8,128)S(1)}, s32[8,6144]{1,0:T(8,128)S(1)}, u32[]{:S(2)}, u32[]{:S(2)}) collective-permute-start(s32[8,6144]{1,0:T(8,128)S(1)} %slice.14), channel_id=1, source_target_pairs={{0,44},{1,45},{2,46},{3,47},{4,48},{5,49},{6,50},{7,51},{8,52},{9,... | collective-permute-start | bytes 589832 | tf_op jit(solution)/shard_map/ppermute | solution.py:453
  16.6 6.1 %copy-start.12 = (f32[2,3,128,128]{3,2,1,0:T(8,128)S(1)}, f32[2,3,128,128]{3,2,1,0:T(8,128)}, u32[]{:S(2)}) copy-start(f32[2,3,128,128]{3,2,1,0:T(8,128)} %constant.69.clone.hx_ref) | copy-start | bytes 1179652
  23.7 1.3 copy-start.1
  25.0 38.9 %copy-start.5 = (bf16[2,256,256]{2,1,0:T(8,128)(2,1)S(1)}, bf16[2,256,256]{2,1,0:T(8,128)(2,1)}, u32[]{:S(2)}) copy-start(bf16[2,256,256]{2,1,0:T(8,128)(2,1)} %constant.57.clone.l_ref.l2_ref) | copy-start | bytes 786436
  25.0 38.9 %copy-start.20 = (f32[2,48,1,128]{3,2,1,0:T(1,128)S(1)}, f32[2,48,1,128]{3,2,1,0:T(1,128)}, u32[]{:S(2)}) copy-start(f32[2,48,1,128]{3,2,1,0:T(1,128)} %constant.55.clone.tw_ref) | copy-start | bytes 147460
  66.1 40.2 %copy-start.3 = (f32[2,6,128,128]{3,2,1,0:T(8,128)S(1)}, f32[2,6,128,128]{3,2,1,0:T(8,128)}, u32[]{:S(2)}) copy-start(f32[2,6,128,128]{3,2,1,0:T(8,128)} %constant.64.clone.tw_ref) | copy-start | bytes 2359300
  66.1 40.2 %copy-start.9 = (bf16[2,256,256]{2,1,0:T(8,128)(2,1)S(1)}, bf16[2,256,256]{2,1,0:T(8,128)(2,1)}, u32[]{:S(2)}) copy-start(bf16[2,256,256]{2,1,0:T(8,128)(2,1)} %constant.60.clone.m_ref) | copy-start | bytes 786436
  66.1 40.2 %copy-start.16 = (bf16[2,256,256]{2,1,0:T(8,128)(2,1)S(1)}, bf16[2,256,256]{2,1,0:T(8,128)(2,1)}, u32[]{:S(2)}) copy-start(bf16[2,256,256]{2,1,0:T(8,128)(2,1)} %constant.61.clone.m2_ref) | copy-start | bytes 786436
  66.1 40.2 %copy-start.17 = (bf16[2,256,256]{2,1,0:T(8,128)(2,1)S(1)}, bf16[2,256,256]{2,1,0:T(8,128)(2,1)}, u32[]{:S(2)}) copy-start(bf16[2,256,256]{2,1,0:T(8,128)(2,1)} %constant.56.clone.l_ref) | copy-start | bytes 786436
  66.1 40.2 %copy-start.18 = (f32[2,6,16,128]{3,2,1,0:T(8,128)S(1)}, f32[2,6,16,128]{3,2,1,0:T(8,128)}, u32[]{:S(2)}) copy-start(f32[2,6,16,128]{3,2,1,0:T(8,128)} %constant.65.clone.tw2_ref) | copy-start | bytes 294916
  66.2 40.2 %copy-start.19 = (f32[2,6,16,128]{3,2,1,0:T(8,128)S(1)}, f32[2,6,16,128]{3,2,1,0:T(8,128)}, u32[]{:S(2)}) copy-start(f32[2,6,16,128]{3,2,1,0:T(8,128)} %constant.63.clone.v2_ref) | copy-start | bytes 294916
  66.2 40.1 %copy-start.21 = (f32[6,8,128]{2,1,0:T(8,128)S(1)}, f32[6,8,128]{2,1,0:T(8,128)}, u32[]{:S(2)}) copy-start(f32[6,8,128]{2,1,0:T(8,128)} %constant.70.clone.ay_ref) | copy-start | bytes 73732
  66.2 40.1 %copy-start.22 = (f32[2,6,1,128]{3,2,1,0:T(1,128)S(1)}, f32[2,6,1,128]{3,2,1,0:T(1,128)}, u32[]{:S(2)}) copy-start(f32[2,6,1,128]{3,2,1,0:T(1,128)} %constant.62.clone.v_ref) | copy-start | bytes 18436
  114.9 34.9 %copy-start.7 = (f32[8,48,768]{2,1,0:T(8,128)}, f32[8,48,768]{2,1,0:T(8,128)S(1)}, u32[]{:S(2)}) copy-start(f32[8,48,768]{2,1,0:T(8,128)S(1)} %get-tuple-element.23) | copy-start | bytes 3538948
  149.8 4.2 %copy-start.23 = (f32[2,3,1,128]{3,2,1,0:T(1,128)S(1)}, f32[2,3,1,128]{3,2,1,0:T(1,128)}, u32[]{:S(2)}) copy-start(f32[2,3,1,128]{3,2,1,0:T(1,128)} %constant.67.clone.v_ref) | copy-start | bytes 9220
  149.8 21.5 %all-to-all-start.4 = ((f32[8,48,768]{2,1,0:T(8,128)}), f32[8,48,768]{2,1,0:T(8,128)S(1)}, u32[]{:S(2)}, u32[]{:S(2)}) async-start(f32[8,48,768]{2,1,0:T(8,128)} %copy-done.7), calls=%async_computation.4 | async-start | bytes 2359296 | tf_op jit(solution)/shard_map/all_to_all | solution.py:448
  154.0 1.5 copy-start.2
  155.6 1.0 copy-start.11
  156.6 0.9 copy-start.15
  167.2 1.3 copy-start
  171.2 34.4 %copy-start.4 = (f32[2,6,128,128]{3,2,1,0:T(8,128)S(1)}, f32[2,6,128,128]{3,2,1,0:T(8,128)}, u32[]{:S(2)}) copy-start(f32[2,6,128,128]{3,2,1,0:T(8,128)} %constant.64.clone.tw_ref) | copy-start | bytes 2359300
  171.2 34.4 %copy-start.8 = (f32[384,768]{1,0:T(8,128)S(1)}, f32[384,768]{1,0:T(8,128)}, u32[]{:S(2)}) copy-start(f32[384,768]{1,0:T(8,128)} %get-tuple-element.25.one_ref) | copy-start | bytes 3538948
  171.2 34.4 %copy-start.10 = (bf16[2,256,256]{2,1,0:T(8,128)(2,1)S(1)}, bf16[2,256,256]{2,1,0:T(8,128)(2,1)}, u32[]{:S(2)}) copy-start(bf16[2,256,256]{2,1,0:T(8,128)(2,1)} %constant.60.clone.m_ref) | copy-start | bytes 786436
  171.2 34.4 %copy-start.13 = (bf16[2,256,176]{2,1,0:T(8,128)(2,1)S(1)}, bf16[2,256,176]{2,1,0:T(8,128)(2,1)}, u32[]{:S(2)}) copy-start(bf16[2,256,176]{2,1,0:T(8,128)(2,1)} %constant.59.clone.lm_ref) | copy-start | bytes 540676
  171.2 34.4 %copy-start.14 = (bf16[2,256,256]{2,1,0:T(8,128)(2,1)S(1)}, bf16[2,256,256]{2,1,0:T(8,128)(2,1)}, u32[]{:S(2)}) copy-start(bf16[2,256,256]{2,1,0:T(8,128)(2,1)} %constant.58.clone.l_ref) | copy-start | bytes 786436
